TPU v7x, 32 devices: a whole 2x2x4 slice. The times are simulated.
32 devices in a mesh: groups: 2 (over x), expert: 16 (over z, y, core).
Axes of the slice: x: 2, y: 2, z: 4, core: 2. Of those that a mesh axis runs over, the one named last changes fastest.
Arguments:
- tokens: bfloat16 [4096, 3584], P(('groups', 'expert')), parts along dimension 0, may hold values from -6 to 6
- expert_weights: bfloat16 [3, 3584, 8192], P(None, None, 'expert'), may hold values from -0.09375 to 0.09375
- expert_ids: int32 [4096, 2], P(('groups', 'expert')), parts along dimension 0, may hold values from 0 to 7, as said below
- copy_ids: int32 [4096, 2], P(('groups', 'expert')), parts along dimension 0, may hold values from 0 to 1, as said below
- gate_weights: bfloat16 [4096, 2], P(('groups', 'expert')), parts along dimension 0, may hold values from 0.099609375 to 1
Outputs:
- moe_out: bfloat16 [4096, 3584], P(('groups', 'expert')), parts along dimension 0
- served: int32 [32, 2], P(('groups', 'expert')), parts along dimension 0
There are 2 independent parts, one for each index of `groups`. A program takes and returns all parts, laid end to end along the dimension named above; an argument that names none is the same for every part. Nothing has to cross between parts.
Inputs may be any that keep to these rules, and one draw needn't show every extreme that they name: `expert_ids`: each row names 2 different experts. In the rows of one device no expert is named more than 2 * 32 times, and one expert, the same on every device, is named exactly 2 * 32 times in the rows of every device. `copy_ids`: in the rows of one device at most 32 routes name one expert with one slot number; both slots of the expert named 2 * 32 times take exactly 32 routes from every device.
All inputs are finite; a program needn't handle non-finite values.
Results may differ from a plain program's by a relative error of at most 0.0057.
Values may be sent and summed in bfloat16 or wider, within the bound.
No kernel may reach another device: no remote copies, remote signals or barrier semaphores. Data moves between devices by JAX's collectives and lax.ppermute only.
A program may use at most 128 MiB of HBM per device.

v0:
```python
import jax
import jax.numpy as jnp
from jax import lax
from jax.sharding import PartitionSpec as P


def expert_rows(row_block, weights):
    gate_act = jnp.dot(row_block, weights[0], preferred_element_type=jnp.float32)
    up_act = jnp.dot(row_block, weights[1], preferred_element_type=jnp.float32)
    hidden = (jax.nn.silu(gate_act) * up_act).astype(jnp.bfloat16)
    product = lax.dot_general(
        hidden, weights[2], (((1,), (1,)), ((), ())), preferred_element_type=jnp.float32
    )
    return product.astype(jnp.bfloat16)


def on_device(tokens, expert_weights, expert_ids, copy_ids, gate_weights):
    devices = lax.axis_size("expert")
    experts = devices // 2
    tok_rows, top_k = expert_ids.shape
    model_width = tokens.shape[1]
    routes = tok_rows * top_k
    capacity = routes // experts
    flat_expert = expert_ids.reshape(routes)
    flat_copy = copy_ids.reshape(routes)
    flat_token = jnp.arange(routes, dtype=jnp.int32) // top_k
    flat_gate = gate_weights.reshape(routes).astype(jnp.float32)
    slot_key = flat_expert * 2 + flat_copy
    key_range = jnp.arange(2 * experts, dtype=jnp.int32)
    load_terms = jnp.sum((slot_key[:, None] == key_range[None, :]).astype(jnp.float32), axis=0)
    per_device = jnp.repeat(load_terms.reshape(experts, 2), 2, axis=0)
    served = lax.psum_scatter(per_device, "expert", scatter_dimension=0, tiled=True).astype(
        jnp.int32
    )
    position = jnp.arange(routes, dtype=jnp.int32)
    before = (slot_key[:, None] == slot_key[None, :]) & (position[None, :] < position[:, None])
    route_rank = jnp.sum(before.astype(jnp.int32), axis=1)
    padded = jnp.concatenate([tokens, jnp.zeros((1, model_width), tokens.dtype)], axis=0)
    lower_slot = (2 * flat_expert * 2 + flat_copy) * capacity + route_rank
    upper_slot = ((2 * flat_expert + 1) * 2 + flat_copy) * capacity + route_rank
    slot_table = jnp.full((devices * 2 * capacity,), tok_rows, jnp.int32)
    slot_table = slot_table.at[lower_slot].set(flat_token).at[upper_slot].set(flat_token)
    outgoing = padded[slot_table].reshape(devices, 2 * capacity, model_width)
    arrived = lax.all_to_all(outgoing, "expert", split_axis=0, concat_axis=0, tiled=True)
    arrived = arrived.reshape(devices, 2, capacity, model_width)
    results = expert_rows(arrived.reshape(devices * 2 * capacity, model_width), expert_weights)
    results = results.reshape(devices, 2 * capacity, model_width)
    returned = lax.all_to_all(results, "expert", split_axis=0, concat_axis=0, tiled=True)
    halves = returned.reshape(experts, 2, 2 * capacity, model_width)
    pick_index = (flat_expert * 2 + flat_copy) * capacity + route_rank
    lower_half = halves[:, 0].reshape(experts * 2 * capacity, model_width)[pick_index]
    upper_half = halves[:, 1].reshape(experts * 2 * capacity, model_width)[pick_index]
    picked = lower_half.astype(jnp.float32) + upper_half.astype(jnp.float32)
    combined = jnp.sum((picked * flat_gate[:, None]).reshape(tok_rows, top_k, model_width), axis=1)
    return (combined.astype(jnp.bfloat16), served)


def solution(mesh):
    return jax.shard_map(
        on_device,
        mesh=mesh,
        in_specs=(
            P(("groups", "expert"), None),
            P(None, None, "expert"),
            P(("groups", "expert"), None),
            P(("groups", "expert"), None),
            P(("groups", "expert"), None),
        ),
        out_specs=(P(("groups", "expert"), None), P(("groups", "expert"), None)),
        check_vma=False,
    )
```

profile of v0, /device:TPU:18, one launch (start us, length us, event | category | flops | bytes accessed | tf_op | source)
XLA Modules:
  0.0 426.9 jit_solution(14146500040745527397)
XLA Ops:
  0.6 0.8 copy.31
  1.4 0.7 broadcast_multiply_fusion
  2.1 0.1 copy.32
  2.2 0.1 add.139
  2.4 0.2 convert_reduce_fusion
  2.6 0.1 copy.30
  2.7 0.1 mul.101
  2.8 0.1 copy.33
  2.9 0.1 mul.104
  3.1 0.1 reshape.179
  3.2 1.4 scatter_custom_fusion
  4.7 1.4 scatter_fusion
  6.1 1.2 concatenate.3
  7.3 7.3 %gather_fusion = bf16[1024,3584]{1,0:T(8,128)(2,1)} fusion(bf16[129,3584]{1,0:T(8,128)(2,1)S(1)} %concatenate.3, s32[1024]{0:T(1024)S(1)} %fusion.14), kind=kCustom, calls=%fused_computation | custom fusion | bytes 14684160 | tf_op jit(solution)/shard_map/gather | solution.py:43
  14.6 166.4 %all_to_all.10 = bf16[16,64,3584]{2,1,0:T(8,128)(2,1)S(1)} all-to-all(bf16[16,64,3584]{2,1,0:T(8,128)(2,1)} %bitcast.36), channel_id=1, replica_groups=mesh['groups'=2,'expert'=16] {'expert'}, dimensions={0} | all-to-all | bytes 14680064 | tf_op jit(solution)/shard_map/all_to_all | solution.py:44
  181.0 3.0 copy-done
  184.0 6.0 %fusion.1 = f32[1024,512]{1,0:T(8,128)S(1)} fusion(bf16[1024,3584]{1,0:T(8,128)(2,1)S(1)} %bitcast.38, bf16[3,3584,512]{2,1,0:T(8,128)(2,1)} %param.6), kind=kOutput, calls=%fused_computation.7 | convolution fusion | flops 3758096384 | bytes 13107200 | tf_op jit(solution)/shard_map/dot_general | solution.py:9
  190.0 14.4 %convolution_convert_fusion = bf16[1024,3584]{1,0:T(8,128)(2,1)} fusion(bf16[3,3584,512]{2,1,0:T(8,128)(2,1)} %param.6, f32[1024,512]{1,0:T(8,128)S(1)} %fusion.1, bf16[1024,3584]{1,0:T(8,128)(2,1)} %bitcast.39), kind=kOutput, calls=%fused_computation.5 | convolution fusion | flops 7523008512 | bytes 24117248 | tf_op jit(solution)/shard_map/dot_general | solution.py:11
  204.4 5.2 %all-to-all-start.1 = ((bf16[16,64,3584]{2,1,0:T(8,128)(2,1)}), bf16[16,64,3584]{2,1,0:T(8,128)(2,1)}, u32[]{:S(2)}, u32[]{:S(2)}) async-start(bf16[16,64,3584]{2,1,0:T(8,128)(2,1)} %bitcast.37), calls=%async_computation.1 | async-start | bytes 14680064 | tf_op jit(solution)/shard_map/all_to_all | solution.py:48
  209.6 0.1 copy.36
  209.7 0.1 convert_reduce_fusion.1
  209.9 0.1 copy.37
  210.1 0.6 dynamic-slice
  210.7 177.1 %all-reduce.1 = f32[16,2]{0,1:T(2,128)S(1)} all-reduce(f32[16,2]{0,1:T(2,128)S(1)} %reshape.184), channel_id=2, replica_groups=mesh['groups'=2,'expert'=16] {'expert'}, use_global_device_ids=true, to_apply=%region_5.6.clone | all-reduce | flops 32 | bytes 256
  387.8 0.7 dynamic-slice_convert_fusion
  388.5 0.6 copy.38
  389.1 6.8 %fusion.19 = (bf16[8,1,64,3584]{3,2,1,0:T(8,128)(2,1)}, bf16[8,1,64,3584]{3,2,1,0:T(8,128)(2,1)}) fusion(bf16[8,2,64,3584]{3,2,1,0:T(8,128)(2,1)} %bitcast.9), kind=kLoop, calls=%fused_computation.40 | loop fusion | bytes 14680064 | tf_op jit(solution)/shard_map/slice | solution.py:51
  395.9 6.0 %gather_fusion.1 = bf16[256,3584]{1,0:T(8,128)(2,1)S(1)} fusion(bf16[512,3584]{1,0:T(8,128)(2,1)} %bitcast.35, s32[1024]{0:T(1024)S(1)} %pad_clamp_fusion), kind=kCustom, calls=%fused_computation.1 | custom fusion | bytes 3671040 | tf_op jit(solution)/shard_map/gather | solution.py:51
  402.0 7.3 %gather_fusion.2 = bf16[256,3584]{1,0:T(8,128)(2,1)} fusion(bf16[512,3584]{1,0:T(8,128)(2,1)} %bitcast.34, s32[1024]{0:T(1024)S(1)} %pad_clamp_fusion), kind=kCustom, calls=%fused_computation.2 | custom fusion | bytes 3671040 | tf_op jit(solution)/shard_map/gather | solution.py:52
  409.3 3.8 convert_add_fusion
  413.1 5.6 %add.153 = f32[128,2,3584]{2,1,0:T(2,128)} reshape(f32[256,3584]{1,0:T(8,128)} %convert_add_fusion) | data formatting | bytes 7340032 | tf_op jit(solution)/shard_map/add | solution.py:53
  418.7 8.2 %multiply_reduce_fusion = bf16[128,3584]{1,0:T(8,128)(2,1)} fusion(f32[128,2,3584]{2,1,0:T(2,128)} %add.153, f32[128,2]{1,0:T(8,128)S(1)} %copy.36), kind=kLoop, calls=%fused_computation.11 | loop fusion | flops 1376256 | bytes 4588544 | tf_op jit(solution)/shard_map/reduce_sum | solution.py:54
  (13 shorter events, 0.3 us)
Async XLA Ops:
  181.0 3.0 copy-start
  204.3 5.2 %copy-start.1 = (bf16[128,2]{0,1:T(2,128)(2,1)S(1)}, bf16[128,2]{0,1:T(2,128)(2,1)}, u32[]{:S(2)}) copy-start(bf16[128,2]{0,1:T(2,128)(2,1)} %param.9) | copy-start | bytes 1540
  204.4 5.8 %copy-start.2 = (u32[32]{0:T(128)S(1)}, u32[32]{0:T(128)}, u32[]{:S(2)}) copy-start(u32[32]{0:T(128)} %constant.45) | copy-start | bytes 388
  204.4 184.8 %all-to-all-start.1 = ((bf16[16,64,3584]{2,1,0:T(8,128)(2,1)}), bf16[16,64,3584]{2,1,0:T(8,128)(2,1)}, u32[]{:S(2)}, u32[]{:S(2)}) async-start(bf16[16,64,3584]{2,1,0:T(8,128)(2,1)} %bitcast.37), calls=%async_computation.1 | async-start | bytes 14680064 | tf_op jit(solution)/shard_map/all_to_all | solution.py:48
where the time goes:
time: 428 us; the launch traced here: 427 us
  blocking collectives  343 us (80%)
  local copies, waits for them, and re-layouts  43.4 us (10%)
  matrix products  20.4 us (5%)
  other arithmetic  13.8 us (3%)
  starting transfers between devices  5.22 us (1%)
    unnamed x1, blocking collectives  177 us
    all_to_all x1, blocking collectives, on_device(): lax.all_to_all(outgoing, 'expert', split_axis=0, concat_axis=0, tiled=True)  166 us
    dot_general x1, matrix products, expert_rows(): lax.dot_general(hidden, weights[2], (((1,), (1,)), ((), ())), preferred_e...  14.4 us
  transfers between devices with their start and end apart: 1, of which 0 were waited for; matrix products, arithmetic and copies ran while one was open for 1% of the time, Pallas kernels for 0%

commit v1 on v0

v1 whole, which is shorter than its diff:
```python
import jax
import jax.numpy as jnp
from jax import lax
from jax.sharding import PartitionSpec as P

CORES = 2


def grid_of(chips):
    inner = 1
    while (2 * inner) * (2 * inner) <= chips and chips % (2 * inner) == 0:
        inner *= 2
    return chips // inner, inner


def ring_of(length):
    return [p for p in range(length) if p % 2 == 0] + [p for p in reversed(range(length)) if p % 2 == 1]


def hidden_of(rows, weights):
    gate_act = jnp.dot(rows, weights[0], preferred_element_type=jnp.float32)
    up_act = jnp.dot(rows, weights[1], preferred_element_type=jnp.float32)
    return (jax.nn.silu(gate_act) * up_act).astype(jnp.bfloat16)


def down_of(hidden, weights):
    return lax.dot_general(hidden, weights[2], (((1,), (1,)), ((), ())), preferred_element_type=jnp.float32)


def on_device(tokens, expert_weights, expert_ids, copy_ids, gate_weights):
    devices = lax.axis_size("expert")
    experts = devices // CORES
    outer, inner = grid_of(experts)
    tok_rows, top_k = expert_ids.shape
    slots = 2 * (tok_rows * top_k // experts)
    me = lax.axis_index("expert")
    core = me % CORES
    chip = me // CORES
    col = chip % inner
    plane = chip // inner

    ring = ring_of(outer)
    place = jnp.asarray([ring.index(p) for p in range(outer)], jnp.int32)[plane]
    ring_list = jnp.asarray(ring, jnp.int32)

    def device_of(p, q, c):
        return (p * inner + q) * CORES + c

    every = [(p, q, c) for p in range(outer) for q in range(inner) for c in range(CORES)]
    ring_pairs = [
        (device_of(p, q, c), device_of(ring[(ring.index(p) + 1) % outer], q, c)) for p, q, c in every
    ]

    def column_pairs(shift):
        return [(device_of(p, q, c), device_of(p, (q + shift) % inner, c)) for p, q, c in every]

    core_pairs = [(device_of(p, q, c), device_of(p, q, 1 - c)) for p, q, c in every]

    def permute(x, pairs):
        return lax.ppermute(x, "expert", pairs)

    keys = (expert_ids * 2 + copy_ids).astype(jnp.float32)
    meta = jnp.concatenate([keys.T, gate_weights.astype(jnp.float32).T], axis=0)
    metas = lax.all_gather(meta, "expert")
    all_keys = metas[:, :top_k].astype(jnp.int32)
    slot_range = jnp.arange(2, dtype=jnp.int32)
    served = jnp.sum(
        (all_keys[None] == (chip * 2 + slot_range)[:, None, None, None]).astype(jnp.int32), axis=(1, 2, 3)
    ).reshape(1, 2)

    tri = (
        jnp.arange(tok_rows, dtype=jnp.int32)[:, None] <= jnp.arange(tok_rows, dtype=jnp.int32)[None, :]
    ).astype(jnp.float32)
    slot_ids = jnp.arange(slots, dtype=jnp.int32)

    def tables(meta_rows):
        ids = meta_rows[:top_k].astype(jnp.int32) // 2
        gates = meta_rows[top_k:]
        wanted = plane * inner + (col + jnp.arange(inner, dtype=jnp.int32)) % inner
        match = (ids[None] == wanted[:, None, None]).astype(jnp.float32)
        hit = jnp.sum(match, axis=1)
        weight = jnp.sum(match * gates[None], axis=1)
        rank = jnp.dot(hit, tri, preferred_element_type=jnp.float32).astype(jnp.int32) - 1
        onehot = ((rank[:, None, :] == slot_ids[None, :, None]) & (hit[:, None, :] > 0)).astype(jnp.float32)
        pack = onehot.astype(jnp.bfloat16)
        combine = (onehot * weight[:, None, :]).astype(jnp.bfloat16)
        return pack.reshape(inner * slots, tok_rows), combine.reshape(inner * slots, tok_rows)

    blocks = [tokens]
    for step in range(1, outer):
        blocks.append(permute(blocks[-1], ring_pairs))
    other_weights = permute(expert_weights, core_pairs)

    combines, parts = [], []
    for step in range(outer):
        if step == 0:
            source_meta = meta
        else:
            source = device_of(ring_list[(place - step + outer) % outer], col, core)
            source_meta = lax.dynamic_index_in_dim(metas, source, 0, keepdims=False)
        pack, combine = tables(source_meta)
        combines.append(combine)
        packed = jnp.dot(pack, blocks[step], preferred_element_type=jnp.float32).astype(jnp.bfloat16)
        rows = [packed[:slots]]
        for shift in range(1, inner):
            rows.append(permute(packed[shift * slots : (shift + 1) * slots], column_pairs(shift)))
        parts.append(jnp.concatenate(rows, axis=0))

    def run(rows):
        own = hidden_of(rows, expert_weights)
        other = hidden_of(rows, other_weights)
        return (down_of(own, expert_weights) + down_of(other, other_weights)).astype(jnp.bfloat16)

    def send_back(rows):
        back = [rows[:slots]]
        for shift in range(1, inner):
            back.append(permute(rows[shift * slots : (shift + 1) * slots], column_pairs(-shift)))
        return jnp.concatenate(back, axis=0)

    block_rows = inner * slots
    results = [None] * outer
    first = run(jnp.concatenate(parts[:2], axis=0))
    results[0], results[1] = first[:block_rows], first[block_rows:]
    for step in range(2, outer):
        results[step] = run(parts[step])

    carry = None
    for step in list(range(1, outer)) + [0]:
        back = send_back(results[step])
        total = lax.dot_general(
            combines[step], back, (((0,), (0,)), ((), ())), preferred_element_type=jnp.float32
        )
        if carry is not None:
            total = total + carry.astype(jnp.float32)
        total = total.astype(jnp.bfloat16)
        if step != 0:
            carry = permute(total, ring_pairs)
    return total, served


def solution(mesh):
    return jax.shard_map(
        on_device,
        mesh=mesh,
        in_specs=(
            P(("groups", "expert"), None),
            P(None, None, "expert"),
            P(("groups", "expert"), None),
            P(("groups", "expert"), None),
            P(("groups", "expert"), None),
        ),
        out_specs=(P(("groups", "expert"), None), P(("groups", "expert"), None)),
        check_vma=False,
    )
```

time: 428 us -> 200 us (0.47)
  the two profiles are of different devices: /device:TPU:18 before, /device:TPU:0 now
where the time goes in v1:
time: 200 us
  waiting for transfers between devices  72.4 us (36%)
  matrix products  67.5 us (34%)
  blocking collectives  27.4 us (14%)
  starting transfers between devices  19.3 us (10%)
  local copies, waits for them, and re-layouts  5.75 us (3%)
  between operations  4.88 us (2%)
  other arithmetic  2.5 us (1%)
    ppermute x15, waiting for transfers between devices, permute(): return lax.ppermute(x, 'expert', pairs)  72.4 us
    dot_general x6, matrix products, down_of(): lax.dot_general(hidden, weights[2], (((1,), (1,)), ((), ())), preferred_e...  38.5 us
    all_gather x1, blocking collectives, on_device(): metas = lax.all_gather(meta, 'expert')  27.4 us
    ppermute x15, starting transfers between devices, permute(): return lax.ppermute(x, 'expert', pairs)  19.3 us
    dot_general x3, matrix products, hidden_of(): up_act = jnp.dot(rows, weights[1], preferred_element_type=jnp.float32)  10.5 us
    dot_general x3, matrix products, hidden_of(): gate_act = jnp.dot(rows, weights[0], preferred_element_type=jnp.float32)  10.2 us
    dot_general x4, matrix products, on_device(): lax.dot_general(combines[step], back, (((0,), (0,)), ((), ())), preferred...  5 us
  transfers between devices with their start and end apart: 15, of which 10 were waited for; matrix products, arithmetic and copies ran while one was open for 30% of the time, Pallas kernels for 0%

profile of v1, /device:TPU:0, one launch (start us, length us, event | category | flops | bytes accessed | tf_op | source)
XLA Modules:
  0.0 199.7 jit_solution(1632713921536711060)
XLA Ops:
  0.6 4.1 %collective-permute-start.1 = (bf16[128,3584]{1,0:T(8,128)(2,1)}, bf16[128,3584]{1,0:T(8,128)(2,1)S(1)}, u32[]{:S(2)}, u32[]{:S(2)}) collective-permute-start(bf16[128,3584]{1,0:T(8,128)(2,1)} %param.7), channel_id=1, source_target_pairs={{0,8},{1,9},{2,10},{3,11},{4,0},{5,1},{6,2},{7,3},{8,12},{9,13},{1... | collective-permute-start | bytes 2752520 | tf_op jit(solution)/shard_map/ppermute | solution.py:60
  12.6 27.4 %all-gather.1 = f32[16,4,128]{2,1,0:T(4,128)S(1)} all-gather(f32[1,4,128]{2,1,0:T(4,128)S(1)} %maximum_bitcast_fusion), channel_id=2, replica_groups=mesh['groups'=2,'expert'=16] {'expert'}, dimensions={0}, use_global_device_ids=true | all-gather | bytes 34816 | tf_op jit(solution)/shard_map/all_gather | solution.py:64
  41.0 1.6 convolution_convert_fusion.4
  43.2 2.1 %collective-permute-start.2 = (bf16[64,3584]{1,0:T(8,128)(2,1)S(1)}, bf16[64,3584]{1,0:T(8,128)(2,1)S(1)}, u32[]{:S(2)}, u32[]{:S(2)}) collective-permute-start(bf16[64,3584]{1,0:T(8,128)(2,1)S(1)} %get-tuple-element.33), channel_id=1, source_target_pairs={{0,2},{1,3},{2,0},{3,1},{4,6},{5,7},{6,4},{7,5},{8,10},{9,11},{10,... | collective-permute-start | bytes 1376264 | tf_op jit(solution)/shard_map/ppermute | solution.py:60
  45.4 10.7 %collective-permute-done = bf16[64,3584]{1,0:T(8,128)(2,1)S(1)} collective-permute-done((bf16[64,3584]{1,0:T(8,128)(2,1)S(1)}, bf16[64,3584]{1,0:T(8,128)(2,1)S(1)}, u32[]{:S(2)}, u32[]{:S(2)}) %collective-permute-start) | collective-permute-done | bytes 458784 | tf_op jit(solution)/shard_map/ppermute | solution.py:60
  56.0 9.2 %collective-permute-done.2 = bf16[64,3584]{1,0:T(8,128)(2,1)S(1)} collective-permute-done((bf16[64,3584]{1,0:T(8,128)(2,1)S(1)}, bf16[64,3584]{1,0:T(8,128)(2,1)S(1)}, u32[]{:S(2)}, u32[]{:S(2)}) %collective-permute-start.2) | collective-permute-done | bytes 458784 | tf_op jit(solution)/shard_map/ppermute | solution.py:60
  65.3 4.1 %fusion.16 = f32[256,512]{1,0:T(8,128)} fusion(bf16[3,3584,512]{2,1,0:T(8,128)(2,1)} %param.8, bf16[64,3584]{1,0:T(8,128)(2,1)S(1)} %collective-permute-done.2, bf16[64,3584]{1,0:T(8,128)(2,1)S(1)} %get-tuple-element.32, bf16[64,3584]{1,0:T(8,128)(2,1)S(1)} %collective-permute-done, bf16[64,3584]{1,0:T(8,128)(2,1)S(1)} %get-tuple-element.30), kind=kOutput, calls=%fused_computation.30 | convolution fusion | flops 946864128 | bytes 6029312 | tf_op jit(solution)/shard_map/dot_general | solution.py:22
  70.9 7.7 %fusion.10 = f32[256,3584]{1,0:T(8,128)} fusion(bf16[3,3584,512]{2,1,0:T(8,128)(2,1)} %param.8, f32[256,512]{1,0:T(8,128)} %fusion.16, bf16[64,3584]{1,0:T(8,128)(2,1)} %copy-done.9, bf16[64,3584]{1,0:T(8,128)(2,1)S(1)} %get-tuple-element.32, bf16[64,3584]{1,0:T(8,128)(2,1)} %copy-done.7, bf16[64,3584]{1,0:T(8,128)(2,1)S(1)} %get-tuple-element.30), kind=kOutput, calls=%fused_computation.24 | convolution fusion | flops 1887174656 | bytes 13369344 | tf_op jit(solution)/shard_map/dot_general | solution.py:27
  78.7 4.3 %collective-permute-done.9 = bf16[64,3584]{1,0:T(8,128)(2,1)} collective-permute-done((bf16[64,3584]{1,0:T(8,128)(2,1)}, bf16[64,3584]{1,0:T(8,128)(2,1)}, u32[]{:S(2)}, u32[]{:S(2)}) %collective-permute-start.9) | collective-permute-done | bytes 458784 | tf_op jit(solution)/shard_map/ppermute | solution.py:60
  82.9 3.5 %fusion.12 = f32[128,512]{1,0:T(8,128)} fusion(bf16[3,3584,512]{2,1,0:T(8,128)(2,1)} %param.8, bf16[64,3584]{1,0:T(8,128)(2,1)} %collective-permute-done.9, bf16[64,3584]{1,0:T(8,128)(2,1)S(1)} %get-tuple-element.28), kind=kOutput, calls=%fused_computation.26 | convolution fusion | flops 471597056 | bytes 4849664 | tf_op jit(solution)/shard_map/dot_general | solution.py:22
  86.5 6.3 %collective-permute-done.6 = bf16[128,3584]{1,0:T(8,128)(2,1)S(1)} collective-permute-done((bf16[128,3584]{1,0:T(8,128)(2,1)S(1)}, bf16[128,3584]{1,0:T(8,128)(2,1)S(1)}, u32[]{:S(2)}, u32[]{:S(2)}) %collective-permute-start.6) | collective-permute-done | bytes 917536 | tf_op jit(solution)/shard_map/ppermute | solution.py:60
  93.2 1.5 collective-permute-start.7
  94.7 6.4 %fusion.6 = f32[128,3584]{1,0:T(8,128)} fusion(bf16[3,3584,512]{2,1,0:T(8,128)(2,1)} %param.8, f32[128,512]{1,0:T(8,128)S(1)} %copy-done.14, bf16[64,3584]{1,0:T(8,128)(2,1)} %collective-permute-done.9, bf16[64,3584]{1,0:T(8,128)(2,1)S(1)} %get-tuple-element.28), kind=kOutput, calls=%fused_computation.20 | convolution fusion | flops 941752320 | bytes 10354688 | tf_op jit(solution)/shard_map/dot_general | solution.py:27
  101.1 3.2 %collective-permute-done.7 = bf16[64,3584]{1,0:T(8,128)(2,1)S(1)} collective-permute-done((bf16[64,3584]{1,0:T(8,128)(2,1)S(1)}, bf16[64,3584]{1,0:T(8,128)(2,1)S(1)}, u32[]{:S(2)}, u32[]{:S(2)}) %collective-permute-start.7) | collective-permute-done | bytes 458784 | tf_op jit(solution)/shard_map/ppermute | solution.py:60
  104.4 2.8 %fusion.14 = f32[128,512]{1,0:T(8,128)S(1)} fusion(bf16[3,3584,512]{2,1,0:T(8,128)(2,1)} %param.8, bf16[64,3584]{1,0:T(8,128)(2,1)S(1)} %collective-permute-done.7, bf16[64,3584]{1,0:T(8,128)(2,1)S(1)} %get-tuple-element.24), kind=kOutput, calls=%fused_computation.28 | convolution fusion | flops 471597056 | bytes 4849664 | tf_op jit(solution)/shard_map/dot_general | solution.py:22
  107.2 6.3 %fusion.8 = f32[128,3584]{1,0:T(8,128)} fusion(bf16[3,3584,512]{2,1,0:T(8,128)(2,1)} %param.8, f32[128,512]{1,0:T(8,128)S(1)} %fusion.14, bf16[64,3584]{1,0:T(8,128)(2,1)S(1)} %collective-permute-done.7, bf16[64,3584]{1,0:T(8,128)(2,1)S(1)} %get-tuple-element.24), kind=kOutput, calls=%fused_computation.22 | convolution fusion | flops 941752320 | bytes 10354688 | tf_op jit(solution)/shard_map/dot_general | solution.py:27
  113.6 4.0 %fusion.26 = f32[256,512]{1,0:T(8,128)} fusion(bf16[3,3584,512]{2,1,0:T(8,128)(2,1)} %collective-permute-done.3, bf16[64,3584]{1,0:T(8,128)(2,1)S(1)} %copy-done.10, bf16[64,3584]{1,0:T(8,128)(2,1)S(1)} %get-tuple-element.32, bf16[64,3584]{1,0:T(8,128)(2,1)S(1)} %copy-done.8, bf16[64,3584]{1,0:T(8,128)(2,1)S(1)} %get-tuple-element.30), kind=kOutput, calls=%fused_computation.40 | convolution fusion | flops 946864128 | bytes 6029312 | tf_op jit(solution)/shard_map/dot_general | solution.py:21
  117.6 6.6 %fusion = bf16[256,3584]{1,0:T(8,128)(2,1)S(1)} fusion(f32[256,3584]{1,0:T(8,128)} %fusion.10, bf16[3,3584,512]{2,1,0:T(8,128)(2,1)} %collective-permute-done.3, f32[256,512]{1,0:T(8,128)} %fusion.26, bf16[64,3584]{1,0:T(8,128)(2,1)S(1)} %copy-done.11, bf16[64,3584]{1,0:T(8,128)(2,1)S(1)} %get-tuple-element.32, bf16[64,3584]{1,0:T(8,128)(2,1)S(1)} %copy-done.8, ...), kind=kOutput, calls=%fused_computation.1 | convolution fusion | flops 1889009664 | bytes 15204352 | tf_op jit(solution)/shard_map/dot_general | solution.py:27
  126.4 2.8 %fusion.24 = f32[128,512]{1,0:T(8,128)S(1)} fusion(bf16[3,3584,512]{2,1,0:T(8,128)(2,1)} %collective-permute-done.3, bf16[64,3584]{1,0:T(8,128)(2,1)} %collective-permute-done.9, bf16[64,3584]{1,0:T(8,128)(2,1)S(1)} %copy-done.3), kind=kOutput, calls=%fused_computation.38 | convolution fusion | flops 471597056 | bytes 4849664 | tf_op jit(solution)/shard_map/dot_general | solution.py:21
  129.2 5.7 %fusion.4 = bf16[128,3584]{1,0:T(8,128)(2,1)S(1)} fusion(f32[128,3584]{1,0:T(8,128)} %fusion.6, bf16[3,3584,512]{2,1,0:T(8,128)(2,1)} %collective-permute-done.3, f32[128,512]{1,0:T(8,128)S(1)} %fusion.24, bf16[64,3584]{1,0:T(8,128)(2,1)} %collective-permute-done.9, bf16[64,3584]{1,0:T(8,128)(2,1)S(1)} %copy-done.3), kind=kOutput, calls=%fused_computation.10 | convolution fusion | flops 942669824 | bytes 11272192 | tf_op jit(solution)/shard_map/dot_general | solution.py:27
  136.7 1.4 convolution_convert_fusion
  138.2 1.5 collective-permute-start.12
  139.7 3.4 %fusion.25 = f32[128,512]{1,0:T(8,128)} fusion(bf16[3,3584,512]{2,1,0:T(8,128)(2,1)} %collective-permute-done.3, bf16[64,3584]{1,0:T(8,128)(2,1)S(1)} %copy-done.13, bf16[64,3584]{1,0:T(8,128)(2,1)S(1)} %copy-done.5), kind=kOutput, calls=%fused_computation.39 | convolution fusion | flops 471597056 | bytes 4849664 | tf_op jit(solution)/shard_map/dot_general | solution.py:21
  143.1 5.8 %fusion.2 = bf16[128,3584]{1,0:T(8,128)(2,1)S(1)} fusion(f32[128,3584]{1,0:T(8,128)} %fusion.8, bf16[3,3584,512]{2,1,0:T(8,128)(2,1)} %collective-permute-done.3, f32[128,512]{1,0:T(8,128)} %fusion.25, bf16[64,3584]{1,0:T(8,128)(2,1)} %copy-done.12, bf16[64,3584]{1,0:T(8,128)(2,1)S(1)} %copy-done.6), kind=kOutput, calls=%fused_computation.8 | convolution fusion | flops 942669824 | bytes 11272192 | tf_op jit(solution)/shard_map/dot_general | solution.py:27
  148.9 8.9 %collective-permute-done.12 = bf16[128,3584]{1,0:T(8,128)(2,1)} collective-permute-done((bf16[128,3584]{1,0:T(8,128)(2,1)S(1)}, bf16[128,3584]{1,0:T(8,128)(2,1)}, u32[]{:S(2)}, u32[]{:S(2)}) %collective-permute-start.12) | collective-permute-done | bytes 917536 | tf_op jit(solution)/shard_map/ppermute | solution.py:60
  157.8 1.8 fusion.5
  159.6 2.8 %collective-permute-start.13 = (bf16[128,3584]{1,0:T(8,128)(2,1)S(1)}, bf16[128,3584]{1,0:T(8,128)(2,1)S(1)}, u32[]{:S(2)}, u32[]{:S(2)}) collective-permute-start(bf16[128,3584]{1,0:T(8,128)(2,1)S(1)} %fusion.5), channel_id=1, source_target_pairs={{0,8},{1,9},{2,10},{3,11},{4,0},{5,1},{6,2},{7,3},{8,12},{9,13},{1... | collective-permute-start | bytes 2752520 | tf_op jit(solution)/shard_map/ppermute | solution.py:60
  163.2 8.0 %collective-permute-done.8 = bf16[64,3584]{1,0:T(8,128)(2,1)S(1)} collective-permute-done((bf16[64,3584]{1,0:T(8,128)(2,1)S(1)}, bf16[64,3584]{1,0:T(8,128)(2,1)S(1)}, u32[]{:S(2)}, u32[]{:S(2)}) %collective-permute-start.8) | collective-permute-done | bytes 458784 | tf_op jit(solution)/shard_map/ppermute | solution.py:60
  171.2 7.8 %collective-permute-done.13 = bf16[128,3584]{1,0:T(8,128)(2,1)S(1)} collective-permute-done((bf16[128,3584]{1,0:T(8,128)(2,1)S(1)}, bf16[128,3584]{1,0:T(8,128)(2,1)S(1)}, u32[]{:S(2)}, u32[]{:S(2)}) %collective-permute-start.13) | collective-permute-done | bytes 917536 | tf_op jit(solution)/shard_map/ppermute | solution.py:60
  179.4 3.4 %collective-permute-start.14 = (bf16[128,3584]{1,0:T(8,128)(2,1)S(1)}, bf16[128,3584]{1,0:T(8,128)(2,1)S(1)}, u32[]{:S(2)}, u32[]{:S(2)}) collective-permute-start(bf16[128,3584]{1,0:T(8,128)(2,1)S(1)} %fusion.3), channel_id=1, source_target_pairs={{0,8},{1,9},{2,10},{3,11},{4,0},{5,1},{6,2},{7,3},{8,12},{9,13},{1... | collective-permute-start | bytes 2752520 | tf_op jit(solution)/shard_map/ppermute | solution.py:60
  184.3 7.0 %collective-permute-done.4 = bf16[64,3584]{1,0:T(8,128)(2,1)S(1)} collective-permute-done((bf16[64,3584]{1,0:T(8,128)(2,1)S(1)}, bf16[64,3584]{1,0:T(8,128)(2,1)S(1)}, u32[]{:S(2)}, u32[]{:S(2)}) %collective-permute-start.4) | collective-permute-done | bytes 458784 | tf_op jit(solution)/shard_map/ppermute | solution.py:60
  191.3 7.0 %collective-permute-done.14 = bf16[128,3584]{1,0:T(8,128)(2,1)S(1)} collective-permute-done((bf16[128,3584]{1,0:T(8,128)(2,1)S(1)}, bf16[128,3584]{1,0:T(8,128)(2,1)S(1)}, u32[]{:S(2)}, u32[]{:S(2)}) %collective-permute-start.14) | collective-permute-done | bytes 917536 | tf_op jit(solution)/shard_map/ppermute | solution.py:60
  (84 shorter events, 15.6 us)
Async XLA Ops:
  0.6 42.1 %collective-permute-start.1 = (bf16[128,3584]{1,0:T(8,128)(2,1)}, bf16[128,3584]{1,0:T(8,128)(2,1)S(1)}, u32[]{:S(2)}, u32[]{:S(2)}) collective-permute-start(bf16[128,3584]{1,0:T(8,128)(2,1)} %param.7), channel_id=1, source_target_pairs={{0,8},{1,9},{2,10},{3,11},{4,0},{5,1},{6,2},{7,3},{8,12},{9,13},{1... | collective-permute-start | bytes 2752520 | tf_op jit(solution)/shard_map/ppermute | solution.py:60
  4.7 108.9 %collective-permute-start.3 = (bf16[3,3584,512]{2,1,0:T(8,128)(2,1)}, bf16[3,3584,512]{2,1,0:T(8,128)(2,1)}, u32[]{:S(2)}, u32[]{:S(2)}) collective-permute-start(bf16[3,3584,512]{2,1,0:T(8,128)(2,1)} %param.8), channel_id=1, source_target_pairs={{0,1},{1,0},{2,3},{3,2},{4,5},{5,4},{6,7},{7,6},{8,9},{9,8},{10,11... | collective-permute-start | bytes 33030152 | tf_op jit(solution)/shard_map/ppermute | solution.py:60
  42.6 71.0 %copy-start = (bf16[64,3584]{1,0:T(8,128)(2,1)}, bf16[64,3584]{1,0:T(8,128)(2,1)S(1)}, u32[]{:S(2)}) copy-start(bf16[64,3584]{1,0:T(8,128)(2,1)S(1)} %get-tuple-element.30) | copy-start | bytes 1376260
  42.6 13.4 %collective-permute-start = (bf16[64,3584]{1,0:T(8,128)(2,1)S(1)}, bf16[64,3584]{1,0:T(8,128)(2,1)S(1)}, u32[]{:S(2)}, u32[]{:S(2)}) collective-permute-start(bf16[64,3584]{1,0:T(8,128)(2,1)S(1)} %get-tuple-element.31), channel_id=1, source_target_pairs={{0,2},{1,3},{2,0},{3,1},{4,6},{5,7},{6,4},{7,5},{8,10},{9,11},{10,... | collective-permute-start | bytes 1376264 | tf_op jit(solution)/shard_map/ppermute | solution.py:60
  43.2 22.1 %collective-permute-start.2 = (bf16[64,3584]{1,0:T(8,128)(2,1)S(1)}, bf16[64,3584]{1,0:T(8,128)(2,1)S(1)}, u32[]{:S(2)}, u32[]{:S(2)}) collective-permute-start(bf16[64,3584]{1,0:T(8,128)(2,1)S(1)} %get-tuple-element.33), channel_id=1, source_target_pairs={{0,2},{1,3},{2,0},{3,1},{4,6},{5,7},{6,4},{7,5},{8,10},{9,11},{10,... | collective-permute-start | bytes 1376264 | tf_op jit(solution)/shard_map/ppermute | solution.py:60
  45.3 24.2 %collective-permute-start.5 = (bf16[128,3584]{1,0:T(8,128)(2,1)S(1)}, bf16[128,3584]{1,0:T(8,128)(2,1)S(1)}, u32[]{:S(2)}, u32[]{:S(2)}) collective-permute-start(bf16[128,3584]{1,0:T(8,128)(2,1)S(1)} %collective-permute-done.1), channel_id=1, source_target_pairs={{0,8},{1,9},{2,10},{3,11},{4,0},{5,1},{6,2},{7,3},{8,12},{9,13},{1... | collective-permute-start | bytes 2752520 | tf_op jit(solution)/shard_map/ppermute | solution.py:60
  56.0 13.4 %copy-start.7 = (bf16[64,3584]{1,0:T(8,128)(2,1)}, bf16[64,3584]{1,0:T(8,128)(2,1)S(1)}, u32[]{:S(2)}) copy-start(bf16[64,3584]{1,0:T(8,128)(2,1)S(1)} %collective-permute-done) | copy-start | bytes 1376260
  65.3 4.1 %copy-start.9 = (bf16[64,3584]{1,0:T(8,128)(2,1)}, bf16[64,3584]{1,0:T(8,128)(2,1)S(1)}, u32[]{:S(2)}) copy-start(bf16[64,3584]{1,0:T(8,128)(2,1)S(1)} %collective-permute-done.2) | copy-start | bytes 1376260
  70.6 24.1 %copy-start.2 = (bf16[64,3584]{1,0:T(8,128)(2,1)}, bf16[64,3584]{1,0:T(8,128)(2,1)S(1)}, u32[]{:S(2)}) copy-start(bf16[64,3584]{1,0:T(8,128)(2,1)S(1)} %get-tuple-element.28) | copy-start | bytes 1376260
  70.6 12.3 %collective-permute-start.9 = (bf16[64,3584]{1,0:T(8,128)(2,1)}, bf16[64,3584]{1,0:T(8,128)(2,1)}, u32[]{:S(2)}, u32[]{:S(2)}) collective-permute-start(bf16[64,3584]{1,0:T(8,128)(2,1)} %get-tuple-element.29), channel_id=1, source_target_pairs={{0,2},{1,3},{2,0},{3,1},{4,6},{5,7},{6,4},{7,5},{8,10},{9,11},{10,... | collective-permute-start | bytes 1376264 | tf_op jit(solution)/shard_map/ppermute | solution.py:60
  70.9 21.8 %collective-permute-start.6 = (bf16[128,3584]{1,0:T(8,128)(2,1)S(1)}, bf16[128,3584]{1,0:T(8,128)(2,1)S(1)}, u32[]{:S(2)}, u32[]{:S(2)}) collective-permute-start(bf16[128,3584]{1,0:T(8,128)(2,1)S(1)} %collective-permute-done.5), channel_id=1, source_target_pairs={{0,8},{1,9},{2,10},{3,11},{4,0},{5,1},{6,2},{7,3},{8,12},{9,13},{1... | collective-permute-start | bytes 2752520 | tf_op jit(solution)/shard_map/ppermute | solution.py:60
  92.8 2.0 copy-start.14
  93.2 14.0 %copy-start.4 = (bf16[64,3584]{1,0:T(8,128)(2,1)}, bf16[64,3584]{1,0:T(8,128)(2,1)S(1)}, u32[]{:S(2)}) copy-start(bf16[64,3584]{1,0:T(8,128)(2,1)S(1)} %get-tuple-element.24) | copy-start | bytes 1376260
  93.2 11.1 %collective-permute-start.7 = (bf16[64,3584]{1,0:T(8,128)(2,1)S(1)}, bf16[64,3584]{1,0:T(8,128)(2,1)S(1)}, u32[]{:S(2)}, u32[]{:S(2)}) collective-permute-start(bf16[64,3584]{1,0:T(8,128)(2,1)S(1)} %get-tuple-element.25), channel_id=1, source_target_pairs={{0,2},{1,3},{2,0},{3,1},{4,6},{5,7},{6,4},{7,5},{8,10},{9,11},{10,... | collective-permute-start | bytes 1376264 | tf_op jit(solution)/shard_map/ppermute | solution.py:60
  104.4 9.2 %copy-start.12 = (bf16[64,3584]{1,0:T(8,128)(2,1)}, bf16[64,3584]{1,0:T(8,128)(2,1)S(1)}, u32[]{:S(2)}) copy-start(bf16[64,3584]{1,0:T(8,128)(2,1)S(1)} %collective-permute-done.7) | copy-start | bytes 1376260
  107.2 6.4 %copy-start.8 = (bf16[64,3584]{1,0:T(8,128)(2,1)S(1)}, bf16[64,3584]{1,0:T(8,128)(2,1)}, u32[]{:S(2)}) copy-start(bf16[64,3584]{1,0:T(8,128)(2,1)} %copy-done.7) | copy-start | bytes 1376260
  107.2 6.4 %copy-start.10 = (bf16[64,3584]{1,0:T(8,128)(2,1)S(1)}, bf16[64,3584]{1,0:T(8,128)(2,1)}, u32[]{:S(2)}) copy-start(bf16[64,3584]{1,0:T(8,128)(2,1)} %copy-done.9) | copy-start | bytes 1376260
  113.6 4.0 %copy-start.11 = (bf16[64,3584]{1,0:T(8,128)(2,1)S(1)}, bf16[64,3584]{1,0:T(8,128)(2,1)}, u32[]{:S(2)}) copy-start(bf16[64,3584]{1,0:T(8,128)(2,1)} %copy-done.9) | copy-start | bytes 1376260
  124.2 2.2 %copy-start.3 = (bf16[64,3584]{1,0:T(8,128)(2,1)S(1)}, bf16[64,3584]{1,0:T(8,128)(2,1)}, u32[]{:S(2)}) copy-start(bf16[64,3584]{1,0:T(8,128)(2,1)} %copy-done.2) | copy-start | bytes 1376260
  125.3 11.4 %collective-permute-start.11 = (bf16[64,3584]{1,0:T(8,128)(2,1)}, bf16[64,3584]{1,0:T(8,128)(2,1)}, u32[]{:S(2)}, u32[]{:S(2)}) collective-permute-start(bf16[64,3584]{1,0:T(8,128)(2,1)} %get-tuple-element.19), channel_id=1, source_target_pairs={{0,2},{1,3},{2,0},{3,1},{4,6},{5,7},{6,4},{7,5},{8,10},{9,11},{10,... | collective-permute-start | bytes 1376264 | tf_op jit(solution)/shard_map/ppermute | solution.py:60
  134.9 4.8 %copy-start.5 = (bf16[64,3584]{1,0:T(8,128)(2,1)S(1)}, bf16[64,3584]{1,0:T(8,128)(2,1)}, u32[]{:S(2)}) copy-start(bf16[64,3584]{1,0:T(8,128)(2,1)} %copy-done.4) | copy-start | bytes 1376260
  134.9 4.8 %copy-start.13 = (bf16[64,3584]{1,0:T(8,128)(2,1)S(1)}, bf16[64,3584]{1,0:T(8,128)(2,1)}, u32[]{:S(2)}) copy-start(bf16[64,3584]{1,0:T(8,128)(2,1)} %copy-done.12) | copy-start | bytes 1376260
  135.8 13.1 %collective-permute-start.10 = (bf16[64,3584]{1,0:T(8,128)(2,1)}, bf16[64,3584]{1,0:T(8,128)(2,1)}, u32[]{:S(2)}, u32[]{:S(2)}) collective-permute-start(bf16[64,3584]{1,0:T(8,128)(2,1)} %get-tuple-element.27), channel_id=1, source_target_pairs={{0,2},{1,3},{2,0},{3,1},{4,6},{5,7},{6,4},{7,5},{8,10},{9,11},{10,... | collective-permute-start | bytes 1376264 | tf_op jit(solution)/shard_map/ppermute | solution.py:60
  138.2 5.0 %copy-start.6 = (bf16[64,3584]{1,0:T(8,128)(2,1)S(1)}, bf16[64,3584]{1,0:T(8,128)(2,1)}, u32[]{:S(2)}) copy-start(bf16[64,3584]{1,0:T(8,128)(2,1)} %copy-done.4) | copy-start | bytes 1376260
  138.2 19.6 %collective-permute-start.12 = (bf16[128,3584]{1,0:T(8,128)(2,1)S(1)}, bf16[128,3584]{1,0:T(8,128)(2,1)}, u32[]{:S(2)}, u32[]{:S(2)}) collective-permute-start(bf16[128,3584]{1,0:T(8,128)(2,1)S(1)} %convolution_convert_fusion), channel_id=1, source_target_pairs={{0,8},{1,9},{2,10},{3,11},{4,0},{5,1},{6,2},{7,3},{8,12},{9,13},{1... | collective-permute-start | bytes 2752520 | tf_op jit(solution)/shard_map/ppermute | solution.py:60
  157.8 25.1 %copy-start.1 = (bf16[64,3584]{1,0:T(8,128)(2,1)S(1)}, bf16[64,3584]{1,0:T(8,128)(2,1)}, u32[]{:S(2)}) copy-start(bf16[64,3584]{1,0:T(8,128)(2,1)} %get-tuple-element.21) | copy-start | bytes 1376260
  159.6 19.4 %collective-permute-start.13 = (bf16[128,3584]{1,0:T(8,128)(2,1)S(1)}, bf16[128,3584]{1,0:T(8,128)(2,1)S(1)}, u32[]{:S(2)}, u32[]{:S(2)}) collective-permute-start(bf16[128,3584]{1,0:T(8,128)(2,1)S(1)} %fusion.5), channel_id=1, source_target_pairs={{0,8},{1,9},{2,10},{3,11},{4,0},{5,1},{6,2},{7,3},{8,12},{9,13},{1... | collective-permute-start | bytes 2752520 | tf_op jit(solution)/shard_map/ppermute | solution.py:60
  162.4 8.8 %collective-permute-start.8 = (bf16[64,3584]{1,0:T(8,128)(2,1)S(1)}, bf16[64,3584]{1,0:T(8,128)(2,1)S(1)}, u32[]{:S(2)}, u32[]{:S(2)}) collective-permute-start(bf16[64,3584]{1,0:T(8,128)(2,1)S(1)} %get-tuple-element.23), channel_id=1, source_target_pairs={{0,2},{1,3},{2,0},{3,1},{4,6},{5,7},{6,4},{7,5},{8,10},{9,11},{10,... | collective-permute-start | bytes 1376264 | tf_op jit(solution)/shard_map/ppermute | solution.py:60
  179.4 18.9 %collective-permute-start.14 = (bf16[128,3584]{1,0:T(8,128)(2,1)S(1)}, bf16[128,3584]{1,0:T(8,128)(2,1)S(1)}, u32[]{:S(2)}, u32[]{:S(2)}) collective-permute-start(bf16[128,3584]{1,0:T(8,128)(2,1)S(1)} %fusion.3), channel_id=1, source_target_pairs={{0,8},{1,9},{2,10},{3,11},{4,0},{5,1},{6,2},{7,3},{8,12},{9,13},{1... | collective-permute-start | bytes 2752520 | tf_op jit(solution)/shard_map/ppermute | solution.py:60
  182.8 8.5 %collective-permute-start.4 = (bf16[64,3584]{1,0:T(8,128)(2,1)S(1)}, bf16[64,3584]{1,0:T(8,128)(2,1)S(1)}, u32[]{:S(2)}, u32[]{:S(2)}) collective-permute-start(bf16[64,3584]{1,0:T(8,128)(2,1)S(1)} %copy-done.1), channel_id=1, source_target_pairs={{0,2},{1,3},{2,0},{3,1},{4,6},{5,7},{6,4},{7,5},{8,10},{9,11},{10,... | collective-permute-start | bytes 1376264 | tf_op jit(solution)/shard_map/ppermute | solution.py:60

commit v2 on v0

v2 whole, which is shorter than its diff:
```python
import functools

import jax
import jax.numpy as jnp
from jax import lax
from jax.experimental import pallas as pl
from jax.experimental.pallas import tpu as pltpu
from jax.sharding import PartitionSpec as P

CORES = 2
LANES = 128
LARGE_VMEM = 60 * 1024 * 1024
VMEM_LIMIT = 48 * 1024 * 1024
SMALL_VMEM = 16 * 1024 * 1024
CHUNK = 896


def grid_of(chips):
    inner = 1
    while (2 * inner) * (2 * inner) <= chips and chips % (2 * inner) == 0:
        inner *= 2
    return chips // inner, inner


def ring_of(length):
    return [p for p in range(length) if p % 2 == 0] + [p for p in reversed(range(length)) if p % 2 == 1]


def tile_of(size, most):
    tile = most
    while size % tile:
        tile -= 128
    return tile


ANYWHERE = pl.BlockSpec(memory_space=pl.ANY)
WHOLE = pl.BlockSpec(memory_space=pltpu.VMEM)


def rows_cost(rows, width):
    return pl.CostEstimate(flops=2 * rows * width, bytes_accessed=4 * rows * width, transcendentals=0)


def eye_of(size):
    row = lax.broadcasted_iota(jnp.int32, (size, size), 0)
    column = lax.broadcasted_iota(jnp.int32, (size, size), 1)
    return row, column


def label_kernel(tokens_ref, experts_ref, copies_ref, gates_ref, out_ref, experts_scr, copies_scr, gates_scr, sem):
    width = tokens_ref.shape[1]
    top_k, tokens = experts_ref.shape
    moves = [
        pltpu.make_async_copy(experts_ref, experts_scr, sem.at[0]),
        pltpu.make_async_copy(copies_ref, copies_scr, sem.at[1]),
        pltpu.make_async_copy(gates_ref, gates_scr, sem.at[2]),
        pltpu.make_async_copy(tokens_ref, out_ref.at[:, pl.ds(0, width)], sem.at[3]),
    ]
    for move in moves:
        move.start()
    for move in moves[:3]:
        move.wait()
    lane = lax.broadcasted_iota(jnp.int32, (LANES, tokens), 0)
    labels = jnp.zeros((LANES, tokens), jnp.float32)
    for k in range(top_k):
        for i, ref in enumerate((experts_scr, copies_scr, gates_scr)):
            values = jnp.broadcast_to(ref[k : k + 1, :].astype(jnp.float32), (LANES, tokens))
            labels = jnp.where(lane == i * top_k + k, values, labels)
    row, column = eye_of(LANES)
    eye = jnp.where(row == column, 1.0, 0.0).astype(jnp.bfloat16)
    turned = lax.dot_general(
        labels.astype(jnp.bfloat16), eye, (((0,), (0,)), ((), ())), preferred_element_type=jnp.float32
    )
    out_ref[:, width:] = turned.astype(jnp.bfloat16)
    moves[3].wait()


def label_rows(tokens, experts, copies, gates):
    rows, width = tokens.shape
    return pl.pallas_call(
        label_kernel,
        out_shape=jax.ShapeDtypeStruct((rows, width + LANES), jnp.bfloat16),
        in_specs=[ANYWHERE] * 4,
        out_specs=WHOLE,
        scratch_shapes=[
            pltpu.VMEM(experts.shape, experts.dtype),
            pltpu.VMEM(copies.shape, copies.dtype),
            pltpu.VMEM(gates.shape, gates.dtype),
            pltpu.SemaphoreType.DMA((4,)),
        ],
        compiler_params=pltpu.CompilerParams(vmem_limit_bytes=LARGE_VMEM),
        cost_estimate=rows_cost(rows, width),
    )(tokens, experts, copies, gates)


def dispatch_kernel(scalars, block_ref, *refs, inner, top_k, behind):
    rows_refs, combine_ref, counts_ref = refs[behind : behind + inner], refs[behind + inner], refs[behind + inner + 1]
    tokens = block_ref.shape[0]
    slots, width = rows_refs[0].shape
    base, col = scalars[0], scalars[1]
    row, column = eye_of(tokens)
    eye = jnp.where(row == column, 1.0, 0.0).astype(jnp.bfloat16)
    upto = jnp.where(row <= column, 1.0, 0.0).astype(jnp.bfloat16)
    labels = lax.dot_general(
        block_ref[:, width:], eye, (((0,), (0,)), ((), ())), preferred_element_type=jnp.float32
    )
    slot = lax.broadcasted_iota(jnp.int32, (slots, tokens), 0)
    lane = lax.broadcasted_iota(jnp.int32, (1, LANES), 1)
    counts_ref[...] = jnp.zeros_like(counts_ref)
    for j in range(inner):
        wanted = (base + lax.rem(col + j, inner)).astype(jnp.float32)
        hit = jnp.zeros((1, tokens), jnp.float32)
        weight = jnp.zeros((1, tokens), jnp.float32)
        upper = jnp.zeros((1, tokens), jnp.float32)
        for k in range(top_k):
            same = labels[k : k + 1] == wanted
            hit = hit + jnp.where(same, 1.0, 0.0)
            upper = upper + jnp.where(same, labels[top_k + k : top_k + k + 1], 0.0)
            weight = weight + jnp.where(same, labels[2 * top_k + k : 2 * top_k + k + 1], 0.0)
        wide = jnp.broadcast_to(hit, (8, tokens)).astype(jnp.bfloat16)
        rank = jnp.dot(wide, upto, preferred_element_type=jnp.float32)[:1].astype(jnp.int32) - 1
        chosen = (slot == rank) & (hit > 0.5)
        pack = jnp.where(chosen, 1.0, 0.0).astype(jnp.bfloat16)
        combine_ref[j] = jnp.where(chosen, weight, 0.0).astype(jnp.bfloat16)
        rows_refs[j][...] = jnp.dot(pack, block_ref[:, :width], preferred_element_type=jnp.float32).astype(jnp.bfloat16)
        ones = jnp.sum(upper, axis=1, keepdims=True)
        zeros = jnp.sum(hit, axis=1, keepdims=True) - ones
        counts_ref[j : j + 1, :] = jnp.where(lane == 0, zeros, jnp.where(lane == 1, ones, 0.0))


def dispatch_rows(scalars, block, top_k, inner, slots, after=()):
    tokens, width = block.shape
    width -= LANES
    outs = pl.pallas_call(
        functools.partial(dispatch_kernel, inner=inner, top_k=top_k, behind=len(after)),
        out_shape=[jax.ShapeDtypeStruct((slots, width), jnp.bfloat16)] * inner
        + [
            jax.ShapeDtypeStruct((inner, slots, tokens), jnp.bfloat16),
            jax.ShapeDtypeStruct((-(-inner // 8) * 8, LANES), jnp.float32),
        ],
        in_specs=[pl.BlockSpec(memory_space=pltpu.SMEM), WHOLE] + [ANYWHERE] * len(after),
        out_specs=[WHOLE] * (inner + 2),
        compiler_params=pltpu.CompilerParams(vmem_limit_bytes=SMALL_VMEM),
        cost_estimate=rows_cost(tokens, width),
    )(scalars, block, *after)
    return list(outs[:inner]), outs[inner], outs[inner + 1]


def combine_kernel(combine_ref, *refs, inner, carried, behind):
    out_ref = refs[-1]
    total = refs[inner][...].astype(jnp.float32) if carried else None
    for j in range(inner):
        part = lax.dot_general(
            combine_ref[j], refs[j][...], (((0,), (0,)), ((), ())), preferred_element_type=jnp.float32
        )
        total = part if total is None else total + part
    out_ref[...] = total.astype(jnp.bfloat16)


def combine_rows(table, rows, carried=(), after=()):
    inner, _, tokens = table.shape
    width = rows[0].shape[1]
    return pl.pallas_call(
        functools.partial(combine_kernel, inner=inner, carried=len(carried), behind=len(after)),
        out_shape=jax.ShapeDtypeStruct((tokens, width), jnp.bfloat16),
        in_specs=[WHOLE] * (1 + inner + len(carried)) + [ANYWHERE] * len(after),
        out_specs=WHOLE,
        compiler_params=pltpu.CompilerParams(vmem_limit_bytes=SMALL_VMEM),
        cost_estimate=rows_cost(tokens, width),
    )(table, *rows, *carried, *after)


def expert_kernel(*refs, pieces, behind, chunks):
    row_refs = refs[:pieces]
    weights = refs[pieces : pieces + 2]
    out_refs = refs[pieces + 2 + behind : 2 * pieces + 2 + behind]
    rows_scr, hidden_scr, own_scr, other_scr, up_sem, down_sem = refs[2 * pieces + 2 + behind :]
    held = (own_scr, other_scr)
    slots = row_refs[0].shape[0]
    chunk = rows_scr.shape[2]

    def up_copy(half, k):
        part = (pl.ds(0, 2), pl.ds(k * chunk, chunk))
        return pltpu.make_async_copy(weights[half].at[part], held[half].at[part], up_sem.at[half, k])

    def down_copy(half, k):
        part = (pl.ds(2, 1), pl.ds(k * chunk, chunk))
        return pltpu.make_async_copy(weights[half].at[part], held[half].at[part], down_sem.at[half, k])

    for half in range(2):
        for k in range(chunks):
            up_copy(half, k).start()
    for k in range(chunks):
        for half in range(2):
            down_copy(half, k).start()
    for i in range(pieces):
        for k in range(chunks):
            rows_scr[k, i * slots : (i + 1) * slots, :] = row_refs[i][:, k * chunk : (k + 1) * chunk]
    for half in range(2):
        gate_act = up_act = None
        for k in range(chunks):
            up_copy(half, k).wait()
            rows = rows_scr[k]
            gate_part = jnp.dot(rows, held[half][0, k * chunk : (k + 1) * chunk], preferred_element_type=jnp.float32)
            up_part = jnp.dot(rows, held[half][1, k * chunk : (k + 1) * chunk], preferred_element_type=jnp.float32)
            gate_act = gate_part if k == 0 else gate_act + gate_part
            up_act = up_part if k == 0 else up_act + up_part
        hidden_scr[half] = (jax.nn.silu(gate_act) * up_act).astype(jnp.bfloat16)
    for k in range(chunks):
        out = None
        for half in range(2):
            down_copy(half, k).wait()
            part = lax.dot_general(
                hidden_scr[half],
                held[half][2, k * chunk : (k + 1) * chunk],
                (((1,), (1,)), ((), ())),
                preferred_element_type=jnp.float32,
            )
            out = part if half == 0 else out + part
        out = out.astype(jnp.bfloat16)
        for i in range(pieces):
            out_refs[i][:, k * chunk : (k + 1) * chunk] = out[i * slots : (i + 1) * slots]


def expert_rows(pieces, own, other, after=()):
    count = len(pieces)
    slots, width = pieces[0].shape
    units = own.shape[2]
    chunk = tile_of(width, CHUNK)
    chunks = width // chunk
    rows = count * slots
    outs = pl.pallas_call(
        functools.partial(expert_kernel, pieces=count, behind=len(after), chunks=chunks),
        out_shape=[jax.ShapeDtypeStruct((slots, width), jnp.bfloat16)] * count,
        in_specs=[WHOLE] * count + [ANYWHERE] * (2 + len(after)),
        out_specs=[WHOLE] * count,
        scratch_shapes=[
            pltpu.VMEM((chunks, rows, chunk), jnp.bfloat16),
            pltpu.VMEM((2, rows, units), jnp.bfloat16),
            pltpu.VMEM(own.shape, jnp.bfloat16),
            pltpu.VMEM(own.shape, jnp.bfloat16),
            pltpu.SemaphoreType.DMA((2, chunks)),
            pltpu.SemaphoreType.DMA((2, chunks)),
        ],
        compiler_params=pltpu.CompilerParams(vmem_limit_bytes=VMEM_LIMIT),
        cost_estimate=pl.CostEstimate(flops=1000, bytes_accessed=1000, transcendentals=0),
    )(*pieces, own, other, *after)
    return list(outs)


def on_device(tokens, expert_weights, expert_ids, copy_ids, gate_weights):
    devices = lax.axis_size("expert")
    experts = devices // CORES
    outer, inner = grid_of(experts)
    tok_rows, top_k = expert_ids.shape
    slots = -(-2 * (tok_rows * top_k // experts) // 16) * 16
    me = lax.axis_index("expert").astype(jnp.int32)
    chip = lax.div(me, CORES)
    col = lax.rem(chip, inner)
    plane = lax.div(chip, inner)
    ring = ring_of(outer)

    def device_of(p, q, c):
        return (p * inner + q) * CORES + c

    every = [(p, q, c) for p in range(outer) for q in range(inner) for c in range(CORES)]

    def ring_pairs(shift):
        return [
            (device_of(p, q, c), device_of(ring[(ring.index(p) + shift) % outer], q, c)) for p, q, c in every
        ]

    def column_pairs(shift):
        return [(device_of(p, q, c), device_of(p, (q + shift) % inner, c)) for p, q, c in every]

    core_pairs = [(device_of(p, q, c), device_of(p, q, 1 - c)) for p, q, c in every]

    def permute(x, pairs):
        return lax.ppermute(x, "expert", pairs)

    blocks = [label_rows(tokens, expert_ids.T, copy_ids.T, gate_weights.T)]
    scalars = jnp.stack([plane * inner, col])
    other_weights = permute(expert_weights, core_pairs)

    def dispatch(step, after=()):
        rows, table, counts = dispatch_rows(scalars, blocks[step], top_k, inner, slots, after)
        arrived = rows[:1] + [permute(rows[shift], column_pairs(shift)) for shift in range(1, inner)]
        return arrived, table, counts

    def send_back(rows):
        return rows[:1] + [permute(rows[shift], column_pairs(-shift)) for shift in range(1, inner)]

    def run(pieces, after=()):
        return expert_rows(pieces, expert_weights, other_weights, after)

    def behind(x, *others):
        return lax.optimization_barrier((x,) + others)[0]

    def pass_on(step, carry):
        return (permute(combine_rows(sent[step][1], back[step], carry), ring_pairs(1)),)

    sent = {0: dispatch(0)}
    blocks.append(permute(blocks[0], ring_pairs(1)))
    blocks[1] = behind(blocks[1], sent[0][0][-1])
    sent[1] = dispatch(1)
    results = {}
    for step in range(2, outer):
        block = behind(blocks[-1], sent[step - 1][1])
        if step == 3:
            results[1] = run(sent[1][0])
            block = behind(block, results[1][0])
        blocks.append(permute(block, ring_pairs(1)))
        if step == 3:
            results[2] = run(sent[2][0])
            blocks[3] = behind(blocks[3], results[2][0])
        sent[step] = dispatch(step)
    for step in list(range(1, outer)) + [0]:
        if step not in results:
            pieces = sent[step][0]
            if step == 2 and outer > 3 and False:
                pieces = [behind(pieces[0], sent[3][1])] + pieces[1:]
            if step == 0:
                pieces = [behind(pieces[0], results[outer - 1][0])] + pieces[1:]
            results[step] = run(pieces)
    back = {}
    for step in range(outer):
        back[step] = send_back(results[step])
    carry = ()
    for step in range(1, outer):
        carry = pass_on(step, carry)
    moe_out = combine_rows(sent[0][1], back[0], carry)

    counts = sum(sent[step][2] for step in range(outer))
    counts = counts + permute(counts, core_pairs)
    served = counts[:1]
    for shift in range(1, inner):
        served = served + permute(counts[shift : shift + 1], column_pairs(shift))
    return moe_out, served[:, :2].astype(jnp.int32)


def solution(mesh):
    return jax.shard_map(
        on_device,
        mesh=mesh,
        in_specs=(
            P(("groups", "expert"), None),
            P(None, None, "expert"),
            P(("groups", "expert"), None),
            P(("groups", "expert"), None),
            P(("groups", "expert"), None),
        ),
        out_specs=(P(("groups", "expert"), None), P(("groups", "expert"), None)),
        check_vma=False,
    )
```

time: 428 us -> 144 us (0.34)
  the two profiles are of different devices: /device:TPU:18 before, /device:TPU:0 now
where the time goes in v2:
time: 144 us; the launch traced here: 143 us
  waiting for transfers between devices  68.4 us (48%)
  Pallas kernels  47.6 us (33%)
  starting transfers between devices  24.9 us (17%)
    ppermute x17, waiting for transfers between devices, permute(): return lax.ppermute(x, 'expert', pairs)  68.4 us
    pallas_call x4, Pallas kernels, expert_rows(): pl.pallas_call(functools.partial(expert_kernel, pieces=count, behind=len(...  36.4 us
    ppermute x17, starting transfers between devices, permute(): return lax.ppermute(x, 'expert', pairs)  24.9 us
    pallas_call x4, Pallas kernels, dispatch_rows(): pl.pallas_call(functools.partial(dispatch_kernel, inner=inner, top_k=top_...  5.47 us
    pallas_call x4, Pallas kernels, combine_rows(): pl.pallas_call(functools.partial(combine_kernel, inner=inner, carried=len...  3.56 us
  transfers between devices with their start and end apart: 17, of which 11 were waited for; matrix products, arithmetic and copies ran while one was open for 0% of the time, Pallas kernels for 32%

profile of v2, /device:TPU:0, one launch (start us, length us, event | category | flops | bytes accessed | tf_op | source)
XLA Modules:
  0.0 143.5 jit_solution(13784707299817257201)
XLA Ops:
  1.1 2.2 %shard_map.68.block_ref = bf16[128,3712]{1,0:T(8,128)(2,1)} custom-call(bf16[128,3584]{1,0:T(8,128)(2,1)} %tokens_ref.1, s32[2,128]{1,0:T(2,128)} %bitcast.5, s32[2,128]{1,0:T(2,128)} %bitcast.6, bf16[2,128]{1,0:T(2,128)(2,1)} %bitcast.7), custom_call_target="tpu_custom_call" | custom-call | flops 917504 | bytes 1835008 | tf_op jit(solution)/shard_map/pallas_call | solution.py:80
  3.3 3.7 %collective-permute-start = (bf16[128,3712]{1,0:T(8,128)(2,1)}, bf16[128,3712]{1,0:T(8,128)(2,1)S(1)}, u32[]{:S(2)}, u32[]{:S(2)}) collective-permute-start(bf16[128,3712]{1,0:T(8,128)(2,1)} %shard_map.68.block_ref), channel_id=1, source_target_pairs={{0,8},{1,9},{2,10},{3,11},{4,0},{5,1},{6,2},{7,3},{8,12},{9,13},{1... | collective-permute-start | bytes 2850824 | tf_op jit(solution)/shard_map/ppermute | solution.py:279
  7.1 1.2 copy-done
  8.3 1.4 shard_map.69
  9.6 1.6 %collective-permute-start.1 = (bf16[64,3584]{1,0:T(8,128)(2,1)S(1)}, bf16[64,3584]{1,0:T(8,128)(2,1)S(1)}, u32[]{:S(2)}, u32[]{:S(2)}) collective-permute-start(bf16[64,3584]{1,0:T(8,128)(2,1)S(1)} %get-tuple-element.34), channel_id=1, source_target_pairs={{0,2},{1,3},{2,0},{3,1},{4,6},{5,7},{6,4},{7,5},{8,10},{9,11},{10,... | collective-permute-start | bytes 1376264 | tf_op jit(solution)/shard_map/ppermute | solution.py:279
  11.2 11.1 %collective-permute-done.1.refs_1_ = bf16[64,3584]{1,0:T(8,128)(2,1)S(1)} collective-permute-done((bf16[64,3584]{1,0:T(8,128)(2,1)S(1)}, bf16[64,3584]{1,0:T(8,128)(2,1)S(1)}, u32[]{:S(2)}, u32[]{:S(2)}) %collective-permute-start.1) | collective-permute-done | bytes 458784 | tf_op jit(solution)/shard_map/ppermute | solution.py:279
  22.3 5.9 %collective-permute-done.block_ref = bf16[128,3712]{1,0:T(8,128)(2,1)S(1)} collective-permute-done((bf16[128,3712]{1,0:T(8,128)(2,1)}, bf16[128,3712]{1,0:T(8,128)(2,1)S(1)}, u32[]{:S(2)}, u32[]{:S(2)}) %collective-permute-start) | collective-permute-done | bytes 950304 | tf_op jit(solution)/shard_map/ppermute | solution.py:279
  28.3 1.4 shard_map.70
  29.7 3.3 %collective-permute-start.2 = (bf16[128,3712]{1,0:T(8,128)(2,1)S(1)}, bf16[128,3712]{1,0:T(8,128)(2,1)S(1)}, u32[]{:S(2)}, u32[]{:S(2)}) collective-permute-start(bf16[128,3712]{1,0:T(8,128)(2,1)S(1)} %collective-permute-done.block_ref), channel_id=1, source_target_pairs={{0,8},{1,9},{2,10},{3,11},{4,0},{5,1},{6,2},{7,3},{8,12},{9,13},{1... | collective-permute-start | bytes 2850824 | tf_op jit(solution)/shard_map/ppermute | solution.py:279
  33.0 1.5 %collective-permute-start.3 = (bf16[64,3584]{1,0:T(8,128)(2,1)S(1)}, bf16[64,3584]{1,0:T(8,128)(2,1)S(1)}, u32[]{:S(2)}, u32[]{:S(2)}) collective-permute-start(bf16[64,3584]{1,0:T(8,128)(2,1)S(1)} %get-tuple-element.41), channel_id=1, source_target_pairs={{0,2},{1,3},{2,0},{3,1},{4,6},{5,7},{6,4},{7,5},{8,10},{9,11},{10,... | collective-permute-start | bytes 1376264 | tf_op jit(solution)/shard_map/ppermute | solution.py:279
  34.5 10.3 %collective-permute-done.3.refs_1_ = bf16[64,3584]{1,0:T(8,128)(2,1)S(1)} collective-permute-done((bf16[64,3584]{1,0:T(8,128)(2,1)S(1)}, bf16[64,3584]{1,0:T(8,128)(2,1)S(1)}, u32[]{:S(2)}, u32[]{:S(2)}) %collective-permute-start.3) | collective-permute-done | bytes 458784 | tf_op jit(solution)/shard_map/ppermute | solution.py:279
  44.8 9.1 %shard_map.72 = (bf16[64,3584]{1,0:T(8,128)(2,1)S(1)}, bf16[64,3584]{1,0:T(8,128)(2,1)S(1)}) custom-call(bf16[64,3584]{1,0:T(8,128)(2,1)S(1)} %get-tuple-element.40.refs_0_, bf16[64,3584]{1,0:T(8,128)(2,1)S(1)} %collective-permute-done.3.refs_1_, bf16[3,3584,512]{2,1,0:T(8,128)(2,1)} %refs_2_.7, bf16[3,3584,512]{2,1,0:T(8,128)(2,1)} %collective-permute-done.4.refs_3_), custom_call_target="tpu_custom_call" | custom-call | flops 1000 | bytes 1000 | tf_op jit(solution)/shard_map/pallas_call | solution.py:232
  54.0 1.6 %collective-permute-start.11 = (bf16[64,3584]{1,0:T(8,128)(2,1)S(1)}, bf16[64,3584]{1,0:T(8,128)(2,1)S(1)}, u32[]{:S(2)}, u32[]{:S(2)}) collective-permute-start(bf16[64,3584]{1,0:T(8,128)(2,1)S(1)} %get-tuple-element.57), channel_id=1, source_target_pairs={{0,2},{1,3},{2,0},{3,1},{4,6},{5,7},{6,4},{7,5},{8,10},{9,11},{10,... | collective-permute-start | bytes 1376264 | tf_op jit(solution)/shard_map/ppermute | solution.py:279
  55.5 1.4 shard_map.71
  56.9 1.1 collective-permute-start.5
  58.0 1.5 %collective-permute-start.6 = (bf16[64,3584]{1,0:T(8,128)(2,1)S(1)}, bf16[64,3584]{1,0:T(8,128)(2,1)S(1)}, u32[]{:S(2)}, u32[]{:S(2)}) collective-permute-start(bf16[64,3584]{1,0:T(8,128)(2,1)S(1)} %get-tuple-element.45), channel_id=1, source_target_pairs={{0,2},{1,3},{2,0},{3,1},{4,6},{5,7},{6,4},{7,5},{8,10},{9,11},{10,... | collective-permute-start | bytes 1376264 | tf_op jit(solution)/shard_map/ppermute | solution.py:279
  59.5 8.0 %collective-permute-done.11.refs_1_ = bf16[64,3584]{1,0:T(8,128)(2,1)S(1)} collective-permute-done((bf16[64,3584]{1,0:T(8,128)(2,1)S(1)}, bf16[64,3584]{1,0:T(8,128)(2,1)S(1)}, u32[]{:S(2)}, u32[]{:S(2)}) %collective-permute-start.11) | collective-permute-done | bytes 458784 | tf_op jit(solution)/shard_map/ppermute | solution.py:279
  68.9 5.9 %collective-permute-done.6.refs_1_ = bf16[64,3584]{1,0:T(8,128)(2,1)S(1)} collective-permute-done((bf16[64,3584]{1,0:T(8,128)(2,1)S(1)}, bf16[64,3584]{1,0:T(8,128)(2,1)S(1)}, u32[]{:S(2)}, u32[]{:S(2)}) %collective-permute-start.6) | collective-permute-done | bytes 458784 | tf_op jit(solution)/shard_map/ppermute | solution.py:279
  74.8 9.1 %shard_map.73 = (bf16[64,3584]{1,0:T(8,128)(2,1)S(1)}, bf16[64,3584]{1,0:T(8,128)(2,1)S(1)}) custom-call(bf16[64,3584]{1,0:T(8,128)(2,1)S(1)} %get-tuple-element.44.refs_0_, bf16[64,3584]{1,0:T(8,128)(2,1)S(1)} %collective-permute-done.6.refs_1_, bf16[3,3584,512]{2,1,0:T(8,128)(2,1)} %refs_2_.7, bf16[3,3584,512]{2,1,0:T(8,128)(2,1)} %collective-permute-done.4.refs_3_), custom_call_target="tpu_custom_call" | custom-call | flops 1000 | bytes 1000 | tf_op jit(solution)/shard_map/pallas_call | solution.py:232
  83.9 1.6 %collective-permute-start.10 = (bf16[64,3584]{1,0:T(8,128)(2,1)S(1)}, bf16[64,3584]{1,0:T(8,128)(2,1)S(1)}, u32[]{:S(2)}, u32[]{:S(2)}) collective-permute-start(bf16[64,3584]{1,0:T(8,128)(2,1)S(1)} %get-tuple-element.56), channel_id=1, source_target_pairs={{0,2},{1,3},{2,0},{3,1},{4,6},{5,7},{6,4},{7,5},{8,10},{9,11},{10,... | collective-permute-start | bytes 1376264 | tf_op jit(solution)/shard_map/ppermute | solution.py:279
  85.5 1.4 shard_map.74
  87.4 10.0 %collective-permute-done.10.refs_1_ = bf16[64,3584]{1,0:T(8,128)(2,1)S(1)} collective-permute-done((bf16[64,3584]{1,0:T(8,128)(2,1)S(1)}, bf16[64,3584]{1,0:T(8,128)(2,1)S(1)}, u32[]{:S(2)}, u32[]{:S(2)}) %collective-permute-start.10) | collective-permute-done | bytes 458784 | tf_op jit(solution)/shard_map/ppermute | solution.py:279
  98.5 2.7 %collective-permute-start.13 = (bf16[128,3584]{1,0:T(8,128)(2,1)S(1)}, bf16[128,3584]{1,0:T(8,128)(2,1)S(1)}, u32[]{:S(2)}, u32[]{:S(2)}) collective-permute-start(bf16[128,3584]{1,0:T(8,128)(2,1)S(1)} %shard_map.78), channel_id=1, source_target_pairs={{0,8},{1,9},{2,10},{3,11},{4,0},{5,1},{6,2},{7,3},{8,12},{9,13},{1... | collective-permute-start | bytes 2752520 | tf_op jit(solution)/shard_map/ppermute | solution.py:279
  101.2 2.6 %collective-permute-done.7.refs_1_ = bf16[64,3584]{1,0:T(8,128)(2,1)S(1)} collective-permute-done((bf16[64,3584]{1,0:T(8,128)(2,1)S(1)}, bf16[64,3584]{1,0:T(8,128)(2,1)S(1)}, u32[]{:S(2)}, u32[]{:S(2)}) %collective-permute-start.7) | collective-permute-done | bytes 458784 | tf_op jit(solution)/shard_map/ppermute | solution.py:279
  103.8 9.1 %shard_map.75 = (bf16[64,3584]{1,0:T(8,128)(2,1)S(1)}, bf16[64,3584]{1,0:T(8,128)(2,1)S(1)}) custom-call(bf16[64,3584]{1,0:T(8,128)(2,1)S(1)} %get-tuple-element.48.refs_0_, bf16[64,3584]{1,0:T(8,128)(2,1)S(1)} %collective-permute-done.7.refs_1_, bf16[3,3584,512]{2,1,0:T(8,128)(2,1)} %refs_2_.7, bf16[3,3584,512]{2,1,0:T(8,128)(2,1)} %collective-permute-done.4.refs_3_), custom_call_target="tpu_custom_call" | custom-call | flops 1000 | bytes 1000 | tf_op jit(solution)/shard_map/pallas_call | solution.py:232
  112.9 1.6 %collective-permute-start.9 = (bf16[64,3584]{1,0:T(8,128)(2,1)S(1)}, bf16[64,3584]{1,0:T(8,128)(2,1)S(1)}, u32[]{:S(2)}, u32[]{:S(2)}) collective-permute-start(bf16[64,3584]{1,0:T(8,128)(2,1)S(1)} %get-tuple-element.55), channel_id=1, source_target_pairs={{0,2},{1,3},{2,0},{3,1},{4,6},{5,7},{6,4},{7,5},{8,10},{9,11},{10,... | collective-permute-start | bytes 1376264 | tf_op jit(solution)/shard_map/ppermute | solution.py:279
  114.5 7.5 %collective-permute-done.9.refs_1_ = bf16[64,3584]{1,0:T(8,128)(2,1)S(1)} collective-permute-done((bf16[64,3584]{1,0:T(8,128)(2,1)S(1)}, bf16[64,3584]{1,0:T(8,128)(2,1)S(1)}, u32[]{:S(2)}, u32[]{:S(2)}) %collective-permute-start.9) | collective-permute-done | bytes 458784 | tf_op jit(solution)/shard_map/ppermute | solution.py:279
  123.5 9.1 %shard_map.76 = (bf16[64,3584]{1,0:T(8,128)(2,1)S(1)}, bf16[64,3584]{1,0:T(8,128)(2,1)S(1)}) custom-call(bf16[64,3584]{1,0:T(8,128)(2,1)S(1)} %get-tuple-element.51.refs_0_, bf16[64,3584]{1,0:T(8,128)(2,1)S(1)} %collective-permute-done.1.refs_1_, bf16[3,3584,512]{2,1,0:T(8,128)(2,1)} %refs_2_.7, bf16[3,3584,512]{2,1,0:T(8,128)(2,1)} %collective-permute-done.4.refs_3_), custom_call_target="tpu_custom_call" | custom-call | flops 1000 | bytes 1000 | tf_op jit(solution)/shard_map/pallas_call | solution.py:232
  132.6 1.6 %collective-permute-start.8 = (bf16[64,3584]{1,0:T(8,128)(2,1)S(1)}, bf16[64,3584]{1,0:T(8,128)(2,1)S(1)}, u32[]{:S(2)}, u32[]{:S(2)}) collective-permute-start(bf16[64,3584]{1,0:T(8,128)(2,1)S(1)} %get-tuple-element.53), channel_id=1, source_target_pairs={{0,2},{1,3},{2,0},{3,1},{4,6},{5,7},{6,4},{7,5},{8,10},{9,11},{10,... | collective-permute-start | bytes 1376264 | tf_op jit(solution)/shard_map/ppermute | solution.py:279
  134.2 1.2 collective-permute-done.15
  135.9 5.5 %collective-permute-done.16 = f32[1,128]{1,0:T(1,128)S(1)} collective-permute-done((f32[1,128]{1,0:T(1,128)S(1)}, f32[1,128]{1,0:T(1,128)S(1)}, u32[]{:S(2)}, u32[]{:S(2)}) %collective-permute-start.16) | collective-permute-done | bytes 544 | tf_op jit(solution)/shard_map/ppermute | solution.py:279
  141.9 1.6 %shard_map.80 = bf16[128,3584]{1,0:T(8,128)(2,1)} custom-call(bf16[2,64,128]{2,1,0:T(8,128)(2,1)S(1)} %get-tuple-element.32.combine_ref, bf16[64,3584]{1,0:T(8,128)(2,1)S(1)} %get-tuple-element.52.refs_0_, bf16[64,3584]{1,0:T(8,128)(2,1)S(1)} %collective-permute-done.8.refs_1_, bf16[128,3584]{1,0:T(8,128)(2,1)S(1)} %collective-permute-done.14.refs_2_), custom_call_target="tpu_custom_call" | custom-call | flops 917504 | bytes 1835008 | tf_op jit(solution)/shard_map/pallas_call | solution.py:163
  (23 shorter events, 6.2 us)
Async XLA Ops:
  0.6 44.2 %collective-permute-start.4 = (bf16[3,3584,512]{2,1,0:T(8,128)(2,1)}, bf16[3,3584,512]{2,1,0:T(8,128)(2,1)}, u32[]{:S(2)}, u32[]{:S(2)}) collective-permute-start(bf16[3,3584,512]{2,1,0:T(8,128)(2,1)} %refs_2_.7), channel_id=1, source_target_pairs={{0,1},{1,0},{2,3},{3,2},{4,5},{5,4},{6,7},{7,6},{8,9},{9,8},{10,11... | collective-permute-start | bytes 33030152 | tf_op jit(solution)/shard_map/ppermute | solution.py:279
  3.3 24.9 %collective-permute-start = (bf16[128,3712]{1,0:T(8,128)(2,1)}, bf16[128,3712]{1,0:T(8,128)(2,1)S(1)}, u32[]{:S(2)}, u32[]{:S(2)}) collective-permute-start(bf16[128,3712]{1,0:T(8,128)(2,1)} %shard_map.68.block_ref), channel_id=1, source_target_pairs={{0,8},{1,9},{2,10},{3,11},{4,0},{5,1},{6,2},{7,3},{8,12},{9,13},{1... | collective-permute-start | bytes 2850824 | tf_op jit(solution)/shard_map/ppermute | solution.py:279
  7.1 1.2 copy-start
  9.6 12.7 %collective-permute-start.1 = (bf16[64,3584]{1,0:T(8,128)(2,1)S(1)}, bf16[64,3584]{1,0:T(8,128)(2,1)S(1)}, u32[]{:S(2)}, u32[]{:S(2)}) collective-permute-start(bf16[64,3584]{1,0:T(8,128)(2,1)S(1)} %get-tuple-element.34), channel_id=1, source_target_pairs={{0,2},{1,3},{2,0},{3,1},{4,6},{5,7},{6,4},{7,5},{8,10},{9,11},{10,... | collective-permute-start | bytes 1376264 | tf_op jit(solution)/shard_map/ppermute | solution.py:279
  29.7 25.9 %collective-permute-start.2 = (bf16[128,3712]{1,0:T(8,128)(2,1)S(1)}, bf16[128,3712]{1,0:T(8,128)(2,1)S(1)}, u32[]{:S(2)}, u32[]{:S(2)}) collective-permute-start(bf16[128,3712]{1,0:T(8,128)(2,1)S(1)} %collective-permute-done.block_ref), channel_id=1, source_target_pairs={{0,8},{1,9},{2,10},{3,11},{4,0},{5,1},{6,2},{7,3},{8,12},{9,13},{1... | collective-permute-start | bytes 2850824 | tf_op jit(solution)/shard_map/ppermute | solution.py:279
  33.0 11.9 %collective-permute-start.3 = (bf16[64,3584]{1,0:T(8,128)(2,1)S(1)}, bf16[64,3584]{1,0:T(8,128)(2,1)S(1)}, u32[]{:S(2)}, u32[]{:S(2)}) collective-permute-start(bf16[64,3584]{1,0:T(8,128)(2,1)S(1)} %get-tuple-element.41), channel_id=1, source_target_pairs={{0,2},{1,3},{2,0},{3,1},{4,6},{5,7},{6,4},{7,5},{8,10},{9,11},{10,... | collective-permute-start | bytes 1376264 | tf_op jit(solution)/shard_map/ppermute | solution.py:279
  54.0 13.5 %collective-permute-start.11 = (bf16[64,3584]{1,0:T(8,128)(2,1)S(1)}, bf16[64,3584]{1,0:T(8,128)(2,1)S(1)}, u32[]{:S(2)}, u32[]{:S(2)}) collective-permute-start(bf16[64,3584]{1,0:T(8,128)(2,1)S(1)} %get-tuple-element.57), channel_id=1, source_target_pairs={{0,2},{1,3},{2,0},{3,1},{4,6},{5,7},{6,4},{7,5},{8,10},{9,11},{10,... | collective-permute-start | bytes 1376264 | tf_op jit(solution)/shard_map/ppermute | solution.py:279
  56.9 28.6 %collective-permute-start.5 = (bf16[128,3712]{1,0:T(8,128)(2,1)S(1)}, bf16[128,3712]{1,0:T(8,128)(2,1)S(1)}, u32[]{:S(2)}, u32[]{:S(2)}) collective-permute-start(bf16[128,3712]{1,0:T(8,128)(2,1)S(1)} %collective-permute-done.2.block_ref), channel_id=1, source_target_pairs={{0,8},{1,9},{2,10},{3,11},{4,0},{5,1},{6,2},{7,3},{8,12},{9,13},{1... | collective-permute-start | bytes 2850824 | tf_op jit(solution)/shard_map/ppermute | solution.py:279
  58.0 16.8 %collective-permute-start.6 = (bf16[64,3584]{1,0:T(8,128)(2,1)S(1)}, bf16[64,3584]{1,0:T(8,128)(2,1)S(1)}, u32[]{:S(2)}, u32[]{:S(2)}) collective-permute-start(bf16[64,3584]{1,0:T(8,128)(2,1)S(1)} %get-tuple-element.45), channel_id=1, source_target_pairs={{0,2},{1,3},{2,0},{3,1},{4,6},{5,7},{6,4},{7,5},{8,10},{9,11},{10,... | collective-permute-start | bytes 1376264 | tf_op jit(solution)/shard_map/ppermute | solution.py:279
  68.1 29.7 %collective-permute-start.12 = (bf16[128,3584]{1,0:T(8,128)(2,1)S(1)}, bf16[128,3584]{1,0:T(8,128)(2,1)S(1)}, u32[]{:S(2)}, u32[]{:S(2)}) collective-permute-start(bf16[128,3584]{1,0:T(8,128)(2,1)S(1)} %shard_map.77), channel_id=1, source_target_pairs={{0,8},{1,9},{2,10},{3,11},{4,0},{5,1},{6,2},{7,3},{8,12},{9,13},{1... | collective-permute-start | bytes 2752520 | tf_op jit(solution)/shard_map/ppermute | solution.py:279
  83.9 13.5 %collective-permute-start.10 = (bf16[64,3584]{1,0:T(8,128)(2,1)S(1)}, bf16[64,3584]{1,0:T(8,128)(2,1)S(1)}, u32[]{:S(2)}, u32[]{:S(2)}) collective-permute-start(bf16[64,3584]{1,0:T(8,128)(2,1)S(1)} %get-tuple-element.56), channel_id=1, source_target_pairs={{0,2},{1,3},{2,0},{3,1},{4,6},{5,7},{6,4},{7,5},{8,10},{9,11},{10,... | collective-permute-start | bytes 1376264 | tf_op jit(solution)/shard_map/ppermute | solution.py:279
  86.8 16.9 %collective-permute-start.7 = (bf16[64,3584]{1,0:T(8,128)(2,1)S(1)}, bf16[64,3584]{1,0:T(8,128)(2,1)S(1)}, u32[]{:S(2)}, u32[]{:S(2)}) collective-permute-start(bf16[64,3584]{1,0:T(8,128)(2,1)S(1)} %get-tuple-element.49), channel_id=1, source_target_pairs={{0,2},{1,3},{2,0},{3,1},{4,6},{5,7},{6,4},{7,5},{8,10},{9,11},{10,... | collective-permute-start | bytes 1376264 | tf_op jit(solution)/shard_map/ppermute | solution.py:279
  98.5 23.5 %collective-permute-start.13 = (bf16[128,3584]{1,0:T(8,128)(2,1)S(1)}, bf16[128,3584]{1,0:T(8,128)(2,1)S(1)}, u32[]{:S(2)}, u32[]{:S(2)}) collective-permute-start(bf16[128,3584]{1,0:T(8,128)(2,1)S(1)} %shard_map.78), channel_id=1, source_target_pairs={{0,8},{1,9},{2,10},{3,11},{4,0},{5,1},{6,2},{7,3},{8,12},{9,13},{1... | collective-permute-start | bytes 2752520 | tf_op jit(solution)/shard_map/ppermute | solution.py:279
  112.9 9.1 %collective-permute-start.9 = (bf16[64,3584]{1,0:T(8,128)(2,1)S(1)}, bf16[64,3584]{1,0:T(8,128)(2,1)S(1)}, u32[]{:S(2)}, u32[]{:S(2)}) collective-permute-start(bf16[64,3584]{1,0:T(8,128)(2,1)S(1)} %get-tuple-element.55), channel_id=1, source_target_pairs={{0,2},{1,3},{2,0},{3,1},{4,6},{5,7},{6,4},{7,5},{8,10},{9,11},{10,... | collective-permute-start | bytes 1376264 | tf_op jit(solution)/shard_map/ppermute | solution.py:279
  122.7 19.2 %collective-permute-start.14 = (bf16[128,3584]{1,0:T(8,128)(2,1)S(1)}, bf16[128,3584]{1,0:T(8,128)(2,1)S(1)}, u32[]{:S(2)}, u32[]{:S(2)}) collective-permute-start(bf16[128,3584]{1,0:T(8,128)(2,1)S(1)} %shard_map.79), channel_id=1, source_target_pairs={{0,8},{1,9},{2,10},{3,11},{4,0},{5,1},{6,2},{7,3},{8,12},{9,13},{1... | collective-permute-start | bytes 2752520 | tf_op jit(solution)/shard_map/ppermute | solution.py:279
  132.6 9.3 %collective-permute-start.8 = (bf16[64,3584]{1,0:T(8,128)(2,1)S(1)}, bf16[64,3584]{1,0:T(8,128)(2,1)S(1)}, u32[]{:S(2)}, u32[]{:S(2)}) collective-permute-start(bf16[64,3584]{1,0:T(8,128)(2,1)S(1)} %get-tuple-element.53), channel_id=1, source_target_pairs={{0,2},{1,3},{2,0},{3,1},{4,6},{5,7},{6,4},{7,5},{8,10},{9,11},{10,... | collective-permute-start | bytes 1376264 | tf_op jit(solution)/shard_map/ppermute | solution.py:279
  134.2 1.2 collective-permute-start.15
  135.3 6.0 %collective-permute-start.16 = (f32[1,128]{1,0:T(1,128)S(1)}, f32[1,128]{1,0:T(1,128)S(1)}, u32[]{:S(2)}, u32[]{:S(2)}) collective-permute-start(f32[1,128]{1,0:T(1,128)S(1)} %slice.10), channel_id=1, source_target_pairs={{0,2},{1,3},{2,0},{3,1},{4,6},{5,7},{6,4},{7,5},{8,10},{9,11},{10,... | collective-permute-start | bytes 1544 | tf_op jit(solution)/shard_map/ppermute | solution.py:279

commit v3 on v2

v3 whole, which is shorter than its diff:
```python
import functools

import jax
import jax.numpy as jnp
from jax import lax
from jax.experimental import pallas as pl
from jax.experimental.pallas import tpu as pltpu
from jax.sharding import PartitionSpec as P

CORES = 2
LANES = 128
PARTS = 2
LARGE_VMEM = 60 * 1024 * 1024
VMEM_LIMIT = 48 * 1024 * 1024
SMALL_VMEM = 16 * 1024 * 1024
CHUNK = 896


def grid_of(chips):
    inner = 1
    while (2 * inner) * (2 * inner) <= chips and chips % (2 * inner) == 0:
        inner *= 2
    return chips // inner, inner


def ring_of(length):
    return [p for p in range(length) if p % 2 == 0] + [p for p in reversed(range(length)) if p % 2 == 1]


def tile_of(size, most):
    tile = most
    while size % tile:
        tile -= 128
    return tile


ANYWHERE = pl.BlockSpec(memory_space=pl.ANY)
WHOLE = pl.BlockSpec(memory_space=pltpu.VMEM)


def rows_cost(rows, width):
    return pl.CostEstimate(flops=2 * rows * width, bytes_accessed=4 * rows * width, transcendentals=0)


def eye_of(size):
    row = lax.broadcasted_iota(jnp.int32, (size, size), 0)
    column = lax.broadcasted_iota(jnp.int32, (size, size), 1)
    return row, column


def label_kernel(tokens_ref, experts_ref, copies_ref, gates_ref, *refs):
    out_refs, (experts_scr, copies_scr, gates_scr, sem) = refs[:PARTS], refs[PARTS:]
    width = tokens_ref.shape[1] // PARTS
    top_k, tokens = experts_ref.shape
    moves = [
        pltpu.make_async_copy(experts_ref, experts_scr, sem.at[0]),
        pltpu.make_async_copy(copies_ref, copies_scr, sem.at[1]),
        pltpu.make_async_copy(gates_ref, gates_scr, sem.at[2]),
    ]
    for i in range(PARTS):
        part = tokens_ref.at[:, pl.ds(i * width, width)]
        moves.append(pltpu.make_async_copy(part, out_refs[i].at[:, pl.ds(0, width)], sem.at[3 + i]))
    for move in moves:
        move.start()
    for move in moves[:3]:
        move.wait()
    lane = lax.broadcasted_iota(jnp.int32, (LANES, tokens), 0)
    labels = jnp.zeros((LANES, tokens), jnp.float32)
    for k in range(top_k):
        for i, ref in enumerate((experts_scr, copies_scr, gates_scr)):
            values = jnp.broadcast_to(ref[k : k + 1, :].astype(jnp.float32), (LANES, tokens))
            labels = jnp.where(lane == i * top_k + k, values, labels)
    row, column = eye_of(LANES)
    eye = jnp.where(row == column, 1.0, 0.0).astype(jnp.bfloat16)
    turned = lax.dot_general(
        labels.astype(jnp.bfloat16), eye, (((0,), (0,)), ((), ())), preferred_element_type=jnp.float32
    )
    out_refs[0][:, width:] = turned.astype(jnp.bfloat16)
    for move in moves[3:]:
        move.wait()


def label_rows(tokens, experts, copies, gates):
    rows, width = tokens.shape
    part = width // PARTS
    return list(
        pl.pallas_call(
            label_kernel,
            out_shape=[
                jax.ShapeDtypeStruct((rows, part + (0 if i else LANES)), jnp.bfloat16) for i in range(PARTS)
            ],
            in_specs=[ANYWHERE] * 4,
            out_specs=[WHOLE] * PARTS,
            scratch_shapes=[
                pltpu.VMEM(experts.shape, experts.dtype),
                pltpu.VMEM(copies.shape, copies.dtype),
                pltpu.VMEM(gates.shape, gates.dtype),
                pltpu.SemaphoreType.DMA((3 + PARTS,)),
            ],
            compiler_params=pltpu.CompilerParams(vmem_limit_bytes=LARGE_VMEM),
            cost_estimate=rows_cost(rows, width),
        )(tokens, experts, copies, gates)
    )


def dispatch_kernel(scalars, block_ref, *refs, inner, top_k):
    rows_refs, (pack_ref, combine_ref, counts_ref) = refs[:inner], refs[inner:]
    tokens = block_ref.shape[0]
    slots, width = rows_refs[0].shape
    base, col = scalars[0], scalars[1]
    row, column = eye_of(tokens)
    eye = jnp.where(row == column, 1.0, 0.0).astype(jnp.bfloat16)
    upto = jnp.where(row <= column, 1.0, 0.0).astype(jnp.bfloat16)
    labels = lax.dot_general(
        block_ref[:, width:], eye, (((0,), (0,)), ((), ())), preferred_element_type=jnp.float32
    )
    slot = lax.broadcasted_iota(jnp.int32, (slots, tokens), 0)
    lane = lax.broadcasted_iota(jnp.int32, (1, LANES), 1)
    counts_ref[...] = jnp.zeros_like(counts_ref)
    for j in range(inner):
        wanted = (base + lax.rem(col + j, inner)).astype(jnp.float32)
        hit = jnp.zeros((1, tokens), jnp.float32)
        weight = jnp.zeros((1, tokens), jnp.float32)
        upper = jnp.zeros((1, tokens), jnp.float32)
        for k in range(top_k):
            same = labels[k : k + 1] == wanted
            hit = hit + jnp.where(same, 1.0, 0.0)
            upper = upper + jnp.where(same, labels[top_k + k : top_k + k + 1], 0.0)
            weight = weight + jnp.where(same, labels[2 * top_k + k : 2 * top_k + k + 1], 0.0)
        wide = jnp.broadcast_to(hit, (8, tokens)).astype(jnp.bfloat16)
        rank = jnp.dot(wide, upto, preferred_element_type=jnp.float32)[:1].astype(jnp.int32) - 1
        chosen = (slot == rank) & (hit > 0.5)
        pack = jnp.where(chosen, 1.0, 0.0).astype(jnp.bfloat16)
        pack_ref[j] = pack
        combine_ref[j] = jnp.where(chosen, weight, 0.0).astype(jnp.bfloat16)
        rows_refs[j][...] = jnp.dot(pack, block_ref[:, :width], preferred_element_type=jnp.float32).astype(jnp.bfloat16)
        ones = jnp.sum(upper, axis=1, keepdims=True)
        zeros = jnp.sum(hit, axis=1, keepdims=True) - ones
        counts_ref[j : j + 1, :] = jnp.where(lane == 0, zeros, jnp.where(lane == 1, ones, 0.0))


def dispatch_rows(scalars, block, top_k, inner, slots):
    tokens, width = block.shape
    width -= LANES
    table = jax.ShapeDtypeStruct((inner, slots, tokens), jnp.bfloat16)
    outs = pl.pallas_call(
        functools.partial(dispatch_kernel, inner=inner, top_k=top_k),
        out_shape=[jax.ShapeDtypeStruct((slots, width), jnp.bfloat16)] * inner
        + [table, table, jax.ShapeDtypeStruct((-(-inner // 8) * 8, LANES), jnp.float32)],
        in_specs=[pl.BlockSpec(memory_space=pltpu.SMEM), WHOLE],
        out_specs=[WHOLE] * (inner + 3),
        compiler_params=pltpu.CompilerParams(vmem_limit_bytes=SMALL_VMEM),
        cost_estimate=rows_cost(tokens, width),
    )(scalars, block)
    return list(outs[:inner]), outs[inner], outs[inner + 1], outs[inner + 2]


def pack_kernel(pack_ref, block_ref, *rows_refs):
    for j, rows_ref in enumerate(rows_refs):
        rows_ref[...] = jnp.dot(pack_ref[j], block_ref[...], preferred_element_type=jnp.float32).astype(jnp.bfloat16)


def pack_rows(pack, block):
    inner, slots, tokens = pack.shape
    width = block.shape[1]
    return list(
        pl.pallas_call(
            pack_kernel,
            out_shape=[jax.ShapeDtypeStruct((slots, width), jnp.bfloat16)] * inner,
            in_specs=[WHOLE] * 2,
            out_specs=[WHOLE] * inner,
            compiler_params=pltpu.CompilerParams(vmem_limit_bytes=SMALL_VMEM),
            cost_estimate=rows_cost(tokens, width),
        )(pack, block)
    )


def combine_kernel(combine_ref, *refs, inner, parts, carried):
    out_ref = refs[-1]
    width = refs[0].shape[1]
    for i in range(parts):
        total = refs[parts * inner + i][...].astype(jnp.float32) if carried else None
        for j in range(inner):
            part = lax.dot_general(
                combine_ref[j], refs[i * inner + j][...], (((0,), (0,)), ((), ())), preferred_element_type=jnp.float32
            )
            total = part if total is None else total + part
        out_ref[:, i * width : (i + 1) * width] = total.astype(jnp.bfloat16)


def combine_rows(table, rows, carried):
    inner, _, tokens = table.shape
    parts = len(rows)
    width = parts * rows[0][0].shape[1]
    flat = sum(rows, [])
    return pl.pallas_call(
        functools.partial(combine_kernel, inner=inner, parts=parts, carried=len(carried)),
        out_shape=jax.ShapeDtypeStruct((tokens, width), jnp.bfloat16),
        in_specs=[WHOLE] * (1 + len(flat) + len(carried)),
        out_specs=WHOLE,
        compiler_params=pltpu.CompilerParams(vmem_limit_bytes=SMALL_VMEM),
        cost_estimate=rows_cost(tokens, width),
    )(table, *flat, *carried)


def expert_kernel(*refs, pieces, chunks):
    count = pieces * PARTS
    row_refs, weights, out_refs = refs[:count], refs[count : count + 2], refs[count + 2 : 2 * count + 2]
    rows_scr, hidden_scr, own_scr, other_scr, up_sem, down_sem = refs[2 * count + 2 :]
    held = (own_scr, other_scr)
    slots = row_refs[0].shape[0]
    chunk = rows_scr.shape[2]

    def up_copy(half, k):
        part = (pl.ds(0, 2), pl.ds(k * chunk, chunk))
        return pltpu.make_async_copy(weights[half].at[part], held[half].at[part], up_sem.at[half, k])

    def down_copy(half, k):
        part = (pl.ds(2, 1), pl.ds(k * chunk, chunk))
        return pltpu.make_async_copy(weights[half].at[part], held[half].at[part], down_sem.at[half, k])

    for half in range(2):
        for k in range(chunks):
            up_copy(half, k).start()
    for k in range(chunks):
        for half in range(2):
            down_copy(half, k).start()
    for i in range(pieces):
        for k in range(chunks):
            part, k_in = divmod(k, chunks // PARTS)
            source = row_refs[i * PARTS + part]
            rows_scr[k, i * slots : (i + 1) * slots, :] = source[:, k_in * chunk : (k_in + 1) * chunk]
    for half in range(2):
        gate_act = up_act = None
        for k in range(chunks):
            up_copy(half, k).wait()
            rows = rows_scr[k]
            gate_part = jnp.dot(rows, held[half][0, k * chunk : (k + 1) * chunk], preferred_element_type=jnp.float32)
            up_part = jnp.dot(rows, held[half][1, k * chunk : (k + 1) * chunk], preferred_element_type=jnp.float32)
            gate_act = gate_part if k == 0 else gate_act + gate_part
            up_act = up_part if k == 0 else up_act + up_part
        hidden_scr[half] = (jax.nn.silu(gate_act) * up_act).astype(jnp.bfloat16)
    for k in range(chunks):
        out = None
        for half in range(2):
            down_copy(half, k).wait()
            part = lax.dot_general(
                hidden_scr[half],
                held[half][2, k * chunk : (k + 1) * chunk],
                (((1,), (1,)), ((), ())),
                preferred_element_type=jnp.float32,
            )
            out = part if half == 0 else out + part
        out = out.astype(jnp.bfloat16)
        for i in range(pieces):
            part, k_in = divmod(k, chunks // PARTS)
            target = out_refs[i * PARTS + part]
            target[:, k_in * chunk : (k_in + 1) * chunk] = out[i * slots : (i + 1) * slots]


def expert_rows(pieces, own, other):
    count = len(pieces)
    slots, part = pieces[0][0].shape
    units = own.shape[2]
    chunk = tile_of(part, CHUNK)
    chunks = PARTS * part // chunk
    rows = count * slots
    outs = pl.pallas_call(
        functools.partial(expert_kernel, pieces=count, chunks=chunks),
        out_shape=[jax.ShapeDtypeStruct((slots, part), jnp.bfloat16)] * (count * PARTS),
        in_specs=[WHOLE] * (count * PARTS) + [ANYWHERE] * 2,
        out_specs=[WHOLE] * (count * PARTS),
        scratch_shapes=[
            pltpu.VMEM((chunks, rows, chunk), jnp.bfloat16),
            pltpu.VMEM((2, rows, units), jnp.bfloat16),
            pltpu.VMEM(own.shape, jnp.bfloat16),
            pltpu.VMEM(own.shape, jnp.bfloat16),
            pltpu.SemaphoreType.DMA((2, chunks)),
            pltpu.SemaphoreType.DMA((2, chunks)),
        ],
        compiler_params=pltpu.CompilerParams(vmem_limit_bytes=VMEM_LIMIT),
        cost_estimate=pl.CostEstimate(flops=1000, bytes_accessed=1000, transcendentals=0),
    )(*sum(pieces, []), own, other)
    return [list(outs[i * PARTS : (i + 1) * PARTS]) for i in range(count)]


def on_device(tokens, expert_weights, expert_ids, copy_ids, gate_weights):
    devices = lax.axis_size("expert")
    experts = devices // CORES
    outer, inner = grid_of(experts)
    tok_rows, top_k = expert_ids.shape
    slots = -(-2 * (tok_rows * top_k // experts) // 16) * 16
    me = lax.axis_index("expert").astype(jnp.int32)
    chip = lax.div(me, CORES)
    col = lax.rem(chip, inner)
    plane = lax.div(chip, inner)
    ring = ring_of(outer)

    def device_of(p, q, c):
        return (p * inner + q) * CORES + c

    every = [(p, q, c) for p in range(outer) for q in range(inner) for c in range(CORES)]

    def ring_pairs(shift):
        return [
            (device_of(p, q, c), device_of(ring[(ring.index(p) + shift) % outer], q, c)) for p, q, c in every
        ]

    def column_pairs(shift):
        return [(device_of(p, q, c), device_of(p, (q + shift) % inner, c)) for p, q, c in every]

    core_pairs = [(device_of(p, q, c), device_of(p, q, 1 - c)) for p, q, c in every]

    def permute(x, pairs):
        return lax.ppermute(x, "expert", pairs)

    scalars = jnp.stack([plane * inner, col])

    def behind(x, *others):
        return lax.optimization_barrier((x,) + others)[0] if others else x

    def swap(rows, sign):
        return rows[:1] + [permute(rows[shift], column_pairs(sign * shift)) for shift in range(1, inner)]

    def run(pieces):
        return expert_rows(pieces, expert_weights, other_weights)

    def transposed(lists):
        return [list(group) for group in zip(*lists)]

    last = outer - 1
    packs, tables, counts = [None] * outer, [None] * outer, [None] * outer
    packed = [[None] * PARTS for _ in range(outer)]
    sent = [[None] * PARTS for _ in range(outer)]
    results, back, sums = [None] * outer, [None] * outer, [None] * outer
    carry = [()] * PARTS

    def dispatch(step, i, block):
        if i == 0:
            packed[step][0], packs[step], tables[step], counts[step] = dispatch_rows(scalars, block, top_k, inner, slots)
        else:
            packed[step][i] = pack_rows(packs[step], block)
        sent[step][i] = swap(packed[step][i], 1)

    def give_back(step, *others):
        parts = transposed(results[step])
        parts[0] = parts[0][:1] + [behind(x, *others) for x in parts[0][1:]]
        back[step] = [swap(rows, -1) for rows in parts]

    def pass_on(step, gates):
        sums[step] = []
        for i in range(PARTS):
            table = behind(tables[step], *gates[i])
            sums[step].append(combine_rows(table, [back[step][i]], carry[i]))
            carry[i] = (permute(sums[step][i], ring_pairs(1)),)

    none = ((),) * PARTS
    block = label_rows(tokens, expert_ids.T, copy_ids.T, gate_weights.T)
    other_weights = permute(expert_weights, core_pairs)
    for i in range(PARTS):
        dispatch(0, i, block[i])
    block = [permute(part, ring_pairs(1)) for part in block]
    for step in range(1, outer):
        onward = []
        for i in range(PARTS):
            here, gates = block[i], ()
            if step == 1 and i == 0:
                gates = tuple(sent[0][j][-1] for j in range(PARTS))
            if step == 2 and i == 1:
                pieces = transposed(sent[1])
                pieces[0][0] = behind(pieces[0][0], tables[2])
                results[1] = run(pieces)
                here = behind(here, results[1][0][0])
                gates = (results[1][0][0],)
            dispatch(step, i, here)
            if step == 1 and i > 0:
                gates = (packed[1][i][0], sent[1][i - 1][-1])
            if step < last:
                onward.append(permute(behind(block[i], *gates), ring_pairs(1)))
        block = onward
    give_back(1, sent[2][0][-1])
    pass_on(1, ((packed[2][-1][0],),) + ((sent[2][-1][-1],),) * (PARTS - 1))
    routes = sum(counts)
    routes = routes + permute(routes, core_pairs)
    served = routes[:1]
    for shift in range(1, inner):
        served = served + permute(routes[shift : shift + 1], column_pairs(shift))
    for step in range(2, outer):
        pieces = transposed(sent[step])
        gates = (sums[step - 1][-1],)
        if step == 2 and last > 2:
            gates += (packed[3][-1][0],)
        pieces[0][0] = behind(pieces[0][0], *gates)
        if step == last:
            pieces = pieces + transposed(sent[0])
        results[step] = run(pieces)
        gates = none
        if step == last:
            results[0], results[step] = results[step][inner:], results[step][:inner]
            give_back(step)
            give_back(0, *(back[step][i][-1] for i in range(PARTS)))
        elif step == 2:
            give_back(step, carry[0][0], *(sent[3][i][-1] for i in range(PARTS)))
        else:
            give_back(step)
        pass_on(step, gates)
    moe_out = combine_rows(tables[0], back[0], sum(carry, ()))

    return moe_out, served[:, :2].astype(jnp.int32)


def solution(mesh):
    return jax.shard_map(
        on_device,
        mesh=mesh,
        in_specs=(
            P(("groups", "expert"), None),
            P(None, None, "expert"),
            P(("groups", "expert"), None),
            P(("groups", "expert"), None),
            P(("groups", "expert"), None),
        ),
        out_specs=(P(("groups", "expert"), None), P(("groups", "expert"), None)),
        check_vma=False,
    )
```

time: 144 us -> 134 us (0.931)
  waiting for transfers between devices: 68.4 us -> 50.8 us
  starting transfers between devices: 24.9 us -> 38.9 us
  Pallas kernels: 47.6 us -> 41.9 us
    ppermute x17 -> x31, waiting for transfers between devices: 68.4 us -> 50.8 us  [permute(): return lax.ppermute(x, 'expert', pairs)]
    ppermute x17 -> x31, starting transfers between devices: 24.9 us -> 38.9 us  [permute(): return lax.ppermute(x, 'expert', pairs)]
    pallas_call x9 -> x15, Pallas kernels: 42.1 us -> 37 us  [the longest x3 28.7 us: expert_rows(): pl.pallas_call(functools.partial(expert_kernel, pieces=count, chunks=chun...]
  transfers between devices with their start and end apart: 17 -> 31, of which waited for: 11 -> 15; matrix products, arithmetic and copies ran while one was open for 0% -> 0% of each run, Pallas kernels for 32% -> 30%
where the time goes in v3:
time: 134 us
  waiting for transfers between devices  50.8 us (38%)
  Pallas kernels  41.9 us (31%)
  starting transfers between devices  38.9 us (29%)
    ppermute x31, waiting for transfers between devices, permute(): return lax.ppermute(x, 'expert', pairs)  50.8 us
    ppermute x31, starting transfers between devices, permute(): return lax.ppermute(x, 'expert', pairs)  38.9 us
    pallas_call x3, Pallas kernels, expert_rows(): pl.pallas_call(functools.partial(expert_kernel, pieces=count, chunks=chun...  28.7 us
    pallas_call x4, Pallas kernels, dispatch_rows(): pl.pallas_call(functools.partial(dispatch_kernel, inner=inner, top_k=top_...  4.84 us
    pallas_call x7, Pallas kernels, combine_rows(): pl.pallas_call(functools.partial(combine_kernel, inner=inner, parts=parts...  4.1 us
  transfers between devices with their start and end apart: 31, of which 15 were waited for; matrix products, arithmetic and copies ran while one was open for 0% of the time, Pallas kernels for 30%

profile of v3, /device:TPU:0, one launch (start us, length us, event | category | flops | bytes accessed | tf_op | source)
XLA Modules:
  0.0 134.0 jit_solution(11440110726622858396)
XLA Ops:
  1.1 2.2 %shard_map.68 = (bf16[128,1920]{1,0:T(8,128)(2,1)}, bf16[128,1792]{1,0:T(8,128)(2,1)}) custom-call(bf16[128,3584]{1,0:T(8,128)(2,1)} %tokens_ref.1, s32[2,128]{1,0:T(2,128)} %bitcast.5, s32[2,128]{1,0:T(2,128)} %bitcast.6, bf16[2,128]{1,0:T(2,128)(2,1)} %bitcast.7), custom_call_target="tpu_custom_call" | custom-call | flops 917504 | bytes 1835008 | tf_op jit(solution)/shard_map/pallas_call | solution.py:87
  3.3 3.7 %collective-permute-start = (bf16[128,1920]{1,0:T(8,128)(2,1)}, bf16[128,1920]{1,0:T(8,128)(2,1)S(1)}, u32[]{:S(2)}, u32[]{:S(2)}) collective-permute-start(bf16[128,1920]{1,0:T(8,128)(2,1)} %get-tuple-element.59.block_ref), channel_id=1, source_target_pairs={{0,8},{1,9},{2,10},{3,11},{4,0},{5,1},{6,2},{7,3},{8,12},{9,13},{1... | collective-permute-start | bytes 1474568 | tf_op jit(solution)/shard_map/ppermute | solution.py:315
  10.6 1.6 %collective-permute-start.2 = (bf16[64,1792]{1,0:T(8,128)(2,1)S(1)}, bf16[64,1792]{1,0:T(8,128)(2,1)S(1)}, u32[]{:S(2)}, u32[]{:S(2)}) collective-permute-start(bf16[64,1792]{1,0:T(8,128)(2,1)S(1)} %get-tuple-element.64), channel_id=1, source_target_pairs={{0,2},{1,3},{2,0},{3,1},{4,6},{5,7},{6,4},{7,5},{8,10},{9,11},{10,... | collective-permute-start | bytes 688136 | tf_op jit(solution)/shard_map/ppermute | solution.py:315
  12.7 1.6 %collective-permute-start.5 = (bf16[128,1792]{1,0:T(8,128)(2,1)}, bf16[128,1792]{1,0:T(8,128)(2,1)S(1)}, u32[]{:S(2)}, u32[]{:S(2)}) collective-permute-start(bf16[128,1792]{1,0:T(8,128)(2,1)} %get-tuple-element.63.block_ref), channel_id=1, source_target_pairs={{0,8},{1,9},{2,10},{3,11},{4,0},{5,1},{6,2},{7,3},{8,12},{9,13},{1... | collective-permute-start | bytes 1376264 | tf_op jit(solution)/shard_map/ppermute | solution.py:315
  14.3 4.8 %collective-permute-done.2.refs_7_ = bf16[64,1792]{1,0:T(8,128)(2,1)S(1)} collective-permute-done((bf16[64,1792]{1,0:T(8,128)(2,1)S(1)}, bf16[64,1792]{1,0:T(8,128)(2,1)S(1)}, u32[]{:S(2)}, u32[]{:S(2)}) %collective-permute-start.2) | collective-permute-done | bytes 229408 | tf_op jit(solution)/shard_map/ppermute | solution.py:315
  19.1 4.2 %collective-permute-done.1.refs_6_ = bf16[64,1792]{1,0:T(8,128)(2,1)S(1)} collective-permute-done((bf16[64,1792]{1,0:T(8,128)(2,1)S(1)}, bf16[64,1792]{1,0:T(8,128)(2,1)S(1)}, u32[]{:S(2)}, u32[]{:S(2)}) %collective-permute-start.1) | collective-permute-done | bytes 229408 | tf_op jit(solution)/shard_map/ppermute | solution.py:315
  23.3 1.6 %collective-permute-start.3 = (bf16[128,1920]{1,0:T(8,128)(2,1)S(1)}, bf16[128,1920]{1,0:T(8,128)(2,1)S(1)}, u32[]{:S(2)}, u32[]{:S(2)}) collective-permute-start(bf16[128,1920]{1,0:T(8,128)(2,1)S(1)} %collective-permute-done.block_ref), channel_id=1, source_target_pairs={{0,8},{1,9},{2,10},{3,11},{4,0},{5,1},{6,2},{7,3},{8,12},{9,13},{1... | collective-permute-start | bytes 1474568 | tf_op jit(solution)/shard_map/ppermute | solution.py:315
  26.1 1.6 %collective-permute-start.6 = (bf16[64,1792]{1,0:T(8,128)(2,1)S(1)}, bf16[64,1792]{1,0:T(8,128)(2,1)S(1)}, u32[]{:S(2)}, u32[]{:S(2)}) collective-permute-start(bf16[64,1792]{1,0:T(8,128)(2,1)S(1)} %get-tuple-element.73), channel_id=1, source_target_pairs={{0,2},{1,3},{2,0},{3,1},{4,6},{5,7},{6,4},{7,5},{8,10},{9,11},{10,... | collective-permute-start | bytes 688136 | tf_op jit(solution)/shard_map/ppermute | solution.py:315
  28.9 3.8 %collective-permute-done.6.refs_2_ = bf16[64,1792]{1,0:T(8,128)(2,1)S(1)} collective-permute-done((bf16[64,1792]{1,0:T(8,128)(2,1)S(1)}, bf16[64,1792]{1,0:T(8,128)(2,1)S(1)}, u32[]{:S(2)}, u32[]{:S(2)}) %collective-permute-start.6) | collective-permute-done | bytes 229408 | tf_op jit(solution)/shard_map/ppermute | solution.py:315
  33.1 1.5 %collective-permute-start.8 = (bf16[64,1792]{1,0:T(8,128)(2,1)S(1)}, bf16[64,1792]{1,0:T(8,128)(2,1)S(1)}, u32[]{:S(2)}, u32[]{:S(2)}) collective-permute-start(bf16[64,1792]{1,0:T(8,128)(2,1)S(1)} %get-tuple-element.77), channel_id=1, source_target_pairs={{0,2},{1,3},{2,0},{3,1},{4,6},{5,7},{6,4},{7,5},{8,10},{9,11},{10,... | collective-permute-start | bytes 688136 | tf_op jit(solution)/shard_map/ppermute | solution.py:315
  34.7 4.4 %collective-permute-done.3.block_ref = bf16[128,1920]{1,0:T(8,128)(2,1)S(1)} collective-permute-done((bf16[128,1920]{1,0:T(8,128)(2,1)S(1)}, bf16[128,1920]{1,0:T(8,128)(2,1)S(1)}, u32[]{:S(2)}, u32[]{:S(2)}) %collective-permute-start.3) | collective-permute-done | bytes 491552 | tf_op jit(solution)/shard_map/ppermute | solution.py:315
  40.3 1.6 %collective-permute-start.13 = (bf16[64,1792]{1,0:T(8,128)(2,1)S(1)}, bf16[64,1792]{1,0:T(8,128)(2,1)S(1)}, u32[]{:S(2)}, u32[]{:S(2)}) collective-permute-start(bf16[64,1792]{1,0:T(8,128)(2,1)S(1)} %get-tuple-element.88), channel_id=1, source_target_pairs={{0,2},{1,3},{2,0},{3,1},{4,6},{5,7},{6,4},{7,5},{8,10},{9,11},{10,... | collective-permute-start | bytes 688136 | tf_op jit(solution)/shard_map/ppermute | solution.py:315
  41.9 3.4 %collective-permute-start.4 = (bf16[128,1920]{1,0:T(8,128)(2,1)S(1)}, bf16[128,1920]{1,0:T(8,128)(2,1)S(1)}, u32[]{:S(2)}, u32[]{:S(2)}) collective-permute-start(bf16[128,1920]{1,0:T(8,128)(2,1)S(1)} %collective-permute-done.3.block_ref), channel_id=1, source_target_pairs={{0,8},{1,9},{2,10},{3,11},{4,0},{5,1},{6,2},{7,3},{8,12},{9,13},{1... | collective-permute-start | bytes 1474568 | tf_op jit(solution)/shard_map/ppermute | solution.py:315
  45.3 9.1 %shard_map.75 = (bf16[64,1792]{1,0:T(8,128)(2,1)S(1)}, bf16[64,1792]{1,0:T(8,128)(2,1)S(1)}, bf16[64,1792]{1,0:T(8,128)(2,1)S(1)}, bf16[64,1792]{1,0:T(8,128)(2,1)S(1)}) custom-call(bf16[64,1792]{1,0:T(8,128)(2,1)S(1)} %get-tuple-element.76.refs_0_, bf16[64,1792]{1,0:T(8,128)(2,1)S(1)} %get-tuple-element.72.refs_1_, ...), custom_call_target="tpu_custom_call" | custom-call | flops 1000 | bytes 1000 | tf_op jit(solution)/shard_map/pallas_call | solution.py:268
  55.9 1.6 %collective-permute-start.10 = (bf16[64,1792]{1,0:T(8,128)(2,1)S(1)}, bf16[64,1792]{1,0:T(8,128)(2,1)S(1)}, u32[]{:S(2)}, u32[]{:S(2)}) collective-permute-start(bf16[64,1792]{1,0:T(8,128)(2,1)S(1)} %get-tuple-element.80), channel_id=1, source_target_pairs={{0,2},{1,3},{2,0},{3,1},{4,6},{5,7},{6,4},{7,5},{8,10},{9,11},{10,... | collective-permute-start | bytes 688136 | tf_op jit(solution)/shard_map/ppermute | solution.py:315
  58.0 5.0 %collective-permute-done.22.refs_1_ = bf16[64,1792]{1,0:T(8,128)(2,1)S(1)} collective-permute-done((bf16[64,1792]{1,0:T(8,128)(2,1)S(1)}, bf16[64,1792]{1,0:T(8,128)(2,1)S(1)}, u32[]{:S(2)}, u32[]{:S(2)}) %collective-permute-start.22) | collective-permute-done | bytes 229408 | tf_op jit(solution)/shard_map/ppermute | solution.py:315
  66.0 2.0 %collective-permute-done.10.refs_3_ = bf16[64,1792]{1,0:T(8,128)(2,1)S(1)} collective-permute-done((bf16[64,1792]{1,0:T(8,128)(2,1)S(1)}, bf16[64,1792]{1,0:T(8,128)(2,1)S(1)}, u32[]{:S(2)}, u32[]{:S(2)}) %collective-permute-start.10) | collective-permute-done | bytes 229408 | tf_op jit(solution)/shard_map/ppermute | solution.py:315
  67.9 4.9 %collective-permute-done.11.refs_1_ = bf16[64,1792]{1,0:T(8,128)(2,1)S(1)} collective-permute-done((bf16[64,1792]{1,0:T(8,128)(2,1)S(1)}, bf16[64,1792]{1,0:T(8,128)(2,1)S(1)}, u32[]{:S(2)}, u32[]{:S(2)}) %collective-permute-start.11) | collective-permute-done | bytes 229408 | tf_op jit(solution)/shard_map/ppermute | solution.py:315
  75.1 9.1 %shard_map.79 = (bf16[64,1792]{1,0:T(8,128)(2,1)S(1)}, bf16[64,1792]{1,0:T(8,128)(2,1)S(1)}, bf16[64,1792]{1,0:T(8,128)(2,1)S(1)}, bf16[64,1792]{1,0:T(8,128)(2,1)S(1)}) custom-call(bf16[64,1792]{1,0:T(8,128)(2,1)S(1)} %get-tuple-element.86.refs_0_, bf16[64,1792]{1,0:T(8,128)(2,1)S(1)} %get-tuple-element.87.refs_1_, ...), custom_call_target="tpu_custom_call" | custom-call | flops 1000 | bytes 1000 | tf_op jit(solution)/shard_map/pallas_call | solution.py:268
  84.2 1.6 %collective-permute-start.14 = (bf16[64,1792]{1,0:T(8,128)(2,1)S(1)}, bf16[64,1792]{1,0:T(8,128)(2,1)S(1)}, u32[]{:S(2)}, u32[]{:S(2)}) collective-permute-start(bf16[64,1792]{1,0:T(8,128)(2,1)S(1)} %get-tuple-element.90), channel_id=1, source_target_pairs={{0,2},{1,3},{2,0},{3,1},{4,6},{5,7},{6,4},{7,5},{8,10},{9,11},{10,... | collective-permute-start | bytes 688136 | tf_op jit(solution)/shard_map/ppermute | solution.py:315
  86.3 2.2 %collective-permute-done.15.refs_2_ = bf16[128,1792]{1,0:T(8,128)(2,1)S(1)} collective-permute-done((bf16[128,1792]{1,0:T(8,128)(2,1)S(1)}, bf16[128,1792]{1,0:T(8,128)(2,1)S(1)}, u32[]{:S(2)}, u32[]{:S(2)}) %collective-permute-start.15) | collective-permute-done | bytes 458784 | tf_op jit(solution)/shard_map/ppermute | solution.py:315
  88.5 1.7 %collective-permute-done.14.refs_1_ = bf16[64,1792]{1,0:T(8,128)(2,1)S(1)} collective-permute-done((bf16[64,1792]{1,0:T(8,128)(2,1)S(1)}, bf16[64,1792]{1,0:T(8,128)(2,1)S(1)}, u32[]{:S(2)}, u32[]{:S(2)}) %collective-permute-start.14) | collective-permute-done | bytes 229408 | tf_op jit(solution)/shard_map/ppermute | solution.py:315
  90.7 2.5 %collective-permute-start.27 = (bf16[128,1792]{1,0:T(8,128)(2,1)S(1)}, bf16[128,1792]{1,0:T(8,128)(2,1)S(1)}, u32[]{:S(2)}, u32[]{:S(2)}) collective-permute-start(bf16[128,1792]{1,0:T(8,128)(2,1)S(1)} %shard_map.80), channel_id=1, source_target_pairs={{0,8},{1,9},{2,10},{3,11},{4,0},{5,1},{6,2},{7,3},{8,12},{9,13},{1... | collective-permute-start | bytes 1376264 | tf_op jit(solution)/shard_map/ppermute | solution.py:315
  93.6 2.0 %collective-permute-start.25 = (bf16[128,1792]{1,0:T(8,128)(2,1)S(1)}, bf16[128,1792]{1,0:T(8,128)(2,1)S(1)}, u32[]{:S(2)}, u32[]{:S(2)}) collective-permute-start(bf16[128,1792]{1,0:T(8,128)(2,1)S(1)} %shard_map.83), channel_id=1, source_target_pairs={{0,8},{1,9},{2,10},{3,11},{4,0},{5,1},{6,2},{7,3},{8,12},{9,13},{1... | collective-permute-start | bytes 1376264 | tf_op jit(solution)/shard_map/ppermute | solution.py:315
  95.6 10.5 %shard_map.81 = (bf16[64,1792]{1,0:T(8,128)(2,1)S(1)}, bf16[64,1792]{1,0:T(8,128)(2,1)S(1)}, bf16[64,1792]{1,0:T(8,128)(2,1)S(1)}, bf16[64,1792]{1,0:T(8,128)(2,...) custom-call(bf16[64,1792]{1,0:T(8,128)(2,1)S(1)} %get-tuple-element., ...), custom_call_target="tpu_custom_call" | custom-call | flops 1000 | bytes 1000 | tf_op jit(solution)/shard_map/pallas_call | solution.py:268
  106.7 1.5 %collective-permute-start.18 = (bf16[64,1792]{1,0:T(8,128)(2,1)S(1)}, bf16[64,1792]{1,0:T(8,128)(2,1)S(1)}, u32[]{:S(2)}, u32[]{:S(2)}) collective-permute-start(bf16[64,1792]{1,0:T(8,128)(2,1)S(1)} %get-tuple-element.98), channel_id=1, source_target_pairs={{0,2},{1,3},{2,0},{3,1},{4,6},{5,7},{6,4},{7,5},{8,10},{9,11},{10,... | collective-permute-start | bytes 688136 | tf_op jit(solution)/shard_map/ppermute | solution.py:315
  108.2 5.0 %collective-permute-done.19.refs_1_ = bf16[64,1792]{1,0:T(8,128)(2,1)S(1)} collective-permute-done((bf16[64,1792]{1,0:T(8,128)(2,1)S(1)}, bf16[64,1792]{1,0:T(8,128)(2,1)S(1)}, u32[]{:S(2)}, u32[]{:S(2)}) %collective-permute-start.19) | collective-permute-done | bytes 229408 | tf_op jit(solution)/shard_map/ppermute | solution.py:315
  118.6 1.5 %collective-permute-start.30 = (f32[1,128]{1,0:T(1,128)S(1)}, f32[1,128]{1,0:T(1,128)S(1)}, u32[]{:S(2)}, u32[]{:S(2)}) collective-permute-start(f32[1,128]{1,0:T(1,128)S(1)} %slice.10), channel_id=1, source_target_pairs={{0,2},{1,3},{2,0},{3,1},{4,6},{5,7},{6,4},{7,5},{8,10},{9,11},{10,... | collective-permute-start | bytes 1544 | tf_op jit(solution)/shard_map/ppermute | solution.py:315
  120.6 1.5 %collective-permute-start.20 = (bf16[64,1792]{1,0:T(8,128)(2,1)S(1)}, bf16[64,1792]{1,0:T(8,128)(2,1)S(1)}, u32[]{:S(2)}, u32[]{:S(2)}) collective-permute-start(bf16[64,1792]{1,0:T(8,128)(2,1)S(1)} %get-tuple-element.100), channel_id=1, source_target_pairs={{0,2},{1,3},{2,0},{3,1},{4,6},{5,7},{6,4},{7,5},{8,10},{9,11},{10,... | collective-permute-start | bytes 688136 | tf_op jit(solution)/shard_map/ppermute | solution.py:315
  122.7 5.9 %collective-permute-done.21.refs_3_ = bf16[64,1792]{1,0:T(8,128)(2,1)S(1)} collective-permute-done((bf16[64,1792]{1,0:T(8,128)(2,1)S(1)}, bf16[64,1792]{1,0:T(8,128)(2,1)S(1)}, u32[]{:S(2)}, u32[]{:S(2)}) %collective-permute-start.21) | collective-permute-done | bytes 229408 | tf_op jit(solution)/shard_map/ppermute | solution.py:315
  128.6 3.8 %collective-permute-done.20.refs_1_ = bf16[64,1792]{1,0:T(8,128)(2,1)S(1)} collective-permute-done((bf16[64,1792]{1,0:T(8,128)(2,1)S(1)}, bf16[64,1792]{1,0:T(8,128)(2,1)S(1)}, u32[]{:S(2)}, u32[]{:S(2)}) %collective-permute-start.20) | collective-permute-done | bytes 229408 | tf_op jit(solution)/shard_map/ppermute | solution.py:315
  132.4 1.6 %shard_map.86 = bf16[128,3584]{1,0:T(8,128)(2,1)} custom-call(bf16[2,64,128]{2,1,0:T(8,128)(2,1)S(1)} %get-tuple-element.60.combine_ref, bf16[64,1792]{1,0:T(8,128)(2,1)S(1)} %get-tuple-element.96.refs_0_, bf16[64,1792]{1,0:T(8,128)(2,1)S(1)} %collective-permute-done.20.refs_1_, bf16[64,1792]{1,0:T(8,128)(2,1)S(1)} %get-tuple-element.101.refs_2_, ...), custom_call_target="tpu_custom_call" | custom-call | flops 917504 | bytes 1835008 | tf_op jit(solution)/shard_map/pallas_call | solution.py:196
  (57 shorter events, 24.2 us)
Async XLA Ops:
  0.6 44.7 %collective-permute-start.9 = (bf16[3,3584,512]{2,1,0:T(8,128)(2,1)}, bf16[3,3584,512]{2,1,0:T(8,128)(2,1)}, u32[]{:S(2)}, u32[]{:S(2)}) collective-permute-start(bf16[3,3584,512]{2,1,0:T(8,128)(2,1)} %refs_8_.1), channel_id=1, source_target_pairs={{0,1},{1,0},{2,3},{3,2},{4,5},{5,4},{6,7},{7,6},{8,9},{9,8},{10,11... | collective-permute-start | bytes 33030152 | tf_op jit(solution)/shard_map/ppermute | solution.py:315
  3.3 20.0 %collective-permute-start = (bf16[128,1920]{1,0:T(8,128)(2,1)}, bf16[128,1920]{1,0:T(8,128)(2,1)S(1)}, u32[]{:S(2)}, u32[]{:S(2)}) collective-permute-start(bf16[128,1920]{1,0:T(8,128)(2,1)} %get-tuple-element.59.block_ref), channel_id=1, source_target_pairs={{0,8},{1,9},{2,10},{3,11},{4,0},{5,1},{6,2},{7,3},{8,12},{9,13},{1... | collective-permute-start | bytes 1474568 | tf_op jit(solution)/shard_map/ppermute | solution.py:315
  7.1 1.0 copy-start
  10.6 8.5 %collective-permute-start.2 = (bf16[64,1792]{1,0:T(8,128)(2,1)S(1)}, bf16[64,1792]{1,0:T(8,128)(2,1)S(1)}, u32[]{:S(2)}, u32[]{:S(2)}) collective-permute-start(bf16[64,1792]{1,0:T(8,128)(2,1)S(1)} %get-tuple-element.64), channel_id=1, source_target_pairs={{0,2},{1,3},{2,0},{3,1},{4,6},{5,7},{6,4},{7,5},{8,10},{9,11},{10,... | collective-permute-start | bytes 688136 | tf_op jit(solution)/shard_map/ppermute | solution.py:315
  12.2 11.1 %collective-permute-start.1 = (bf16[64,1792]{1,0:T(8,128)(2,1)S(1)}, bf16[64,1792]{1,0:T(8,128)(2,1)S(1)}, u32[]{:S(2)}, u32[]{:S(2)}) collective-permute-start(bf16[64,1792]{1,0:T(8,128)(2,1)S(1)} %get-tuple-element.61), channel_id=1, source_target_pairs={{0,2},{1,3},{2,0},{3,1},{4,6},{5,7},{6,4},{7,5},{8,10},{9,11},{10,... | collective-permute-start | bytes 688136 | tf_op jit(solution)/shard_map/ppermute | solution.py:315
  12.7 16.0 %collective-permute-start.5 = (bf16[128,1792]{1,0:T(8,128)(2,1)}, bf16[128,1792]{1,0:T(8,128)(2,1)S(1)}, u32[]{:S(2)}, u32[]{:S(2)}) collective-permute-start(bf16[128,1792]{1,0:T(8,128)(2,1)} %get-tuple-element.63.block_ref), channel_id=1, source_target_pairs={{0,8},{1,9},{2,10},{3,11},{4,0},{5,1},{6,2},{7,3},{8,12},{9,13},{1... | collective-permute-start | bytes 1376264 | tf_op jit(solution)/shard_map/ppermute | solution.py:315
  23.3 15.8 %collective-permute-start.3 = (bf16[128,1920]{1,0:T(8,128)(2,1)S(1)}, bf16[128,1920]{1,0:T(8,128)(2,1)S(1)}, u32[]{:S(2)}, u32[]{:S(2)}) collective-permute-start(bf16[128,1920]{1,0:T(8,128)(2,1)S(1)} %collective-permute-done.block_ref), channel_id=1, source_target_pairs={{0,8},{1,9},{2,10},{3,11},{4,0},{5,1},{6,2},{7,3},{8,12},{9,13},{1... | collective-permute-start | bytes 1474568 | tf_op jit(solution)/shard_map/ppermute | solution.py:315
  26.1 6.7 %collective-permute-start.6 = (bf16[64,1792]{1,0:T(8,128)(2,1)S(1)}, bf16[64,1792]{1,0:T(8,128)(2,1)S(1)}, u32[]{:S(2)}, u32[]{:S(2)}) collective-permute-start(bf16[64,1792]{1,0:T(8,128)(2,1)S(1)} %get-tuple-element.73), channel_id=1, source_target_pairs={{0,2},{1,3},{2,0},{3,1},{4,6},{5,7},{6,4},{7,5},{8,10},{9,11},{10,... | collective-permute-start | bytes 688136 | tf_op jit(solution)/shard_map/ppermute | solution.py:315
  32.8 21.6 %collective-permute-start.7 = (bf16[128,1792]{1,0:T(8,128)(2,1)S(1)}, bf16[128,1792]{1,0:T(8,128)(2,1)S(1)}, u32[]{:S(2)}, u32[]{:S(2)}) collective-permute-start(bf16[128,1792]{1,0:T(8,128)(2,1)S(1)} %collective-permute-done.5.block_ref), channel_id=1, source_target_pairs={{0,8},{1,9},{2,10},{3,11},{4,0},{5,1},{6,2},{7,3},{8,12},{9,13},{1... | collective-permute-start | bytes 1376264 | tf_op jit(solution)/shard_map/ppermute | solution.py:315
  33.1 12.2 %collective-permute-start.8 = (bf16[64,1792]{1,0:T(8,128)(2,1)S(1)}, bf16[64,1792]{1,0:T(8,128)(2,1)S(1)}, u32[]{:S(2)}, u32[]{:S(2)}) collective-permute-start(bf16[64,1792]{1,0:T(8,128)(2,1)S(1)} %get-tuple-element.77), channel_id=1, source_target_pairs={{0,2},{1,3},{2,0},{3,1},{4,6},{5,7},{6,4},{7,5},{8,10},{9,11},{10,... | collective-permute-start | bytes 688136 | tf_op jit(solution)/shard_map/ppermute | solution.py:315
  40.3 14.1 %collective-permute-start.13 = (bf16[64,1792]{1,0:T(8,128)(2,1)S(1)}, bf16[64,1792]{1,0:T(8,128)(2,1)S(1)}, u32[]{:S(2)}, u32[]{:S(2)}) collective-permute-start(bf16[64,1792]{1,0:T(8,128)(2,1)S(1)} %get-tuple-element.88), channel_id=1, source_target_pairs={{0,2},{1,3},{2,0},{3,1},{4,6},{5,7},{6,4},{7,5},{8,10},{9,11},{10,... | collective-permute-start | bytes 688136 | tf_op jit(solution)/shard_map/ppermute | solution.py:315
  41.9 22.3 %collective-permute-start.4 = (bf16[128,1920]{1,0:T(8,128)(2,1)S(1)}, bf16[128,1920]{1,0:T(8,128)(2,1)S(1)}, u32[]{:S(2)}, u32[]{:S(2)}) collective-permute-start(bf16[128,1920]{1,0:T(8,128)(2,1)S(1)} %collective-permute-done.3.block_ref), channel_id=1, source_target_pairs={{0,8},{1,9},{2,10},{3,11},{4,0},{5,1},{6,2},{7,3},{8,12},{9,13},{1... | collective-permute-start | bytes 1474568 | tf_op jit(solution)/shard_map/ppermute | solution.py:315
  54.4 8.6 %collective-permute-start.22 = (bf16[64,1792]{1,0:T(8,128)(2,1)S(1)}, bf16[64,1792]{1,0:T(8,128)(2,1)S(1)}, u32[]{:S(2)}, u32[]{:S(2)}) collective-permute-start(bf16[64,1792]{1,0:T(8,128)(2,1)S(1)} %get-tuple-element.109), channel_id=1, source_target_pairs={{0,2},{1,3},{2,0},{3,1},{4,6},{5,7},{6,4},{7,5},{8,10},{9,11},{10,... | collective-permute-start | bytes 688136 | tf_op jit(solution)/shard_map/ppermute | solution.py:315
  55.0 19.2 %collective-permute-start.12 = (bf16[128,1792]{1,0:T(8,128)(2,1)S(1)}, bf16[128,1792]{1,0:T(8,128)(2,1)S(1)}, u32[]{:S(2)}, u32[]{:S(2)}) collective-permute-start(bf16[128,1792]{1,0:T(8,128)(2,1)S(1)} %collective-permute-done.7.block_ref), channel_id=1, source_target_pairs={{0,8},{1,9},{2,10},{3,11},{4,0},{5,1},{6,2},{7,3},{8,12},{9,13},{1... | collective-permute-start | bytes 1376264 | tf_op jit(solution)/shard_map/ppermute | solution.py:315
  55.9 12.0 %collective-permute-start.10 = (bf16[64,1792]{1,0:T(8,128)(2,1)S(1)}, bf16[64,1792]{1,0:T(8,128)(2,1)S(1)}, u32[]{:S(2)}, u32[]{:S(2)}) collective-permute-start(bf16[64,1792]{1,0:T(8,128)(2,1)S(1)} %get-tuple-element.80), channel_id=1, source_target_pairs={{0,2},{1,3},{2,0},{3,1},{4,6},{5,7},{6,4},{7,5},{8,10},{9,11},{10,... | collective-permute-start | bytes 688136 | tf_op jit(solution)/shard_map/ppermute | solution.py:315
  57.5 15.3 %collective-permute-start.11 = (bf16[64,1792]{1,0:T(8,128)(2,1)S(1)}, bf16[64,1792]{1,0:T(8,128)(2,1)S(1)}, u32[]{:S(2)}, u32[]{:S(2)}) collective-permute-start(bf16[64,1792]{1,0:T(8,128)(2,1)S(1)} %get-tuple-element.83), channel_id=1, source_target_pairs={{0,2},{1,3},{2,0},{3,1},{4,6},{5,7},{6,4},{7,5},{8,10},{9,11},{10,... | collective-permute-start | bytes 688136 | tf_op jit(solution)/shard_map/ppermute | solution.py:315
  63.5 22.3 %collective-permute-start.23 = (bf16[128,1792]{1,0:T(8,128)(2,1)S(1)}, bf16[128,1792]{1,0:T(8,128)(2,1)S(1)}, u32[]{:S(2)}, u32[]{:S(2)}) collective-permute-start(bf16[128,1792]{1,0:T(8,128)(2,1)S(1)} %shard_map.82), channel_id=1, source_target_pairs={{0,8},{1,9},{2,10},{3,11},{4,0},{5,1},{6,2},{7,3},{8,12},{9,13},{1... | collective-permute-start | bytes 1376264 | tf_op jit(solution)/shard_map/ppermute | solution.py:315
  65.4 20.4 %collective-permute-start.16 = (bf16[64,1792]{1,0:T(8,128)(2,1)S(1)}, bf16[64,1792]{1,0:T(8,128)(2,1)S(1)}, u32[]{:S(2)}, u32[]{:S(2)}) collective-permute-start(bf16[64,1792]{1,0:T(8,128)(2,1)S(1)} %get-tuple-element.92), channel_id=1, source_target_pairs={{0,2},{1,3},{2,0},{3,1},{4,6},{5,7},{6,4},{7,5},{8,10},{9,11},{10,... | collective-permute-start | bytes 688136 | tf_op jit(solution)/shard_map/ppermute | solution.py:315
  73.3 15.3 %collective-permute-start.15 = (bf16[128,1792]{1,0:T(8,128)(2,1)S(1)}, bf16[128,1792]{1,0:T(8,128)(2,1)S(1)}, u32[]{:S(2)}, u32[]{:S(2)}) collective-permute-start(bf16[128,1792]{1,0:T(8,128)(2,1)S(1)} %shard_map.77), channel_id=1, source_target_pairs={{0,8},{1,9},{2,10},{3,11},{4,0},{5,1},{6,2},{7,3},{8,12},{9,13},{1... | collective-permute-start | bytes 1376264 | tf_op jit(solution)/shard_map/ppermute | solution.py:315
  74.5 11.3 %collective-permute-start.17 = (bf16[64,1792]{1,0:T(8,128)(2,1)S(1)}, bf16[64,1792]{1,0:T(8,128)(2,1)S(1)}, u32[]{:S(2)}, u32[]{:S(2)}) collective-permute-start(bf16[64,1792]{1,0:T(8,128)(2,1)S(1)} %get-tuple-element.93), channel_id=1, source_target_pairs={{0,2},{1,3},{2,0},{3,1},{4,6},{5,7},{6,4},{7,5},{8,10},{9,11},{10,... | collective-permute-start | bytes 688136 | tf_op jit(solution)/shard_map/ppermute | solution.py:315
  84.2 6.1 %collective-permute-start.14 = (bf16[64,1792]{1,0:T(8,128)(2,1)S(1)}, bf16[64,1792]{1,0:T(8,128)(2,1)S(1)}, u32[]{:S(2)}, u32[]{:S(2)}) collective-permute-start(bf16[64,1792]{1,0:T(8,128)(2,1)S(1)} %get-tuple-element.90), channel_id=1, source_target_pairs={{0,2},{1,3},{2,0},{3,1},{4,6},{5,7},{6,4},{7,5},{8,10},{9,11},{10,... | collective-permute-start | bytes 688136 | tf_op jit(solution)/shard_map/ppermute | solution.py:315
  85.8 7.4 %collective-permute-start.24 = (bf16[64,1792]{1,0:T(8,128)(2,1)S(1)}, bf16[64,1792]{1,0:T(8,128)(2,1)S(1)}, u32[]{:S(2)}, u32[]{:S(2)}) collective-permute-start(bf16[64,1792]{1,0:T(8,128)(2,1)S(1)} %get-tuple-element.110), channel_id=1, source_target_pairs={{0,2},{1,3},{2,0},{3,1},{4,6},{5,7},{6,4},{7,5},{8,10},{9,11},{10,... | collective-permute-start | bytes 688136 | tf_op jit(solution)/shard_map/ppermute | solution.py:315
  90.7 22.5 %collective-permute-start.27 = (bf16[128,1792]{1,0:T(8,128)(2,1)S(1)}, bf16[128,1792]{1,0:T(8,128)(2,1)S(1)}, u32[]{:S(2)}, u32[]{:S(2)}) collective-permute-start(bf16[128,1792]{1,0:T(8,128)(2,1)S(1)} %shard_map.80), channel_id=1, source_target_pairs={{0,8},{1,9},{2,10},{3,11},{4,0},{5,1},{6,2},{7,3},{8,12},{9,13},{1... | collective-permute-start | bytes 1376264 | tf_op jit(solution)/shard_map/ppermute | solution.py:315
  93.6 22.1 %collective-permute-start.25 = (bf16[128,1792]{1,0:T(8,128)(2,1)S(1)}, bf16[128,1792]{1,0:T(8,128)(2,1)S(1)}, u32[]{:S(2)}, u32[]{:S(2)}) collective-permute-start(bf16[128,1792]{1,0:T(8,128)(2,1)S(1)} %shard_map.83), channel_id=1, source_target_pairs={{0,8},{1,9},{2,10},{3,11},{4,0},{5,1},{6,2},{7,3},{8,12},{9,13},{1... | collective-permute-start | bytes 1376264 | tf_op jit(solution)/shard_map/ppermute | solution.py:315
  106.1 7.1 %collective-permute-start.19 = (bf16[64,1792]{1,0:T(8,128)(2,1)S(1)}, bf16[64,1792]{1,0:T(8,128)(2,1)S(1)}, u32[]{:S(2)}, u32[]{:S(2)}) collective-permute-start(bf16[64,1792]{1,0:T(8,128)(2,1)S(1)} %get-tuple-element.99), channel_id=1, source_target_pairs={{0,2},{1,3},{2,0},{3,1},{4,6},{5,7},{6,4},{7,5},{8,10},{9,11},{10,... | collective-permute-start | bytes 688136 | tf_op jit(solution)/shard_map/ppermute | solution.py:315
  106.7 9.0 %collective-permute-start.18 = (bf16[64,1792]{1,0:T(8,128)(2,1)S(1)}, bf16[64,1792]{1,0:T(8,128)(2,1)S(1)}, u32[]{:S(2)}, u32[]{:S(2)}) collective-permute-start(bf16[64,1792]{1,0:T(8,128)(2,1)S(1)} %get-tuple-element.98), channel_id=1, source_target_pairs={{0,2},{1,3},{2,0},{3,1},{4,6},{5,7},{6,4},{7,5},{8,10},{9,11},{10,... | collective-permute-start | bytes 688136 | tf_op jit(solution)/shard_map/ppermute | solution.py:315
  113.6 18.8 %collective-permute-start.28 = (bf16[128,1792]{1,0:T(8,128)(2,1)S(1)}, bf16[128,1792]{1,0:T(8,128)(2,1)S(1)}, u32[]{:S(2)}, u32[]{:S(2)}) collective-permute-start(bf16[128,1792]{1,0:T(8,128)(2,1)S(1)} %shard_map.85), channel_id=1, source_target_pairs={{0,8},{1,9},{2,10},{3,11},{4,0},{5,1},{6,2},{7,3},{8,12},{9,13},{1... | collective-permute-start | bytes 1376264 | tf_op jit(solution)/shard_map/ppermute | solution.py:315
  116.1 16.3 %collective-permute-start.26 = (bf16[128,1792]{1,0:T(8,128)(2,1)S(1)}, bf16[128,1792]{1,0:T(8,128)(2,1)S(1)}, u32[]{:S(2)}, u32[]{:S(2)}) collective-permute-start(bf16[128,1792]{1,0:T(8,128)(2,1)S(1)} %shard_map.84), channel_id=1, source_target_pairs={{0,8},{1,9},{2,10},{3,11},{4,0},{5,1},{6,2},{7,3},{8,12},{9,13},{1... | collective-permute-start | bytes 1376264 | tf_op jit(solution)/shard_map/ppermute | solution.py:315
  117.4 1.2 collective-permute-start.29
  118.6 3.5 %collective-permute-start.30 = (f32[1,128]{1,0:T(1,128)S(1)}, f32[1,128]{1,0:T(1,128)S(1)}, u32[]{:S(2)}, u32[]{:S(2)}) collective-permute-start(f32[1,128]{1,0:T(1,128)S(1)} %slice.10), channel_id=1, source_target_pairs={{0,2},{1,3},{2,0},{3,1},{4,6},{5,7},{6,4},{7,5},{8,10},{9,11},{10,... | collective-permute-start | bytes 1544 | tf_op jit(solution)/shard_map/ppermute | solution.py:315
  120.1 8.5 %collective-permute-start.21 = (bf16[64,1792]{1,0:T(8,128)(2,1)S(1)}, bf16[64,1792]{1,0:T(8,128)(2,1)S(1)}, u32[]{:S(2)}, u32[]{:S(2)}) collective-permute-start(bf16[64,1792]{1,0:T(8,128)(2,1)S(1)} %get-tuple-element.102), channel_id=1, source_target_pairs={{0,2},{1,3},{2,0},{3,1},{4,6},{5,7},{6,4},{7,5},{8,10},{9,11},{10,... | collective-permute-start | bytes 688136 | tf_op jit(solution)/shard_map/ppermute | solution.py:315
  120.6 11.8 %collective-permute-start.20 = (bf16[64,1792]{1,0:T(8,128)(2,1)S(1)}, bf16[64,1792]{1,0:T(8,128)(2,1)S(1)}, u32[]{:S(2)}, u32[]{:S(2)}) collective-permute-start(bf16[64,1792]{1,0:T(8,128)(2,1)S(1)} %get-tuple-element.100), channel_id=1, source_target_pairs={{0,2},{1,3},{2,0},{3,1},{4,6},{5,7},{6,4},{7,5},{8,10},{9,11},{10,... | collective-permute-start | bytes 688136 | tf_op jit(solution)/shard_map/ppermute | solution.py:315

commit v4 on v3

--- a/solution.py
+++ b/solution.py
@@ -279,7 +279,9 @@
             pltpu.SemaphoreType.DMA((2, chunks)),
         ],
         compiler_params=pltpu.CompilerParams(vmem_limit_bytes=VMEM_LIMIT),
-        cost_estimate=pl.CostEstimate(flops=1000, bytes_accessed=1000, transcendentals=0),
+        cost_estimate=pl.CostEstimate(
+            flops=12 * rows * PARTS * part * units, bytes_accessed=4 * own.size, transcendentals=0
+        ),
     )(*sum(pieces, []), own, other)
     return [list(outs[i * PARTS : (i + 1) * PARTS]) for i in range(count)]
 
@@ -342,14 +344,15 @@
             packed[step][i] = pack_rows(packs[step], block)
         sent[step][i] = swap(packed[step][i], 1)
 
-    def give_back(step, *others):
+    def give_back(step, *others, late=()):
         parts = transposed(results[step])
         parts[0] = parts[0][:1] + [behind(x, *others) for x in parts[0][1:]]
+        parts[1:] = [part[:1] + [behind(x, *late) for x in part[1:]] for part in parts[1:]]
         back[step] = [swap(rows, -1) for rows in parts]
 
-    def pass_on(step, gates):
-        sums[step] = []
-        for i in range(PARTS):
+    def pass_on(step, gates, these=range(PARTS)):
+        sums[step] = sums[step] or []
+        for i in these:
             table = behind(tables[step], *gates[i])
             sums[step].append(combine_rows(table, [back[step][i]], carry[i]))
             carry[i] = (permute(sums[step][i], ring_pairs(1)),)
@@ -372,14 +375,17 @@
                 results[1] = run(pieces)
                 here = behind(here, results[1][0][0])
                 gates = (results[1][0][0],)
+            if step == 3 and i == 0:
+                here = behind(here, sums[1][0])
             dispatch(step, i, here)
             if step == 1 and i > 0:
                 gates = (packed[1][i][0], sent[1][i - 1][-1])
             if step < last:
                 onward.append(permute(behind(block[i], *gates), ring_pairs(1)))
         block = onward
-    give_back(1, sent[2][0][-1])
-    pass_on(1, ((packed[2][-1][0],),) + ((sent[2][-1][-1],),) * (PARTS - 1))
+        if step == 2:
+            give_back(1, sent[2][0][-1])
+            pass_on(1, ((packed[2][-1][0],),) + none[1:], range(1))
     routes = sum(counts)
     routes = routes + permute(routes, core_pairs)
     served = routes[:1]
@@ -387,23 +393,24 @@
         served = served + permute(routes[shift : shift + 1], column_pairs(shift))
     for step in range(2, outer):
         pieces = transposed(sent[step])
-        gates = (sums[step - 1][-1],)
-        if step == 2 and last > 2:
-            gates += (packed[3][-1][0],)
+        if step == 2:
+            gates = (sums[1][0], packed[3][0][0])
+        else:
+            gates = (sums[2][0],)
         pieces[0][0] = behind(pieces[0][0], *gates)
         if step == last:
             pieces = pieces + transposed(sent[0])
         results[step] = run(pieces)
-        gates = none
+        if step == 2:
+            pass_on(1, none[:1] + ((results[2][0][0],),) * (PARTS - 1), range(1, PARTS))
         if step == last:
             results[0], results[step] = results[step][inner:], results[step][:inner]
-            give_back(step)
-            give_back(0, *(back[step][i][-1] for i in range(PARTS)))
-        elif step == 2:
-            give_back(step, carry[0][0], *(sent[3][i][-1] for i in range(PARTS)))
+        if step == 2:
+            give_back(step, carry[0][0], sums[1][1], packed[3][-1][0], sent[3][0][-1], late=(sent[3][-1][-1],))
         else:
             give_back(step)
-        pass_on(step, gates)
+        pass_on(step, none)
+    give_back(0, *(back[last][i][-1] for i in range(PARTS)))
     moe_out = combine_rows(tables[0], back[0], sum(carry, ()))
 
     return moe_out, served[:, :2].astype(jnp.int32)

time: 134 us -> 134 us (level)
  starting transfers between devices: 38.9 us -> 33.3 us
  waiting for transfers between devices: 50.8 us -> 56 us
    ppermute x31, starting transfers between devices: 38.9 us -> 33.3 us  [permute(): return lax.ppermute(x, 'expert', pairs)]
    ppermute x31, waiting for transfers between devices: 50.8 us -> 56 us  [permute(): return lax.ppermute(x, 'expert', pairs)]
  transfers between devices with their start and end apart: 31 -> 31, of which waited for: 15 -> 17; matrix products, arithmetic and copies ran while one was open for 0% -> 0% of each run, Pallas kernels for 30% -> 30%
where the time goes in v4:
time: 134 us
  waiting for transfers between devices  56 us (42%)
  Pallas kernels  41.9 us (31%)
  starting transfers between devices  33.3 us (25%)
    ppermute x31, waiting for transfers between devices, permute(): return lax.ppermute(x, 'expert', pairs)  56 us
    ppermute x31, starting transfers between devices, permute(): return lax.ppermute(x, 'expert', pairs)  33.3 us
    pallas_call x3, Pallas kernels, expert_rows(): pl.pallas_call(functools.partial(expert_kernel, pieces=count, chunks=chun...  28.7 us
    pallas_call x4, Pallas kernels, dispatch_rows(): pl.pallas_call(functools.partial(dispatch_kernel, inner=inner, top_k=top_...  4.84 us
    pallas_call x7, Pallas kernels, combine_rows(): pl.pallas_call(functools.partial(combine_kernel, inner=inner, parts=parts...  4.1 us
  transfers between devices with their start and end apart: 31, of which 17 were waited for; matrix products, arithmetic and copies ran while one was open for 0% of the time, Pallas kernels for 30%

profile of v4, /device:TPU:0, one launch (start us, length us, event | category | flops | bytes accessed | tf_op | source)
XLA Modules:
  0.0 133.6 jit_solution(6316020225100828281)
XLA Ops:
  1.1 2.2 %shard_map.68 = (bf16[128,1920]{1,0:T(8,128)(2,1)}, bf16[128,1792]{1,0:T(8,128)(2,1)}) custom-call(bf16[128,3584]{1,0:T(8,128)(2,1)} %tokens_ref.1, s32[2,128]{1,0:T(2,128)} %bitcast.5, s32[2,128]{1,0:T(2,128)} %bitcast.6, bf16[2,128]{1,0:T(2,128)(2,1)} %bitcast.7), custom_call_target="tpu_custom_call" | custom-call | flops 917504 | bytes 1835008 | tf_op jit(solution)/shard_map/pallas_call | solution.py:87
  3.3 3.7 %collective-permute-start = (bf16[128,1920]{1,0:T(8,128)(2,1)}, bf16[128,1920]{1,0:T(8,128)(2,1)S(1)}, u32[]{:S(2)}, u32[]{:S(2)}) collective-permute-start(bf16[128,1920]{1,0:T(8,128)(2,1)} %get-tuple-element.61.block_ref), channel_id=1, source_target_pairs={{0,8},{1,9},{2,10},{3,11},{4,0},{5,1},{6,2},{7,3},{8,12},{9,13},{1... | collective-permute-start | bytes 1474568 | tf_op jit(solution)/shard_map/ppermute | solution.py:317
  8.1 1.2 shard_map.69
  9.3 1.3 shard_map.70
  10.6 1.6 %collective-permute-start.2 = (bf16[64,1792]{1,0:T(8,128)(2,1)S(1)}, bf16[64,1792]{1,0:T(8,128)(2,1)S(1)}, u32[]{:S(2)}, u32[]{:S(2)}) collective-permute-start(bf16[64,1792]{1,0:T(8,128)(2,1)S(1)} %get-tuple-element.66), channel_id=1, source_target_pairs={{0,2},{1,3},{2,0},{3,1},{4,6},{5,7},{6,4},{7,5},{8,10},{9,11},{10,... | collective-permute-start | bytes 688136 | tf_op jit(solution)/shard_map/ppermute | solution.py:317
  12.7 1.6 %collective-permute-start.5 = (bf16[128,1792]{1,0:T(8,128)(2,1)}, bf16[128,1792]{1,0:T(8,128)(2,1)S(1)}, u32[]{:S(2)}, u32[]{:S(2)}) collective-permute-start(bf16[128,1792]{1,0:T(8,128)(2,1)} %get-tuple-element.65.block_ref), channel_id=1, source_target_pairs={{0,8},{1,9},{2,10},{3,11},{4,0},{5,1},{6,2},{7,3},{8,12},{9,13},{1... | collective-permute-start | bytes 1376264 | tf_op jit(solution)/shard_map/ppermute | solution.py:317
  14.3 4.8 %collective-permute-done.2.refs_7_ = bf16[64,1792]{1,0:T(8,128)(2,1)S(1)} collective-permute-done((bf16[64,1792]{1,0:T(8,128)(2,1)S(1)}, bf16[64,1792]{1,0:T(8,128)(2,1)S(1)}, u32[]{:S(2)}, u32[]{:S(2)}) %collective-permute-start.2) | collective-permute-done | bytes 229408 | tf_op jit(solution)/shard_map/ppermute | solution.py:317
  19.1 4.2 %collective-permute-done.1.refs_6_ = bf16[64,1792]{1,0:T(8,128)(2,1)S(1)} collective-permute-done((bf16[64,1792]{1,0:T(8,128)(2,1)S(1)}, bf16[64,1792]{1,0:T(8,128)(2,1)S(1)}, u32[]{:S(2)}, u32[]{:S(2)}) %collective-permute-start.1) | collective-permute-done | bytes 229408 | tf_op jit(solution)/shard_map/ppermute | solution.py:317
  23.3 1.6 %collective-permute-start.3 = (bf16[128,1920]{1,0:T(8,128)(2,1)S(1)}, bf16[128,1920]{1,0:T(8,128)(2,1)S(1)}, u32[]{:S(2)}, u32[]{:S(2)}) collective-permute-start(bf16[128,1920]{1,0:T(8,128)(2,1)S(1)} %collective-permute-done.block_ref), channel_id=1, source_target_pairs={{0,8},{1,9},{2,10},{3,11},{4,0},{5,1},{6,2},{7,3},{8,12},{9,13},{1... | collective-permute-start | bytes 1474568 | tf_op jit(solution)/shard_map/ppermute | solution.py:317
  26.1 1.6 %collective-permute-start.6 = (bf16[64,1792]{1,0:T(8,128)(2,1)S(1)}, bf16[64,1792]{1,0:T(8,128)(2,1)S(1)}, u32[]{:S(2)}, u32[]{:S(2)}) collective-permute-start(bf16[64,1792]{1,0:T(8,128)(2,1)S(1)} %get-tuple-element.72), channel_id=1, source_target_pairs={{0,2},{1,3},{2,0},{3,1},{4,6},{5,7},{6,4},{7,5},{8,10},{9,11},{10,... | collective-permute-start | bytes 688136 | tf_op jit(solution)/shard_map/ppermute | solution.py:317
  28.9 1.6 %collective-permute-start.8 = (bf16[64,1792]{1,0:T(8,128)(2,1)S(1)}, bf16[64,1792]{1,0:T(8,128)(2,1)S(1)}, u32[]{:S(2)}, u32[]{:S(2)}) collective-permute-start(bf16[64,1792]{1,0:T(8,128)(2,1)S(1)} %get-tuple-element.77), channel_id=1, source_target_pairs={{0,2},{1,3},{2,0},{3,1},{4,6},{5,7},{6,4},{7,5},{8,10},{9,11},{10,... | collective-permute-start | bytes 688136 | tf_op jit(solution)/shard_map/ppermute | solution.py:317
  30.5 4.1 %collective-permute-done.6.refs_2_ = bf16[64,1792]{1,0:T(8,128)(2,1)S(1)} collective-permute-done((bf16[64,1792]{1,0:T(8,128)(2,1)S(1)}, bf16[64,1792]{1,0:T(8,128)(2,1)S(1)}, u32[]{:S(2)}, u32[]{:S(2)}) %collective-permute-start.6) | collective-permute-done | bytes 229408 | tf_op jit(solution)/shard_map/ppermute | solution.py:317
  34.6 4.5 %collective-permute-done.3.block_ref = bf16[128,1920]{1,0:T(8,128)(2,1)S(1)} collective-permute-done((bf16[128,1920]{1,0:T(8,128)(2,1)S(1)}, bf16[128,1920]{1,0:T(8,128)(2,1)S(1)}, u32[]{:S(2)}, u32[]{:S(2)}) %collective-permute-start.3) | collective-permute-done | bytes 491552 | tf_op jit(solution)/shard_map/ppermute | solution.py:317
  40.3 1.6 %collective-permute-start.10 = (bf16[64,1792]{1,0:T(8,128)(2,1)S(1)}, bf16[64,1792]{1,0:T(8,128)(2,1)S(1)}, u32[]{:S(2)}, u32[]{:S(2)}) collective-permute-start(bf16[64,1792]{1,0:T(8,128)(2,1)S(1)} %get-tuple-element.83), channel_id=1, source_target_pairs={{0,2},{1,3},{2,0},{3,1},{4,6},{5,7},{6,4},{7,5},{8,10},{9,11},{10,... | collective-permute-start | bytes 688136 | tf_op jit(solution)/shard_map/ppermute | solution.py:317
  41.9 3.4 %collective-permute-start.4 = (bf16[128,1920]{1,0:T(8,128)(2,1)S(1)}, bf16[128,1920]{1,0:T(8,128)(2,1)S(1)}, u32[]{:S(2)}, u32[]{:S(2)}) collective-permute-start(bf16[128,1920]{1,0:T(8,128)(2,1)S(1)} %collective-permute-done.3.block_ref), channel_id=1, source_target_pairs={{0,8},{1,9},{2,10},{3,11},{4,0},{5,1},{6,2},{7,3},{8,12},{9,13},{1... | collective-permute-start | bytes 1474568 | tf_op jit(solution)/shard_map/ppermute | solution.py:317
  45.3 9.1 %shard_map.74 = (bf16[64,1792]{1,0:T(8,128)(2,1)S(1)}, bf16[64,1792]{1,0:T(8,128)(2,1)S(1)}, bf16[64,1792]{1,0:T(8,128)(2,1)S(1)}, bf16[64,1792]{1,0:T(8,128)(2,1)S(1)}) custom-call(bf16[64,1792]{1,0:T(8,128)(2,1)S(1)} %get-tuple-element.76.refs_0_, bf16[64,1792]{1,0:T(8,128)(2,1)S(1)} %get-tuple-element.71.refs_1_, ...), custom_call_target="tpu_custom_call" | custom-call | flops 2818572288 | bytes 22020096 | tf_op jit(solution)/shard_map/pallas_call | solution.py:268
  55.3 1.6 %collective-permute-start.12 = (bf16[64,1792]{1,0:T(8,128)(2,1)S(1)}, bf16[64,1792]{1,0:T(8,128)(2,1)S(1)}, u32[]{:S(2)}, u32[]{:S(2)}) collective-permute-start(bf16[64,1792]{1,0:T(8,128)(2,1)S(1)} %get-tuple-element.89), channel_id=1, source_target_pairs={{0,2},{1,3},{2,0},{3,1},{4,6},{5,7},{6,4},{7,5},{8,10},{9,11},{10,... | collective-permute-start | bytes 688136 | tf_op jit(solution)/shard_map/ppermute | solution.py:317
  58.0 5.0 %collective-permute-done.11.refs_1_ = bf16[64,1792]{1,0:T(8,128)(2,1)S(1)} collective-permute-done((bf16[64,1792]{1,0:T(8,128)(2,1)S(1)}, bf16[64,1792]{1,0:T(8,128)(2,1)S(1)}, u32[]{:S(2)}, u32[]{:S(2)}) %collective-permute-start.11) | collective-permute-done | bytes 229408 | tf_op jit(solution)/shard_map/ppermute | solution.py:317
  64.3 1.2 shard_map.77
  66.1 1.8 %collective-permute-done.12.refs_3_ = bf16[64,1792]{1,0:T(8,128)(2,1)S(1)} collective-permute-done((bf16[64,1792]{1,0:T(8,128)(2,1)S(1)}, bf16[64,1792]{1,0:T(8,128)(2,1)S(1)}, u32[]{:S(2)}, u32[]{:S(2)}) %collective-permute-start.12) | collective-permute-done | bytes 229408 | tf_op jit(solution)/shard_map/ppermute | solution.py:317
  67.9 9.1 %shard_map.78 = (bf16[64,1792]{1,0:T(8,128)(2,1)S(1)}, bf16[64,1792]{1,0:T(8,128)(2,1)S(1)}, bf16[64,1792]{1,0:T(8,128)(2,1)S(1)}, bf16[64,1792]{1,0:T(8,128)(2,1)S(1)}) custom-call(bf16[64,1792]{1,0:T(8,128)(2,1)S(1)} %get-tuple-element.88.refs_0_, bf16[64,1792]{1,0:T(8,128)(2,1)S(1)} %get-tuple-element.80.refs_1_, ...), custom_call_target="tpu_custom_call" | custom-call | flops 2818572288 | bytes 22020096 | tf_op jit(solution)/shard_map/pallas_call | solution.py:268
  80.6 5.2 %collective-permute-done.18.refs_3_ = bf16[64,1792]{1,0:T(8,128)(2,1)S(1)} collective-permute-done((bf16[64,1792]{1,0:T(8,128)(2,1)S(1)}, bf16[64,1792]{1,0:T(8,128)(2,1)S(1)}, u32[]{:S(2)}, u32[]{:S(2)}) %collective-permute-start.18) | collective-permute-done | bytes 229408 | tf_op jit(solution)/shard_map/ppermute | solution.py:317
  85.8 4.9 %collective-permute-done.17.refs_1_ = bf16[64,1792]{1,0:T(8,128)(2,1)S(1)} collective-permute-done((bf16[64,1792]{1,0:T(8,128)(2,1)S(1)}, bf16[64,1792]{1,0:T(8,128)(2,1)S(1)}, u32[]{:S(2)}, u32[]{:S(2)}) %collective-permute-start.17) | collective-permute-done | bytes 229408 | tf_op jit(solution)/shard_map/ppermute | solution.py:317
  91.5 1.7 %collective-permute-done.25.refs_1_ = bf16[64,1792]{1,0:T(8,128)(2,1)S(1)} collective-permute-done((bf16[64,1792]{1,0:T(8,128)(2,1)S(1)}, bf16[64,1792]{1,0:T(8,128)(2,1)S(1)}, u32[]{:S(2)}, u32[]{:S(2)}) %collective-permute-start.25) | collective-permute-done | bytes 229408 | tf_op jit(solution)/shard_map/ppermute | solution.py:317
  94.7 10.5 %shard_map.82 = (bf16[64,1792]{1,0:T(8,128)(2,1)S(1)}, bf16[64,1792]{1,0:T(8,128)(2,1)S(1)}, bf16[64,1792]{1,0:T(8,128)(2,1)S(1)}, bf16[64,1792]{1,0:T(8,128)(2,...) custom-call(bf16[64,1792]{1,0:T(8,128)(2,1)S(1)} %get-tuple-element., ...), custom_call_target="tpu_custom_call" | custom-call | flops 5637144576 | bytes 22020096 | tf_op jit(solution)/shard_map/pallas_call | solution.py:268
  105.2 1.6 %collective-permute-start.20 = (bf16[64,1792]{1,0:T(8,128)(2,1)S(1)}, bf16[64,1792]{1,0:T(8,128)(2,1)S(1)}, u32[]{:S(2)}, u32[]{:S(2)}) collective-permute-start(bf16[64,1792]{1,0:T(8,128)(2,1)S(1)} %get-tuple-element.106), channel_id=1, source_target_pairs={{0,2},{1,3},{2,0},{3,1},{4,6},{5,7},{6,4},{7,5},{8,10},{9,11},{10,... | collective-permute-start | bytes 688136 | tf_op jit(solution)/shard_map/ppermute | solution.py:317
  107.3 6.1 %collective-permute-done.20.refs_1_ = bf16[64,1792]{1,0:T(8,128)(2,1)S(1)} collective-permute-done((bf16[64,1792]{1,0:T(8,128)(2,1)S(1)}, bf16[64,1792]{1,0:T(8,128)(2,1)S(1)}, u32[]{:S(2)}, u32[]{:S(2)}) %collective-permute-start.20) | collective-permute-done | bytes 229408 | tf_op jit(solution)/shard_map/ppermute | solution.py:317
  113.7 1.3 collective-permute-start.28
  116.2 1.3 collective-permute-start.24
  122.7 5.5 %collective-permute-done.22.refs_3_ = bf16[64,1792]{1,0:T(8,128)(2,1)S(1)} collective-permute-done((bf16[64,1792]{1,0:T(8,128)(2,1)S(1)}, bf16[64,1792]{1,0:T(8,128)(2,1)S(1)}, u32[]{:S(2)}, u32[]{:S(2)}) %collective-permute-start.22) | collective-permute-done | bytes 229408 | tf_op jit(solution)/shard_map/ppermute | solution.py:317
  128.2 3.8 %collective-permute-done.21.refs_1_ = bf16[64,1792]{1,0:T(8,128)(2,1)S(1)} collective-permute-done((bf16[64,1792]{1,0:T(8,128)(2,1)S(1)}, bf16[64,1792]{1,0:T(8,128)(2,1)S(1)}, u32[]{:S(2)}, u32[]{:S(2)}) %collective-permute-start.21) | collective-permute-done | bytes 229408 | tf_op jit(solution)/shard_map/ppermute | solution.py:317
  132.0 1.6 %shard_map.86 = bf16[128,3584]{1,0:T(8,128)(2,1)} custom-call(bf16[2,64,128]{2,1,0:T(8,128)(2,1)S(1)} %get-tuple-element.62.combine_ref, bf16[64,1792]{1,0:T(8,128)(2,1)S(1)} %get-tuple-element.103.refs_0_, bf16[64,1792]{1,0:T(8,128)(2,1)S(1)} %collective-permute-done.21.refs_1_, bf16[64,1792]{1,0:T(8,128)(2,1)S(1)} %get-tuple-element.108.refs_2_, ...), custom_call_target="tpu_custom_call" | custom-call | flops 917504 | bytes 1835008 | tf_op jit(solution)/shard_map/pallas_call | solution.py:196
  (57 shorter events, 22.9 us)
Async XLA Ops:
  0.6 44.7 %collective-permute-start.9 = (bf16[3,3584,512]{2,1,0:T(8,128)(2,1)}, bf16[3,3584,512]{2,1,0:T(8,128)(2,1)}, u32[]{:S(2)}, u32[]{:S(2)}) collective-permute-start(bf16[3,3584,512]{2,1,0:T(8,128)(2,1)} %refs_8_.1), channel_id=1, source_target_pairs={{0,1},{1,0},{2,3},{3,2},{4,5},{5,4},{6,7},{7,6},{8,9},{9,8},{10,11... | collective-permute-start | bytes 33030152 | tf_op jit(solution)/shard_map/ppermute | solution.py:317
  3.3 20.0 %collective-permute-start = (bf16[128,1920]{1,0:T(8,128)(2,1)}, bf16[128,1920]{1,0:T(8,128)(2,1)S(1)}, u32[]{:S(2)}, u32[]{:S(2)}) collective-permute-start(bf16[128,1920]{1,0:T(8,128)(2,1)} %get-tuple-element.61.block_ref), channel_id=1, source_target_pairs={{0,8},{1,9},{2,10},{3,11},{4,0},{5,1},{6,2},{7,3},{8,12},{9,13},{1... | collective-permute-start | bytes 1474568 | tf_op jit(solution)/shard_map/ppermute | solution.py:317
  7.1 1.0 copy-start
  10.6 8.5 %collective-permute-start.2 = (bf16[64,1792]{1,0:T(8,128)(2,1)S(1)}, bf16[64,1792]{1,0:T(8,128)(2,1)S(1)}, u32[]{:S(2)}, u32[]{:S(2)}) collective-permute-start(bf16[64,1792]{1,0:T(8,128)(2,1)S(1)} %get-tuple-element.66), channel_id=1, source_target_pairs={{0,2},{1,3},{2,0},{3,1},{4,6},{5,7},{6,4},{7,5},{8,10},{9,11},{10,... | collective-permute-start | bytes 688136 | tf_op jit(solution)/shard_map/ppermute | solution.py:317
  12.2 11.1 %collective-permute-start.1 = (bf16[64,1792]{1,0:T(8,128)(2,1)S(1)}, bf16[64,1792]{1,0:T(8,128)(2,1)S(1)}, u32[]{:S(2)}, u32[]{:S(2)}) collective-permute-start(bf16[64,1792]{1,0:T(8,128)(2,1)S(1)} %get-tuple-element.63), channel_id=1, source_target_pairs={{0,2},{1,3},{2,0},{3,1},{4,6},{5,7},{6,4},{7,5},{8,10},{9,11},{10,... | collective-permute-start | bytes 688136 | tf_op jit(solution)/shard_map/ppermute | solution.py:317
  12.7 16.0 %collective-permute-start.5 = (bf16[128,1792]{1,0:T(8,128)(2,1)}, bf16[128,1792]{1,0:T(8,128)(2,1)S(1)}, u32[]{:S(2)}, u32[]{:S(2)}) collective-permute-start(bf16[128,1792]{1,0:T(8,128)(2,1)} %get-tuple-element.65.block_ref), channel_id=1, source_target_pairs={{0,8},{1,9},{2,10},{3,11},{4,0},{5,1},{6,2},{7,3},{8,12},{9,13},{1... | collective-permute-start | bytes 1376264 | tf_op jit(solution)/shard_map/ppermute | solution.py:317
  23.3 15.8 %collective-permute-start.3 = (bf16[128,1920]{1,0:T(8,128)(2,1)S(1)}, bf16[128,1920]{1,0:T(8,128)(2,1)S(1)}, u32[]{:S(2)}, u32[]{:S(2)}) collective-permute-start(bf16[128,1920]{1,0:T(8,128)(2,1)S(1)} %collective-permute-done.block_ref), channel_id=1, source_target_pairs={{0,8},{1,9},{2,10},{3,11},{4,0},{5,1},{6,2},{7,3},{8,12},{9,13},{1... | collective-permute-start | bytes 1474568 | tf_op jit(solution)/shard_map/ppermute | solution.py:317
  26.1 8.5 %collective-permute-start.6 = (bf16[64,1792]{1,0:T(8,128)(2,1)S(1)}, bf16[64,1792]{1,0:T(8,128)(2,1)S(1)}, u32[]{:S(2)}, u32[]{:S(2)}) collective-permute-start(bf16[64,1792]{1,0:T(8,128)(2,1)S(1)} %get-tuple-element.72), channel_id=1, source_target_pairs={{0,2},{1,3},{2,0},{3,1},{4,6},{5,7},{6,4},{7,5},{8,10},{9,11},{10,... | collective-permute-start | bytes 688136 | tf_op jit(solution)/shard_map/ppermute | solution.py:317
  28.9 16.3 %collective-permute-start.8 = (bf16[64,1792]{1,0:T(8,128)(2,1)S(1)}, bf16[64,1792]{1,0:T(8,128)(2,1)S(1)}, u32[]{:S(2)}, u32[]{:S(2)}) collective-permute-start(bf16[64,1792]{1,0:T(8,128)(2,1)S(1)} %get-tuple-element.77), channel_id=1, source_target_pairs={{0,2},{1,3},{2,0},{3,1},{4,6},{5,7},{6,4},{7,5},{8,10},{9,11},{10,... | collective-permute-start | bytes 688136 | tf_op jit(solution)/shard_map/ppermute | solution.py:317
  34.6 20.4 %collective-permute-start.7 = (bf16[128,1792]{1,0:T(8,128)(2,1)S(1)}, bf16[128,1792]{1,0:T(8,128)(2,1)S(1)}, u32[]{:S(2)}, u32[]{:S(2)}) collective-permute-start(bf16[128,1792]{1,0:T(8,128)(2,1)S(1)} %collective-permute-done.5.block_ref), channel_id=1, source_target_pairs={{0,8},{1,9},{2,10},{3,11},{4,0},{5,1},{6,2},{7,3},{8,12},{9,13},{1... | collective-permute-start | bytes 1376264 | tf_op jit(solution)/shard_map/ppermute | solution.py:317
  40.3 14.1 %collective-permute-start.10 = (bf16[64,1792]{1,0:T(8,128)(2,1)S(1)}, bf16[64,1792]{1,0:T(8,128)(2,1)S(1)}, u32[]{:S(2)}, u32[]{:S(2)}) collective-permute-start(bf16[64,1792]{1,0:T(8,128)(2,1)S(1)} %get-tuple-element.83), channel_id=1, source_target_pairs={{0,2},{1,3},{2,0},{3,1},{4,6},{5,7},{6,4},{7,5},{8,10},{9,11},{10,... | collective-permute-start | bytes 688136 | tf_op jit(solution)/shard_map/ppermute | solution.py:317
  41.9 22.5 %collective-permute-start.4 = (bf16[128,1920]{1,0:T(8,128)(2,1)S(1)}, bf16[128,1920]{1,0:T(8,128)(2,1)S(1)}, u32[]{:S(2)}, u32[]{:S(2)}) collective-permute-start(bf16[128,1920]{1,0:T(8,128)(2,1)S(1)} %collective-permute-done.3.block_ref), channel_id=1, source_target_pairs={{0,8},{1,9},{2,10},{3,11},{4,0},{5,1},{6,2},{7,3},{8,12},{9,13},{1... | collective-permute-start | bytes 1474568 | tf_op jit(solution)/shard_map/ppermute | solution.py:317
  54.4 8.6 %collective-permute-start.11 = (bf16[64,1792]{1,0:T(8,128)(2,1)S(1)}, bf16[64,1792]{1,0:T(8,128)(2,1)S(1)}, u32[]{:S(2)}, u32[]{:S(2)}) collective-permute-start(bf16[64,1792]{1,0:T(8,128)(2,1)S(1)} %get-tuple-element.84), channel_id=1, source_target_pairs={{0,2},{1,3},{2,0},{3,1},{4,6},{5,7},{6,4},{7,5},{8,10},{9,11},{10,... | collective-permute-start | bytes 688136 | tf_op jit(solution)/shard_map/ppermute | solution.py:317
  55.3 12.7 %collective-permute-start.12 = (bf16[64,1792]{1,0:T(8,128)(2,1)S(1)}, bf16[64,1792]{1,0:T(8,128)(2,1)S(1)}, u32[]{:S(2)}, u32[]{:S(2)}) collective-permute-start(bf16[64,1792]{1,0:T(8,128)(2,1)S(1)} %get-tuple-element.89), channel_id=1, source_target_pairs={{0,2},{1,3},{2,0},{3,1},{4,6},{5,7},{6,4},{7,5},{8,10},{9,11},{10,... | collective-permute-start | bytes 688136 | tf_op jit(solution)/shard_map/ppermute | solution.py:317
  56.9 20.2 %collective-permute-start.15 = (bf16[128,1792]{1,0:T(8,128)(2,1)S(1)}, bf16[128,1792]{1,0:T(8,128)(2,1)S(1)}, u32[]{:S(2)}, u32[]{:S(2)}) collective-permute-start(bf16[128,1792]{1,0:T(8,128)(2,1)S(1)} %collective-permute-done.7.block_ref), channel_id=1, source_target_pairs={{0,8},{1,9},{2,10},{3,11},{4,0},{5,1},{6,2},{7,3},{8,12},{9,13},{1... | collective-permute-start | bytes 1376264 | tf_op jit(solution)/shard_map/ppermute | solution.py:317
  57.5 20.4 %collective-permute-start.14 = (bf16[64,1792]{1,0:T(8,128)(2,1)S(1)}, bf16[64,1792]{1,0:T(8,128)(2,1)S(1)}, u32[]{:S(2)}, u32[]{:S(2)}) collective-permute-start(bf16[64,1792]{1,0:T(8,128)(2,1)S(1)} %get-tuple-element.94), channel_id=1, source_target_pairs={{0,2},{1,3},{2,0},{3,1},{4,6},{5,7},{6,4},{7,5},{8,10},{9,11},{10,... | collective-permute-start | bytes 688136 | tf_op jit(solution)/shard_map/ppermute | solution.py:317
  63.4 16.7 %collective-permute-start.13 = (bf16[128,1792]{1,0:T(8,128)(2,1)S(1)}, bf16[128,1792]{1,0:T(8,128)(2,1)S(1)}, u32[]{:S(2)}, u32[]{:S(2)}) collective-permute-start(bf16[128,1792]{1,0:T(8,128)(2,1)S(1)} %shard_map.76), channel_id=1, source_target_pairs={{0,8},{1,9},{2,10},{3,11},{4,0},{5,1},{6,2},{7,3},{8,12},{9,13},{1... | collective-permute-start | bytes 1376264 | tf_op jit(solution)/shard_map/ppermute | solution.py:317
  65.6 13.5 %collective-permute-start.16 = (bf16[64,1792]{1,0:T(8,128)(2,1)S(1)}, bf16[64,1792]{1,0:T(8,128)(2,1)S(1)}, u32[]{:S(2)}, u32[]{:S(2)}) collective-permute-start(bf16[64,1792]{1,0:T(8,128)(2,1)S(1)} %get-tuple-element.97), channel_id=1, source_target_pairs={{0,2},{1,3},{2,0},{3,1},{4,6},{5,7},{6,4},{7,5},{8,10},{9,11},{10,... | collective-permute-start | bytes 688136 | tf_op jit(solution)/shard_map/ppermute | solution.py:317
  77.3 8.5 %collective-permute-start.18 = (bf16[64,1792]{1,0:T(8,128)(2,1)S(1)}, bf16[64,1792]{1,0:T(8,128)(2,1)S(1)}, u32[]{:S(2)}, u32[]{:S(2)}) collective-permute-start(bf16[64,1792]{1,0:T(8,128)(2,1)S(1)} %get-tuple-element.100), channel_id=1, source_target_pairs={{0,2},{1,3},{2,0},{3,1},{4,6},{5,7},{6,4},{7,5},{8,10},{9,11},{10,... | collective-permute-start | bytes 688136 | tf_op jit(solution)/shard_map/ppermute | solution.py:317
  78.3 13.2 %collective-permute-start.26 = (bf16[128,1792]{1,0:T(8,128)(2,1)S(1)}, bf16[128,1792]{1,0:T(8,128)(2,1)S(1)}, u32[]{:S(2)}, u32[]{:S(2)}) collective-permute-start(bf16[128,1792]{1,0:T(8,128)(2,1)S(1)} %shard_map.79), channel_id=1, source_target_pairs={{0,8},{1,9},{2,10},{3,11},{4,0},{5,1},{6,2},{7,3},{8,12},{9,13},{1... | collective-permute-start | bytes 1376264 | tf_op jit(solution)/shard_map/ppermute | solution.py:317
  80.1 10.6 %collective-permute-start.17 = (bf16[64,1792]{1,0:T(8,128)(2,1)S(1)}, bf16[64,1792]{1,0:T(8,128)(2,1)S(1)}, u32[]{:S(2)}, u32[]{:S(2)}) collective-permute-start(bf16[64,1792]{1,0:T(8,128)(2,1)S(1)} %get-tuple-element.98), channel_id=1, source_target_pairs={{0,2},{1,3},{2,0},{3,1},{4,6},{5,7},{6,4},{7,5},{8,10},{9,11},{10,... | collective-permute-start | bytes 688136 | tf_op jit(solution)/shard_map/ppermute | solution.py:317
  85.8 7.4 %collective-permute-start.25 = (bf16[64,1792]{1,0:T(8,128)(2,1)S(1)}, bf16[64,1792]{1,0:T(8,128)(2,1)S(1)}, u32[]{:S(2)}, u32[]{:S(2)}) collective-permute-start(bf16[64,1792]{1,0:T(8,128)(2,1)S(1)} %get-tuple-element.115), channel_id=1, source_target_pairs={{0,2},{1,3},{2,0},{3,1},{4,6},{5,7},{6,4},{7,5},{8,10},{9,11},{10,... | collective-permute-start | bytes 688136 | tf_op jit(solution)/shard_map/ppermute | solution.py:317
  91.1 24.6 %collective-permute-start.23 = (bf16[128,1792]{1,0:T(8,128)(2,1)S(1)}, bf16[128,1792]{1,0:T(8,128)(2,1)S(1)}, u32[]{:S(2)}, u32[]{:S(2)}) collective-permute-start(bf16[128,1792]{1,0:T(8,128)(2,1)S(1)} %shard_map.81), channel_id=1, source_target_pairs={{0,8},{1,9},{2,10},{3,11},{4,0},{5,1},{6,2},{7,3},{8,12},{9,13},{1... | collective-permute-start | bytes 1376264 | tf_op jit(solution)/shard_map/ppermute | solution.py:317
  93.7 19.7 %collective-permute-start.27 = (bf16[128,1792]{1,0:T(8,128)(2,1)S(1)}, bf16[128,1792]{1,0:T(8,128)(2,1)S(1)}, u32[]{:S(2)}, u32[]{:S(2)}) collective-permute-start(bf16[128,1792]{1,0:T(8,128)(2,1)S(1)} %shard_map.84), channel_id=1, source_target_pairs={{0,8},{1,9},{2,10},{3,11},{4,0},{5,1},{6,2},{7,3},{8,12},{9,13},{1... | collective-permute-start | bytes 1376264 | tf_op jit(solution)/shard_map/ppermute | solution.py:317
  105.2 8.1 %collective-permute-start.20 = (bf16[64,1792]{1,0:T(8,128)(2,1)S(1)}, bf16[64,1792]{1,0:T(8,128)(2,1)S(1)}, u32[]{:S(2)}, u32[]{:S(2)}) collective-permute-start(bf16[64,1792]{1,0:T(8,128)(2,1)S(1)} %get-tuple-element.106), channel_id=1, source_target_pairs={{0,2},{1,3},{2,0},{3,1},{4,6},{5,7},{6,4},{7,5},{8,10},{9,11},{10,... | collective-permute-start | bytes 688136 | tf_op jit(solution)/shard_map/ppermute | solution.py:317
  106.8 9.0 %collective-permute-start.19 = (bf16[64,1792]{1,0:T(8,128)(2,1)S(1)}, bf16[64,1792]{1,0:T(8,128)(2,1)S(1)}, u32[]{:S(2)}, u32[]{:S(2)}) collective-permute-start(bf16[64,1792]{1,0:T(8,128)(2,1)S(1)} %get-tuple-element.105), channel_id=1, source_target_pairs={{0,2},{1,3},{2,0},{3,1},{4,6},{5,7},{6,4},{7,5},{8,10},{9,11},{10,... | collective-permute-start | bytes 688136 | tf_op jit(solution)/shard_map/ppermute | solution.py:317
  113.7 18.2 %collective-permute-start.28 = (bf16[128,1792]{1,0:T(8,128)(2,1)S(1)}, bf16[128,1792]{1,0:T(8,128)(2,1)S(1)}, u32[]{:S(2)}, u32[]{:S(2)}) collective-permute-start(bf16[128,1792]{1,0:T(8,128)(2,1)S(1)} %shard_map.85), channel_id=1, source_target_pairs={{0,8},{1,9},{2,10},{3,11},{4,0},{5,1},{6,2},{7,3},{8,12},{9,13},{1... | collective-permute-start | bytes 1376264 | tf_op jit(solution)/shard_map/ppermute | solution.py:317
  116.2 15.8 %collective-permute-start.24 = (bf16[128,1792]{1,0:T(8,128)(2,1)S(1)}, bf16[128,1792]{1,0:T(8,128)(2,1)S(1)}, u32[]{:S(2)}, u32[]{:S(2)}) collective-permute-start(bf16[128,1792]{1,0:T(8,128)(2,1)S(1)} %shard_map.83), channel_id=1, source_target_pairs={{0,8},{1,9},{2,10},{3,11},{4,0},{5,1},{6,2},{7,3},{8,12},{9,13},{1... | collective-permute-start | bytes 1376264 | tf_op jit(solution)/shard_map/ppermute | solution.py:317
  117.5 1.2 collective-permute-start.29
  118.6 3.5 %collective-permute-start.30 = (f32[1,128]{1,0:T(1,128)S(1)}, f32[1,128]{1,0:T(1,128)S(1)}, u32[]{:S(2)}, u32[]{:S(2)}) collective-permute-start(f32[1,128]{1,0:T(1,128)S(1)} %slice.10), channel_id=1, source_target_pairs={{0,2},{1,3},{2,0},{3,1},{4,6},{5,7},{6,4},{7,5},{8,10},{9,11},{10,... | collective-permute-start | bytes 1544 | tf_op jit(solution)/shard_map/ppermute | solution.py:317
  119.7 8.5 %collective-permute-start.22 = (bf16[64,1792]{1,0:T(8,128)(2,1)S(1)}, bf16[64,1792]{1,0:T(8,128)(2,1)S(1)}, u32[]{:S(2)}, u32[]{:S(2)}) collective-permute-start(bf16[64,1792]{1,0:T(8,128)(2,1)S(1)} %get-tuple-element.109), channel_id=1, source_target_pairs={{0,2},{1,3},{2,0},{3,1},{4,6},{5,7},{6,4},{7,5},{8,10},{9,11},{10,... | collective-permute-start | bytes 688136 | tf_op jit(solution)/shard_map/ppermute | solution.py:317
  120.7 11.3 %collective-permute-start.21 = (bf16[64,1792]{1,0:T(8,128)(2,1)S(1)}, bf16[64,1792]{1,0:T(8,128)(2,1)S(1)}, u32[]{:S(2)}, u32[]{:S(2)}) collective-permute-start(bf16[64,1792]{1,0:T(8,128)(2,1)S(1)} %get-tuple-element.107), channel_id=1, source_target_pairs={{0,2},{1,3},{2,0},{3,1},{4,6},{5,7},{6,4},{7,5},{8,10},{9,11},{10,... | collective-permute-start | bytes 688136 | tf_op jit(solution)/shard_map/ppermute | solution.py:317

commit v5 on v4

--- a/solution.py
+++ b/solution.py
@@ -359,7 +359,7 @@
 
     none = ((),) * PARTS
     block = label_rows(tokens, expert_ids.T, copy_ids.T, gate_weights.T)
-    other_weights = permute(expert_weights, core_pairs)
+    other_weights = permute(behind(expert_weights, block[0]), core_pairs)
     for i in range(PARTS):
         dispatch(0, i, block[i])
     block = [permute(part, ring_pairs(1)) for part in block]
@@ -410,7 +410,7 @@
         else:
             give_back(step)
         pass_on(step, none)
-    give_back(0, *(back[last][i][-1] for i in range(PARTS)))
+    give_back(0, back[last][0][-1], late=(back[last][0][-1],))
     moe_out = combine_rows(tables[0], back[0], sum(carry, ()))
 
     return moe_out, served[:, :2].astype(jnp.int32)

time: 134 us -> 134 us (level)
  transfers between devices with their start and end apart: 31 -> 31, of which waited for: 17 -> 17; matrix products, arithmetic and copies ran while one was open for 0% -> 0% of each run, Pallas kernels for 30% -> 29%
where the time goes in v5:
time: 134 us; the launch traced here: 133 us
  waiting for transfers between devices  55.7 us (42%)
  Pallas kernels  41.9 us (31%)
  starting transfers between devices  33.3 us (25%)
    ppermute x31, waiting for transfers between devices, permute(): return lax.ppermute(x, 'expert', pairs)  55.7 us
    ppermute x31, starting transfers between devices, permute(): return lax.ppermute(x, 'expert', pairs)  33.3 us
    pallas_call x3, Pallas kernels, expert_rows(): pl.pallas_call(functools.partial(expert_kernel, pieces=count, chunks=chun...  28.7 us
    pallas_call x4, Pallas kernels, dispatch_rows(): pl.pallas_call(functools.partial(dispatch_kernel, inner=inner, top_k=top_...  4.84 us
    pallas_call x7, Pallas kernels, combine_rows(): pl.pallas_call(functools.partial(combine_kernel, inner=inner, parts=parts...  4.1 us
  transfers between devices with their start and end apart: 31, of which 17 were waited for; matrix products, arithmetic and copies ran while one was open for 0% of the time, Pallas kernels for 29%

profile of v5, /device:TPU:0, one launch (start us, length us, event | category | flops | bytes accessed | tf_op | source)
XLA Modules:
  0.0 133.3 jit_solution(11460696636696577737)
XLA Ops:
  0.6 2.2 %shard_map.68 = (bf16[128,1920]{1,0:T(8,128)(2,1)}, bf16[128,1792]{1,0:T(8,128)(2,1)}) custom-call(bf16[128,3584]{1,0:T(8,128)(2,1)} %tokens_ref.1, s32[2,128]{1,0:T(2,128)} %bitcast.5, s32[2,128]{1,0:T(2,128)} %bitcast.6, bf16[2,128]{1,0:T(2,128)(2,1)} %bitcast.7), custom_call_target="tpu_custom_call" | custom-call | flops 917504 | bytes 1835008 | tf_op jit(solution)/shard_map/pallas_call | solution.py:87
  3.3 3.7 %collective-permute-start = (bf16[128,1920]{1,0:T(8,128)(2,1)}, bf16[128,1920]{1,0:T(8,128)(2,1)S(1)}, u32[]{:S(2)}, u32[]{:S(2)}) collective-permute-start(bf16[128,1920]{1,0:T(8,128)(2,1)} %get-tuple-element.63.block_ref), channel_id=1, source_target_pairs={{0,8},{1,9},{2,10},{3,11},{4,0},{5,1},{6,2},{7,3},{8,12},{9,13},{1... | collective-permute-start | bytes 1474568 | tf_op jit(solution)/shard_map/ppermute | solution.py:317
  9.3 1.3 shard_map.70
  10.6 1.6 %collective-permute-start.2 = (bf16[64,1792]{1,0:T(8,128)(2,1)S(1)}, bf16[64,1792]{1,0:T(8,128)(2,1)S(1)}, u32[]{:S(2)}, u32[]{:S(2)}) collective-permute-start(bf16[64,1792]{1,0:T(8,128)(2,1)S(1)} %get-tuple-element.68), channel_id=1, source_target_pairs={{0,2},{1,3},{2,0},{3,1},{4,6},{5,7},{6,4},{7,5},{8,10},{9,11},{10,... | collective-permute-start | bytes 688136 | tf_op jit(solution)/shard_map/ppermute | solution.py:317
  12.7 1.6 %collective-permute-start.5 = (bf16[128,1792]{1,0:T(8,128)(2,1)}, bf16[128,1792]{1,0:T(8,128)(2,1)S(1)}, u32[]{:S(2)}, u32[]{:S(2)}) collective-permute-start(bf16[128,1792]{1,0:T(8,128)(2,1)} %get-tuple-element.67.block_ref), channel_id=1, source_target_pairs={{0,8},{1,9},{2,10},{3,11},{4,0},{5,1},{6,2},{7,3},{8,12},{9,13},{1... | collective-permute-start | bytes 1376264 | tf_op jit(solution)/shard_map/ppermute | solution.py:317
  14.3 4.8 %collective-permute-done.2.refs_7_ = bf16[64,1792]{1,0:T(8,128)(2,1)S(1)} collective-permute-done((bf16[64,1792]{1,0:T(8,128)(2,1)S(1)}, bf16[64,1792]{1,0:T(8,128)(2,1)S(1)}, u32[]{:S(2)}, u32[]{:S(2)}) %collective-permute-start.2) | collective-permute-done | bytes 229408 | tf_op jit(solution)/shard_map/ppermute | solution.py:317
  19.1 4.1 %collective-permute-done.1.refs_6_ = bf16[64,1792]{1,0:T(8,128)(2,1)S(1)} collective-permute-done((bf16[64,1792]{1,0:T(8,128)(2,1)S(1)}, bf16[64,1792]{1,0:T(8,128)(2,1)S(1)}, u32[]{:S(2)}, u32[]{:S(2)}) %collective-permute-start.1) | collective-permute-done | bytes 229408 | tf_op jit(solution)/shard_map/ppermute | solution.py:317
  23.3 1.6 %collective-permute-start.3 = (bf16[128,1920]{1,0:T(8,128)(2,1)S(1)}, bf16[128,1920]{1,0:T(8,128)(2,1)S(1)}, u32[]{:S(2)}, u32[]{:S(2)}) collective-permute-start(bf16[128,1920]{1,0:T(8,128)(2,1)S(1)} %collective-permute-done.block_ref), channel_id=1, source_target_pairs={{0,8},{1,9},{2,10},{3,11},{4,0},{5,1},{6,2},{7,3},{8,12},{9,13},{1... | collective-permute-start | bytes 1474568 | tf_op jit(solution)/shard_map/ppermute | solution.py:317
  26.1 1.6 %collective-permute-start.6 = (bf16[64,1792]{1,0:T(8,128)(2,1)S(1)}, bf16[64,1792]{1,0:T(8,128)(2,1)S(1)}, u32[]{:S(2)}, u32[]{:S(2)}) collective-permute-start(bf16[64,1792]{1,0:T(8,128)(2,1)S(1)} %get-tuple-element.74), channel_id=1, source_target_pairs={{0,2},{1,3},{2,0},{3,1},{4,6},{5,7},{6,4},{7,5},{8,10},{9,11},{10,... | collective-permute-start | bytes 688136 | tf_op jit(solution)/shard_map/ppermute | solution.py:317
  29.0 1.6 %collective-permute-start.8 = (bf16[64,1792]{1,0:T(8,128)(2,1)S(1)}, bf16[64,1792]{1,0:T(8,128)(2,1)S(1)}, u32[]{:S(2)}, u32[]{:S(2)}) collective-permute-start(bf16[64,1792]{1,0:T(8,128)(2,1)S(1)} %get-tuple-element.79), channel_id=1, source_target_pairs={{0,2},{1,3},{2,0},{3,1},{4,6},{5,7},{6,4},{7,5},{8,10},{9,11},{10,... | collective-permute-start | bytes 688136 | tf_op jit(solution)/shard_map/ppermute | solution.py:317
  30.5 4.0 %collective-permute-done.6.refs_2_ = bf16[64,1792]{1,0:T(8,128)(2,1)S(1)} collective-permute-done((bf16[64,1792]{1,0:T(8,128)(2,1)S(1)}, bf16[64,1792]{1,0:T(8,128)(2,1)S(1)}, u32[]{:S(2)}, u32[]{:S(2)}) %collective-permute-start.6) | collective-permute-done | bytes 229408 | tf_op jit(solution)/shard_map/ppermute | solution.py:317
  34.5 4.6 %collective-permute-done.3.block_ref = bf16[128,1920]{1,0:T(8,128)(2,1)S(1)} collective-permute-done((bf16[128,1920]{1,0:T(8,128)(2,1)S(1)}, bf16[128,1920]{1,0:T(8,128)(2,1)S(1)}, u32[]{:S(2)}, u32[]{:S(2)}) %collective-permute-start.3) | collective-permute-done | bytes 491552 | tf_op jit(solution)/shard_map/ppermute | solution.py:317
  40.3 1.6 %collective-permute-start.10 = (bf16[64,1792]{1,0:T(8,128)(2,1)S(1)}, bf16[64,1792]{1,0:T(8,128)(2,1)S(1)}, u32[]{:S(2)}, u32[]{:S(2)}) collective-permute-start(bf16[64,1792]{1,0:T(8,128)(2,1)S(1)} %get-tuple-element.86), channel_id=1, source_target_pairs={{0,2},{1,3},{2,0},{3,1},{4,6},{5,7},{6,4},{7,5},{8,10},{9,11},{10,... | collective-permute-start | bytes 688136 | tf_op jit(solution)/shard_map/ppermute | solution.py:317
  41.9 3.4 %collective-permute-start.4 = (bf16[128,1920]{1,0:T(8,128)(2,1)S(1)}, bf16[128,1920]{1,0:T(8,128)(2,1)S(1)}, u32[]{:S(2)}, u32[]{:S(2)}) collective-permute-start(bf16[128,1920]{1,0:T(8,128)(2,1)S(1)} %collective-permute-done.3.block_ref), channel_id=1, source_target_pairs={{0,8},{1,9},{2,10},{3,11},{4,0},{5,1},{6,2},{7,3},{8,12},{9,13},{1... | collective-permute-start | bytes 1474568 | tf_op jit(solution)/shard_map/ppermute | solution.py:317
  45.3 9.1 %shard_map.74 = (bf16[64,1792]{1,0:T(8,128)(2,1)S(1)}, bf16[64,1792]{1,0:T(8,128)(2,1)S(1)}, bf16[64,1792]{1,0:T(8,128)(2,1)S(1)}, bf16[64,1792]{1,0:T(8,128)(2,1)S(1)}) custom-call(bf16[64,1792]{1,0:T(8,128)(2,1)S(1)} %get-tuple-element.78.refs_0_, bf16[64,1792]{1,0:T(8,128)(2,1)S(1)} %get-tuple-element.73.refs_1_, ...), custom_call_target="tpu_custom_call" | custom-call | flops 2818572288 | bytes 22020096 | tf_op jit(solution)/shard_map/pallas_call | solution.py:268
  55.3 1.6 %collective-permute-start.12 = (bf16[64,1792]{1,0:T(8,128)(2,1)S(1)}, bf16[64,1792]{1,0:T(8,128)(2,1)S(1)}, u32[]{:S(2)}, u32[]{:S(2)}) collective-permute-start(bf16[64,1792]{1,0:T(8,128)(2,1)S(1)} %get-tuple-element.92), channel_id=1, source_target_pairs={{0,2},{1,3},{2,0},{3,1},{4,6},{5,7},{6,4},{7,5},{8,10},{9,11},{10,... | collective-permute-start | bytes 688136 | tf_op jit(solution)/shard_map/ppermute | solution.py:317
  58.0 5.0 %collective-permute-done.11.refs_1_ = bf16[64,1792]{1,0:T(8,128)(2,1)S(1)} collective-permute-done((bf16[64,1792]{1,0:T(8,128)(2,1)S(1)}, bf16[64,1792]{1,0:T(8,128)(2,1)S(1)}, u32[]{:S(2)}, u32[]{:S(2)}) %collective-permute-start.11) | collective-permute-done | bytes 229408 | tf_op jit(solution)/shard_map/ppermute | solution.py:317
  64.4 1.2 shard_map.77
  66.1 1.8 %collective-permute-done.12.refs_3_ = bf16[64,1792]{1,0:T(8,128)(2,1)S(1)} collective-permute-done((bf16[64,1792]{1,0:T(8,128)(2,1)S(1)}, bf16[64,1792]{1,0:T(8,128)(2,1)S(1)}, u32[]{:S(2)}, u32[]{:S(2)}) %collective-permute-start.12) | collective-permute-done | bytes 229408 | tf_op jit(solution)/shard_map/ppermute | solution.py:317
  67.9 9.1 %shard_map.78 = (bf16[64,1792]{1,0:T(8,128)(2,1)S(1)}, bf16[64,1792]{1,0:T(8,128)(2,1)S(1)}, bf16[64,1792]{1,0:T(8,128)(2,1)S(1)}, bf16[64,1792]{1,0:T(8,128)(2,1)S(1)}) custom-call(bf16[64,1792]{1,0:T(8,128)(2,1)S(1)} %get-tuple-element.91.refs_0_, bf16[64,1792]{1,0:T(8,128)(2,1)S(1)} %get-tuple-element.83.refs_1_, ...), custom_call_target="tpu_custom_call" | custom-call | flops 2818572288 | bytes 22020096 | tf_op jit(solution)/shard_map/pallas_call | solution.py:268
  80.7 5.2 %collective-permute-done.18.refs_3_ = bf16[64,1792]{1,0:T(8,128)(2,1)S(1)} collective-permute-done((bf16[64,1792]{1,0:T(8,128)(2,1)S(1)}, bf16[64,1792]{1,0:T(8,128)(2,1)S(1)}, u32[]{:S(2)}, u32[]{:S(2)}) %collective-permute-start.18) | collective-permute-done | bytes 229408 | tf_op jit(solution)/shard_map/ppermute | solution.py:317
  85.9 4.9 %collective-permute-done.17.refs_1_ = bf16[64,1792]{1,0:T(8,128)(2,1)S(1)} collective-permute-done((bf16[64,1792]{1,0:T(8,128)(2,1)S(1)}, bf16[64,1792]{1,0:T(8,128)(2,1)S(1)}, u32[]{:S(2)}, u32[]{:S(2)}) %collective-permute-start.17) | collective-permute-done | bytes 229408 | tf_op jit(solution)/shard_map/ppermute | solution.py:317
  91.5 1.7 %collective-permute-done.25.refs_1_ = bf16[64,1792]{1,0:T(8,128)(2,1)S(1)} collective-permute-done((bf16[64,1792]{1,0:T(8,128)(2,1)S(1)}, bf16[64,1792]{1,0:T(8,128)(2,1)S(1)}, u32[]{:S(2)}, u32[]{:S(2)}) %collective-permute-start.25) | collective-permute-done | bytes 229408 | tf_op jit(solution)/shard_map/ppermute | solution.py:317
  94.6 10.5 %shard_map.82 = (bf16[64,1792]{1,0:T(8,128)(2,1)S(1)}, bf16[64,1792]{1,0:T(8,128)(2,1)S(1)}, bf16[64,1792]{1,0:T(8,128)(2,1)S(1)}, bf16[64,1792]{1,0:T(8,128)(2,...) custom-call(bf16[64,1792]{1,0:T(8,128)(2,1)S(1)} %get-tuple-element., ...), custom_call_target="tpu_custom_call" | custom-call | flops 5637144576 | bytes 22020096 | tf_op jit(solution)/shard_map/pallas_call | solution.py:268
  105.1 1.6 %collective-permute-start.24 = (bf16[64,1792]{1,0:T(8,128)(2,1)S(1)}, bf16[64,1792]{1,0:T(8,128)(2,1)S(1)}, u32[]{:S(2)}, u32[]{:S(2)}) collective-permute-start(bf16[64,1792]{1,0:T(8,128)(2,1)S(1)} %get-tuple-element.116), channel_id=1, source_target_pairs={{0,2},{1,3},{2,0},{3,1},{4,6},{5,7},{6,4},{7,5},{8,10},{9,11},{10,... | collective-permute-start | bytes 688136 | tf_op jit(solution)/shard_map/ppermute | solution.py:317
  107.2 5.9 %collective-permute-done.24.refs_1_ = bf16[64,1792]{1,0:T(8,128)(2,1)S(1)} collective-permute-done((bf16[64,1792]{1,0:T(8,128)(2,1)S(1)}, bf16[64,1792]{1,0:T(8,128)(2,1)S(1)}, u32[]{:S(2)}, u32[]{:S(2)}) %collective-permute-start.24) | collective-permute-done | bytes 229408 | tf_op jit(solution)/shard_map/ppermute | solution.py:317
  113.5 1.4 %collective-permute-start.28 = (bf16[128,1792]{1,0:T(8,128)(2,1)S(1)}, bf16[128,1792]{1,0:T(8,128)(2,1)S(1)}, u32[]{:S(2)}, u32[]{:S(2)}) collective-permute-start(bf16[128,1792]{1,0:T(8,128)(2,1)S(1)} %shard_map.85), channel_id=1, source_target_pairs={{0,8},{1,9},{2,10},{3,11},{4,0},{5,1},{6,2},{7,3},{8,12},{9,13},{1... | collective-permute-start | bytes 1376264 | tf_op jit(solution)/shard_map/ppermute | solution.py:317
  116.0 1.4 %collective-permute-start.23 = (bf16[128,1792]{1,0:T(8,128)(2,1)S(1)}, bf16[128,1792]{1,0:T(8,128)(2,1)S(1)}, u32[]{:S(2)}, u32[]{:S(2)}) collective-permute-start(bf16[128,1792]{1,0:T(8,128)(2,1)S(1)} %shard_map.83), channel_id=1, source_target_pairs={{0,8},{1,9},{2,10},{3,11},{4,0},{5,1},{6,2},{7,3},{8,12},{9,13},{1... | collective-permute-start | bytes 1376264 | tf_op jit(solution)/shard_map/ppermute | solution.py:317
  119.4 1.2 collective-permute-start.21
  122.7 5.2 %collective-permute-done.21.refs_3_ = bf16[64,1792]{1,0:T(8,128)(2,1)S(1)} collective-permute-done((bf16[64,1792]{1,0:T(8,128)(2,1)S(1)}, bf16[64,1792]{1,0:T(8,128)(2,1)S(1)}, u32[]{:S(2)}, u32[]{:S(2)}) %collective-permute-start.21) | collective-permute-done | bytes 229408 | tf_op jit(solution)/shard_map/ppermute | solution.py:317
  127.9 3.8 %collective-permute-done.20.refs_1_ = bf16[64,1792]{1,0:T(8,128)(2,1)S(1)} collective-permute-done((bf16[64,1792]{1,0:T(8,128)(2,1)S(1)}, bf16[64,1792]{1,0:T(8,128)(2,1)S(1)}, u32[]{:S(2)}, u32[]{:S(2)}) %collective-permute-start.20) | collective-permute-done | bytes 229408 | tf_op jit(solution)/shard_map/ppermute | solution.py:317
  131.7 1.6 %shard_map.86 = bf16[128,3584]{1,0:T(8,128)(2,1)} custom-call(bf16[2,64,128]{2,1,0:T(8,128)(2,1)S(1)} %get-tuple-element.64.combine_ref, bf16[64,1792]{1,0:T(8,128)(2,1)S(1)} %get-tuple-element.106.refs_0_, bf16[64,1792]{1,0:T(8,128)(2,1)S(1)} %collective-permute-done.20.refs_1_, bf16[64,1792]{1,0:T(8,128)(2,1)S(1)} %get-tuple-element.110.refs_2_, ...), custom_call_target="tpu_custom_call" | custom-call | flops 917504 | bytes 1835008 | tf_op jit(solution)/shard_map/pallas_call | solution.py:196
  (57 shorter events, 22.7 us)
Async XLA Ops:
  2.8 42.5 %collective-permute-start.9 = (bf16[3,3584,512]{2,1,0:T(8,128)(2,1)}, bf16[3,3584,512]{2,1,0:T(8,128)(2,1)}, u32[]{:S(2)}, u32[]{:S(2)}) collective-permute-start(bf16[3,3584,512]{2,1,0:T(8,128)(2,1)} %refs_8_.1), channel_id=1, source_target_pairs={{0,1},{1,0},{2,3},{3,2},{4,5},{5,4},{6,7},{7,6},{8,9},{9,8},{10,11... | collective-permute-start | bytes 33030152 | tf_op jit(solution)/shard_map/ppermute | solution.py:317
  3.3 19.9 %collective-permute-start = (bf16[128,1920]{1,0:T(8,128)(2,1)}, bf16[128,1920]{1,0:T(8,128)(2,1)S(1)}, u32[]{:S(2)}, u32[]{:S(2)}) collective-permute-start(bf16[128,1920]{1,0:T(8,128)(2,1)} %get-tuple-element.63.block_ref), channel_id=1, source_target_pairs={{0,8},{1,9},{2,10},{3,11},{4,0},{5,1},{6,2},{7,3},{8,12},{9,13},{1... | collective-permute-start | bytes 1474568 | tf_op jit(solution)/shard_map/ppermute | solution.py:317
  7.1 1.0 copy-start
  10.6 8.5 %collective-permute-start.2 = (bf16[64,1792]{1,0:T(8,128)(2,1)S(1)}, bf16[64,1792]{1,0:T(8,128)(2,1)S(1)}, u32[]{:S(2)}, u32[]{:S(2)}) collective-permute-start(bf16[64,1792]{1,0:T(8,128)(2,1)S(1)} %get-tuple-element.68), channel_id=1, source_target_pairs={{0,2},{1,3},{2,0},{3,1},{4,6},{5,7},{6,4},{7,5},{8,10},{9,11},{10,... | collective-permute-start | bytes 688136 | tf_op jit(solution)/shard_map/ppermute | solution.py:317
  12.2 11.0 %collective-permute-start.1 = (bf16[64,1792]{1,0:T(8,128)(2,1)S(1)}, bf16[64,1792]{1,0:T(8,128)(2,1)S(1)}, u32[]{:S(2)}, u32[]{:S(2)}) collective-permute-start(bf16[64,1792]{1,0:T(8,128)(2,1)S(1)} %get-tuple-element.65), channel_id=1, source_target_pairs={{0,2},{1,3},{2,0},{3,1},{4,6},{5,7},{6,4},{7,5},{8,10},{9,11},{10,... | collective-permute-start | bytes 688136 | tf_op jit(solution)/shard_map/ppermute | solution.py:317
  12.7 16.0 %collective-permute-start.5 = (bf16[128,1792]{1,0:T(8,128)(2,1)}, bf16[128,1792]{1,0:T(8,128)(2,1)S(1)}, u32[]{:S(2)}, u32[]{:S(2)}) collective-permute-start(bf16[128,1792]{1,0:T(8,128)(2,1)} %get-tuple-element.67.block_ref), channel_id=1, source_target_pairs={{0,8},{1,9},{2,10},{3,11},{4,0},{5,1},{6,2},{7,3},{8,12},{9,13},{1... | collective-permute-start | bytes 1376264 | tf_op jit(solution)/shard_map/ppermute | solution.py:317
  23.3 15.8 %collective-permute-start.3 = (bf16[128,1920]{1,0:T(8,128)(2,1)S(1)}, bf16[128,1920]{1,0:T(8,128)(2,1)S(1)}, u32[]{:S(2)}, u32[]{:S(2)}) collective-permute-start(bf16[128,1920]{1,0:T(8,128)(2,1)S(1)} %collective-permute-done.block_ref), channel_id=1, source_target_pairs={{0,8},{1,9},{2,10},{3,11},{4,0},{5,1},{6,2},{7,3},{8,12},{9,13},{1... | collective-permute-start | bytes 1474568 | tf_op jit(solution)/shard_map/ppermute | solution.py:317
  26.1 8.5 %collective-permute-start.6 = (bf16[64,1792]{1,0:T(8,128)(2,1)S(1)}, bf16[64,1792]{1,0:T(8,128)(2,1)S(1)}, u32[]{:S(2)}, u32[]{:S(2)}) collective-permute-start(bf16[64,1792]{1,0:T(8,128)(2,1)S(1)} %get-tuple-element.74), channel_id=1, source_target_pairs={{0,2},{1,3},{2,0},{3,1},{4,6},{5,7},{6,4},{7,5},{8,10},{9,11},{10,... | collective-permute-start | bytes 688136 | tf_op jit(solution)/shard_map/ppermute | solution.py:317
  29.0 16.3 %collective-permute-start.8 = (bf16[64,1792]{1,0:T(8,128)(2,1)S(1)}, bf16[64,1792]{1,0:T(8,128)(2,1)S(1)}, u32[]{:S(2)}, u32[]{:S(2)}) collective-permute-start(bf16[64,1792]{1,0:T(8,128)(2,1)S(1)} %get-tuple-element.79), channel_id=1, source_target_pairs={{0,2},{1,3},{2,0},{3,1},{4,6},{5,7},{6,4},{7,5},{8,10},{9,11},{10,... | collective-permute-start | bytes 688136 | tf_op jit(solution)/shard_map/ppermute | solution.py:317
  34.5 20.5 %collective-permute-start.7 = (bf16[128,1792]{1,0:T(8,128)(2,1)S(1)}, bf16[128,1792]{1,0:T(8,128)(2,1)S(1)}, u32[]{:S(2)}, u32[]{:S(2)}) collective-permute-start(bf16[128,1792]{1,0:T(8,128)(2,1)S(1)} %collective-permute-done.5.block_ref), channel_id=1, source_target_pairs={{0,8},{1,9},{2,10},{3,11},{4,0},{5,1},{6,2},{7,3},{8,12},{9,13},{1... | collective-permute-start | bytes 1376264 | tf_op jit(solution)/shard_map/ppermute | solution.py:317
  40.3 14.1 %collective-permute-start.10 = (bf16[64,1792]{1,0:T(8,128)(2,1)S(1)}, bf16[64,1792]{1,0:T(8,128)(2,1)S(1)}, u32[]{:S(2)}, u32[]{:S(2)}) collective-permute-start(bf16[64,1792]{1,0:T(8,128)(2,1)S(1)} %get-tuple-element.86), channel_id=1, source_target_pairs={{0,2},{1,3},{2,0},{3,1},{4,6},{5,7},{6,4},{7,5},{8,10},{9,11},{10,... | collective-permute-start | bytes 688136 | tf_op jit(solution)/shard_map/ppermute | solution.py:317
  41.9 22.5 %collective-permute-start.4 = (bf16[128,1920]{1,0:T(8,128)(2,1)S(1)}, bf16[128,1920]{1,0:T(8,128)(2,1)S(1)}, u32[]{:S(2)}, u32[]{:S(2)}) collective-permute-start(bf16[128,1920]{1,0:T(8,128)(2,1)S(1)} %collective-permute-done.3.block_ref), channel_id=1, source_target_pairs={{0,8},{1,9},{2,10},{3,11},{4,0},{5,1},{6,2},{7,3},{8,12},{9,13},{1... | collective-permute-start | bytes 1474568 | tf_op jit(solution)/shard_map/ppermute | solution.py:317
  54.4 8.6 %collective-permute-start.11 = (bf16[64,1792]{1,0:T(8,128)(2,1)S(1)}, bf16[64,1792]{1,0:T(8,128)(2,1)S(1)}, u32[]{:S(2)}, u32[]{:S(2)}) collective-permute-start(bf16[64,1792]{1,0:T(8,128)(2,1)S(1)} %get-tuple-element.87), channel_id=1, source_target_pairs={{0,2},{1,3},{2,0},{3,1},{4,6},{5,7},{6,4},{7,5},{8,10},{9,11},{10,... | collective-permute-start | bytes 688136 | tf_op jit(solution)/shard_map/ppermute | solution.py:317
  55.3 12.7 %collective-permute-start.12 = (bf16[64,1792]{1,0:T(8,128)(2,1)S(1)}, bf16[64,1792]{1,0:T(8,128)(2,1)S(1)}, u32[]{:S(2)}, u32[]{:S(2)}) collective-permute-start(bf16[64,1792]{1,0:T(8,128)(2,1)S(1)} %get-tuple-element.92), channel_id=1, source_target_pairs={{0,2},{1,3},{2,0},{3,1},{4,6},{5,7},{6,4},{7,5},{8,10},{9,11},{10,... | collective-permute-start | bytes 688136 | tf_op jit(solution)/shard_map/ppermute | solution.py:317
  56.9 20.2 %collective-permute-start.15 = (bf16[128,1792]{1,0:T(8,128)(2,1)S(1)}, bf16[128,1792]{1,0:T(8,128)(2,1)S(1)}, u32[]{:S(2)}, u32[]{:S(2)}) collective-permute-start(bf16[128,1792]{1,0:T(8,128)(2,1)S(1)} %collective-permute-done.7.block_ref), channel_id=1, source_target_pairs={{0,8},{1,9},{2,10},{3,11},{4,0},{5,1},{6,2},{7,3},{8,12},{9,13},{1... | collective-permute-start | bytes 1376264 | tf_op jit(solution)/shard_map/ppermute | solution.py:317
  57.5 20.4 %collective-permute-start.14 = (bf16[64,1792]{1,0:T(8,128)(2,1)S(1)}, bf16[64,1792]{1,0:T(8,128)(2,1)S(1)}, u32[]{:S(2)}, u32[]{:S(2)}) collective-permute-start(bf16[64,1792]{1,0:T(8,128)(2,1)S(1)} %get-tuple-element.97), channel_id=1, source_target_pairs={{0,2},{1,3},{2,0},{3,1},{4,6},{5,7},{6,4},{7,5},{8,10},{9,11},{10,... | collective-permute-start | bytes 688136 | tf_op jit(solution)/shard_map/ppermute | solution.py:317
  63.4 16.7 %collective-permute-start.13 = (bf16[128,1792]{1,0:T(8,128)(2,1)S(1)}, bf16[128,1792]{1,0:T(8,128)(2,1)S(1)}, u32[]{:S(2)}, u32[]{:S(2)}) collective-permute-start(bf16[128,1792]{1,0:T(8,128)(2,1)S(1)} %shard_map.76), channel_id=1, source_target_pairs={{0,8},{1,9},{2,10},{3,11},{4,0},{5,1},{6,2},{7,3},{8,12},{9,13},{1... | collective-permute-start | bytes 1376264 | tf_op jit(solution)/shard_map/ppermute | solution.py:317
  65.6 13.5 %collective-permute-start.16 = (bf16[64,1792]{1,0:T(8,128)(2,1)S(1)}, bf16[64,1792]{1,0:T(8,128)(2,1)S(1)}, u32[]{:S(2)}, u32[]{:S(2)}) collective-permute-start(bf16[64,1792]{1,0:T(8,128)(2,1)S(1)} %get-tuple-element.100), channel_id=1, source_target_pairs={{0,2},{1,3},{2,0},{3,1},{4,6},{5,7},{6,4},{7,5},{8,10},{9,11},{10,... | collective-permute-start | bytes 688136 | tf_op jit(solution)/shard_map/ppermute | solution.py:317
  77.3 8.5 %collective-permute-start.18 = (bf16[64,1792]{1,0:T(8,128)(2,1)S(1)}, bf16[64,1792]{1,0:T(8,128)(2,1)S(1)}, u32[]{:S(2)}, u32[]{:S(2)}) collective-permute-start(bf16[64,1792]{1,0:T(8,128)(2,1)S(1)} %get-tuple-element.103), channel_id=1, source_target_pairs={{0,2},{1,3},{2,0},{3,1},{4,6},{5,7},{6,4},{7,5},{8,10},{9,11},{10,... | collective-permute-start | bytes 688136 | tf_op jit(solution)/shard_map/ppermute | solution.py:317
  78.3 13.2 %collective-permute-start.26 = (bf16[128,1792]{1,0:T(8,128)(2,1)S(1)}, bf16[128,1792]{1,0:T(8,128)(2,1)S(1)}, u32[]{:S(2)}, u32[]{:S(2)}) collective-permute-start(bf16[128,1792]{1,0:T(8,128)(2,1)S(1)} %shard_map.79), channel_id=1, source_target_pairs={{0,8},{1,9},{2,10},{3,11},{4,0},{5,1},{6,2},{7,3},{8,12},{9,13},{1... | collective-permute-start | bytes 1376264 | tf_op jit(solution)/shard_map/ppermute | solution.py:317
  80.1 10.6 %collective-permute-start.17 = (bf16[64,1792]{1,0:T(8,128)(2,1)S(1)}, bf16[64,1792]{1,0:T(8,128)(2,1)S(1)}, u32[]{:S(2)}, u32[]{:S(2)}) collective-permute-start(bf16[64,1792]{1,0:T(8,128)(2,1)S(1)} %get-tuple-element.101), channel_id=1, source_target_pairs={{0,2},{1,3},{2,0},{3,1},{4,6},{5,7},{6,4},{7,5},{8,10},{9,11},{10,... | collective-permute-start | bytes 688136 | tf_op jit(solution)/shard_map/ppermute | solution.py:317
  85.9 7.3 %collective-permute-start.25 = (bf16[64,1792]{1,0:T(8,128)(2,1)S(1)}, bf16[64,1792]{1,0:T(8,128)(2,1)S(1)}, u32[]{:S(2)}, u32[]{:S(2)}) collective-permute-start(bf16[64,1792]{1,0:T(8,128)(2,1)S(1)} %get-tuple-element.119), channel_id=1, source_target_pairs={{0,2},{1,3},{2,0},{3,1},{4,6},{5,7},{6,4},{7,5},{8,10},{9,11},{10,... | collective-permute-start | bytes 688136 | tf_op jit(solution)/shard_map/ppermute | solution.py:317
  91.2 24.4 %collective-permute-start.22 = (bf16[128,1792]{1,0:T(8,128)(2,1)S(1)}, bf16[128,1792]{1,0:T(8,128)(2,1)S(1)}, u32[]{:S(2)}, u32[]{:S(2)}) collective-permute-start(bf16[128,1792]{1,0:T(8,128)(2,1)S(1)} %shard_map.81), channel_id=1, source_target_pairs={{0,8},{1,9},{2,10},{3,11},{4,0},{5,1},{6,2},{7,3},{8,12},{9,13},{1... | collective-permute-start | bytes 1376264 | tf_op jit(solution)/shard_map/ppermute | solution.py:317
  93.6 19.5 %collective-permute-start.27 = (bf16[128,1792]{1,0:T(8,128)(2,1)S(1)}, bf16[128,1792]{1,0:T(8,128)(2,1)S(1)}, u32[]{:S(2)}, u32[]{:S(2)}) collective-permute-start(bf16[128,1792]{1,0:T(8,128)(2,1)S(1)} %shard_map.84), channel_id=1, source_target_pairs={{0,8},{1,9},{2,10},{3,11},{4,0},{5,1},{6,2},{7,3},{8,12},{9,13},{1... | collective-permute-start | bytes 1376264 | tf_op jit(solution)/shard_map/ppermute | solution.py:317
  105.1 8.0 %collective-permute-start.24 = (bf16[64,1792]{1,0:T(8,128)(2,1)S(1)}, bf16[64,1792]{1,0:T(8,128)(2,1)S(1)}, u32[]{:S(2)}, u32[]{:S(2)}) collective-permute-start(bf16[64,1792]{1,0:T(8,128)(2,1)S(1)} %get-tuple-element.116), channel_id=1, source_target_pairs={{0,2},{1,3},{2,0},{3,1},{4,6},{5,7},{6,4},{7,5},{8,10},{9,11},{10,... | collective-permute-start | bytes 688136 | tf_op jit(solution)/shard_map/ppermute | solution.py:317
  106.6 8.9 %collective-permute-start.19 = (bf16[64,1792]{1,0:T(8,128)(2,1)S(1)}, bf16[64,1792]{1,0:T(8,128)(2,1)S(1)}, u32[]{:S(2)}, u32[]{:S(2)}) collective-permute-start(bf16[64,1792]{1,0:T(8,128)(2,1)S(1)} %get-tuple-element.108), channel_id=1, source_target_pairs={{0,2},{1,3},{2,0},{3,1},{4,6},{5,7},{6,4},{7,5},{8,10},{9,11},{10,... | collective-permute-start | bytes 688136 | tf_op jit(solution)/shard_map/ppermute | solution.py:317
  113.5 18.2 %collective-permute-start.28 = (bf16[128,1792]{1,0:T(8,128)(2,1)S(1)}, bf16[128,1792]{1,0:T(8,128)(2,1)S(1)}, u32[]{:S(2)}, u32[]{:S(2)}) collective-permute-start(bf16[128,1792]{1,0:T(8,128)(2,1)S(1)} %shard_map.85), channel_id=1, source_target_pairs={{0,8},{1,9},{2,10},{3,11},{4,0},{5,1},{6,2},{7,3},{8,12},{9,13},{1... | collective-permute-start | bytes 1376264 | tf_op jit(solution)/shard_map/ppermute | solution.py:317
  116.0 15.7 %collective-permute-start.23 = (bf16[128,1792]{1,0:T(8,128)(2,1)S(1)}, bf16[128,1792]{1,0:T(8,128)(2,1)S(1)}, u32[]{:S(2)}, u32[]{:S(2)}) collective-permute-start(bf16[128,1792]{1,0:T(8,128)(2,1)S(1)} %shard_map.83), channel_id=1, source_target_pairs={{0,8},{1,9},{2,10},{3,11},{4,0},{5,1},{6,2},{7,3},{8,12},{9,13},{1... | collective-permute-start | bytes 1376264 | tf_op jit(solution)/shard_map/ppermute | solution.py:317
  117.4 1.2 collective-permute-start.29
  118.6 3.5 %collective-permute-start.30 = (f32[1,128]{1,0:T(1,128)S(1)}, f32[1,128]{1,0:T(1,128)S(1)}, u32[]{:S(2)}, u32[]{:S(2)}) collective-permute-start(f32[1,128]{1,0:T(1,128)S(1)} %slice.10), channel_id=1, source_target_pairs={{0,2},{1,3},{2,0},{3,1},{4,6},{5,7},{6,4},{7,5},{8,10},{9,11},{10,... | collective-permute-start | bytes 1544 | tf_op jit(solution)/shard_map/ppermute | solution.py:317
  119.4 8.5 %collective-permute-start.21 = (bf16[64,1792]{1,0:T(8,128)(2,1)S(1)}, bf16[64,1792]{1,0:T(8,128)(2,1)S(1)}, u32[]{:S(2)}, u32[]{:S(2)}) collective-permute-start(bf16[64,1792]{1,0:T(8,128)(2,1)S(1)} %get-tuple-element.112), channel_id=1, source_target_pairs={{0,2},{1,3},{2,0},{3,1},{4,6},{5,7},{6,4},{7,5},{8,10},{9,11},{10,... | collective-permute-start | bytes 688136 | tf_op jit(solution)/shard_map/ppermute | solution.py:317
  120.6 11.1 %collective-permute-start.20 = (bf16[64,1792]{1,0:T(8,128)(2,1)S(1)}, bf16[64,1792]{1,0:T(8,128)(2,1)S(1)}, u32[]{:S(2)}, u32[]{:S(2)}) collective-permute-start(bf16[64,1792]{1,0:T(8,128)(2,1)S(1)} %get-tuple-element.109), channel_id=1, source_target_pairs={{0,2},{1,3},{2,0},{3,1},{4,6},{5,7},{6,4},{7,5},{8,10},{9,11},{10,... | collective-permute-start | bytes 688136 | tf_op jit(solution)/shard_map/ppermute | solution.py:317
